TPU v7x, 128 devices: a whole 4x4x4 slice. The times are simulated.
128 devices in a mesh: dp: 16 (over z, x_hi, core), expert: 8 (over y, x_lo).
Axes of the slice: x: 4 (x_hi: 2, x_lo: 2; x = x_hi * 2 + x_lo), y: 4, z: 4, core: 2. Of those that a mesh axis runs over, the one named last changes fastest.
Arguments:
- tokens: bfloat16 [16384, 3584], P(('dp', 'expert')), may hold values from -6 to 6
- grad_out: bfloat16 [16384, 3584], P(('dp', 'expert')), may hold values from -1.5 to 1.5
- routes: int32 [16384, 2], P(('dp', 'expert')), may hold values from 0 to 7, all different within a row; in each aligned block of 128 rows (0 to 127, 128 to 255, ...) at most 64 rows name the same one
- probs: bfloat16 [16384, 2], P(('dp', 'expert')), may hold values from 0.099609375 to 1
- w_gate: bfloat16 [8, 3584, 1024], P('expert'), may hold values from -0.09375 to 0.09375
- w_up: bfloat16 [8, 3584, 1024], P('expert'), may hold values from -0.09375 to 0.09375
- w_down: bfloat16 [8, 3584, 1024], P('expert'), may hold values from -0.1875 to 0.1875
Outputs:
- grad_tokens: bfloat16 [16384, 3584], P(('dp', 'expert'))
- grad_weights: bfloat16 [16384, 2], P(('dp', 'expert'))
- grad_gate: bfloat16 [8, 3584, 1024], P('expert', 'dp')
- grad_up: bfloat16 [8, 3584, 1024], P('expert', 'dp')
- grad_down: bfloat16 [8, 3584, 1024], P('expert', 'dp')
Inputs may be any that keep to these rules, and one draw needn't show every extreme that they name: `routes`: each row names 2 different experts; within the rows of one device no expert is named by more than 64 rows, and some device has an expert named by exactly 64 rows.
All inputs are finite; a program needn't handle non-finite values.
Results may differ from a plain program's by a relative error of at most 0.017.
Values may be sent and summed in bfloat16 or wider, within the bound.
No kernel may reach another device: no remote copies, remote signals or barrier semaphores. Data moves between devices by JAX's collectives and lax.ppermute only.
A program may use at most 256 MiB of HBM per device.

v0:
```python
import jax
import jax.numpy as jnp
from jax import lax
from jax.sharding import PartitionSpec as P

D = 3584
FF = 1024
TOP = 2
CAP = 64


def slot_number(routes, experts, capacity):
    flat_routes = routes.reshape(-1)
    onehot = (flat_routes[:, None] == jnp.arange(experts, dtype=jnp.int32)[None, :]).astype(
        jnp.int32
    )
    earlier = jnp.cumsum(onehot, axis=0) - onehot
    return flat_routes * capacity + jnp.sum(earlier * onehot, axis=1)


def contract_rows(left_rows, right_rows):
    return lax.dot_general(
        left_rows, right_rows, (((0,), (0,)), ((), ())), preferred_element_type=jnp.float32
    )


def expert_rows(row_tokens, row_grads, row_probs, gate_weight, up_weight, down_weight):
    gate_pre = jnp.dot(row_tokens, gate_weight, preferred_element_type=jnp.float32)
    up_pre = jnp.dot(row_tokens, up_weight, preferred_element_type=jnp.float32)
    sigmoid = jax.nn.sigmoid(gate_pre)
    active = gate_pre * sigmoid
    hidden = (active * up_pre).astype(jnp.bfloat16)
    back_grad = jnp.dot(row_grads, down_weight, preferred_element_type=jnp.float32)
    weight_grad = jnp.sum(back_grad * hidden.astype(jnp.float32), axis=1).astype(jnp.bfloat16)
    scaling = row_probs.astype(jnp.float32)[:, None]
    scaled = scaling * back_grad
    grad_gate_pre = (scaled * up_pre * sigmoid * (1.0 + gate_pre * (1.0 - sigmoid))).astype(
        jnp.bfloat16
    )
    grad_up_pre = (scaled * active).astype(jnp.bfloat16)
    weighted = (scaling * row_grads.astype(jnp.float32)).astype(jnp.bfloat16)
    contract = (((1,), (1,)), ((), ()))
    row_grad = lax.dot_general(
        grad_gate_pre, gate_weight, contract, preferred_element_type=jnp.float32
    )
    row_grad = row_grad + lax.dot_general(
        grad_up_pre, up_weight, contract, preferred_element_type=jnp.float32
    )
    return (
        row_grad.astype(jnp.bfloat16),
        weight_grad,
        grad_gate_pre,
        grad_up_pre,
        hidden,
        weighted,
    )


def local(tokens, grad_out, routes, probs, w_gate, w_up, w_down):
    tok_dev = tokens.shape[0]
    experts = lax.axis_size("expert")
    pair_count = tok_dev * TOP
    zero_value = jnp.zeros((), jnp.bfloat16)
    slot_ids = slot_number(routes, experts, CAP)
    empty_slots = jnp.full((experts * CAP,), pair_count, jnp.int32)
    slot_owner = empty_slots.at[slot_ids].set(jnp.arange(pair_count, dtype=jnp.int32))
    live_slot = slot_owner < pair_count
    token_row = jnp.where(live_slot, slot_owner // TOP, 0)
    slot_pick = jnp.where(live_slot, slot_owner % TOP, 0)
    send_tokens = jnp.where(live_slot[:, None], tokens[token_row], zero_value).reshape(
        experts, CAP, D
    )
    send_grads = jnp.where(live_slot[:, None], grad_out[token_row], zero_value).reshape(
        experts, CAP, D
    )
    send_probs = jnp.where(live_slot, probs[token_row, slot_pick], zero_value).reshape(experts, CAP)
    arrived_tokens, arrived_grads, arrived_probs = (
        lax.all_to_all(send_tokens, "expert", split_axis=0, concat_axis=0, tiled=True),
        lax.all_to_all(send_grads, "expert", split_axis=0, concat_axis=0, tiled=True),
        lax.all_to_all(send_probs, "expert", split_axis=0, concat_axis=0, tiled=True),
    )
    slot_rows = experts * CAP
    row_tokens = arrived_tokens.reshape(slot_rows, D)
    row_grads = arrived_grads.reshape(slot_rows, D)
    row_probs = arrived_probs.reshape(slot_rows)
    gate_weight = w_gate[0]
    up_weight = w_up[0]
    down_weight = w_down[0]
    row_grad, weight_grad, grad_gate_pre, grad_up_pre, hidden, weighted = expert_rows(
        row_tokens, row_grads, row_probs, gate_weight, up_weight, down_weight
    )
    paired = jnp.concatenate([grad_gate_pre, grad_up_pre], axis=1)
    summed = lax.psum_scatter(
        jnp.concatenate(
            [contract_rows(row_tokens, paired), contract_rows(weighted, hidden)], axis=1
        ).astype(jnp.bfloat16),
        "dp",
        scatter_dimension=0,
        tiled=True,
    ).astype(jnp.float32)
    gate_up_sum = summed[:, : 2 * FF]
    down_sum = summed[:, 2 * FF :]
    returned_rows, returned_weight = (
        lax.all_to_all(
            row_grad.reshape(experts, CAP, D), "expert", split_axis=0, concat_axis=0, tiled=True
        ),
        lax.all_to_all(
            weight_grad.reshape(experts, CAP), "expert", split_axis=0, concat_axis=0, tiled=True
        ),
    )
    pair_rows = returned_rows.reshape(slot_rows, D)[slot_ids].reshape(tok_dev, TOP, D)
    grad_tokens = jnp.sum(pair_rows.astype(jnp.float32), axis=1).astype(jnp.bfloat16)
    grad_weights = returned_weight.reshape(slot_rows)[slot_ids].reshape(tok_dev, TOP)
    grad_gate = gate_up_sum[:, :FF].astype(jnp.bfloat16)[None]
    grad_up = gate_up_sum[:, FF:].astype(jnp.bfloat16)[None]
    grad_down = down_sum.astype(jnp.bfloat16)[None]
    return (grad_tokens, grad_weights, grad_gate, grad_up, grad_down)


def solution(mesh):
    in_specs = (
        P(("dp", "expert"), None),
        P(("dp", "expert"), None),
        P(("dp", "expert"), None),
        P(("dp", "expert"), None),
        P("expert", None, None),
        P("expert", None, None),
        P("expert", None, None),
    )
    out_specs = (
        P(("dp", "expert"), None),
        P(("dp", "expert"), None),
        P("expert", "dp", None),
        P("expert", "dp", None),
        P("expert", "dp", None),
    )
    return jax.shard_map(local, mesh=mesh, in_specs=in_specs, out_specs=out_specs, check_vma=False)
```

profile of v0, /device:TPU:0, one launch (start us, length us, event | category | flops | bytes accessed | tf_op | source)
XLA Modules:
  0.0 417.2 jit_solution(14625306270004843529)
XLA Ops:
  11.7 4.6 %gather_fusion = bf16[512]{0:T(512)(128)(2,1)S(1)} fusion(bf16[128,2]{0,1:T(2,128)(2,1)} %param.10, s32[512]{0:T(512)S(1)} %get-tuple-element.22), kind=kCustom, calls=%fused_computation | custom fusion | bytes 6144 | tf_op jit(solution)/shard_map/gather | solution.py:76
  17.0 5.5 %all-to-all-start = ((bf16[8,1,64]{2,1,0:T(2,128)(2,1)}), bf16[8,1,64]{2,1,0:T(2,128)(2,1)S(1)}, u32[]{:S(2)}, u32[]{:S(2)}) async-start(bf16[8,1,64]{2,1,0:T(2,128)(2,1)} %all_to_all.25), calls=%async_computation | async-start | bytes 8192 | tf_op jit(solution)/shard_map/all_to_all | solution.py:80
  22.6 4.2 %gather_fusion.2 = bf16[512,3584]{1,0:T(8,128)(2,1)} fusion(bf16[128,3584]{1,0:T(8,128)(2,1)S(1)} %copy-done, s32[1024]{0:T(1024)S(1)} %pad_clamp_fusion.1), kind=kCustom, calls=%fused_computation.2 | custom fusion | bytes 7342080 | tf_op jit(solution)/shard_map/gather | solution.py:70
  26.8 4.1 gather_fusion.1
  30.9 5.5 %broadcast_select_fusion.1 = (bf16[8,64,3584]{2,1,0:T(8,128)(2,1)}, bf16[8,64,3584]{2,1,0:T(8,128)(2,1)}) fusion(bf16[8,64,3584]{2,1,0:T(8,128)(2,1)} %bitcast.46, pred[8,64]{1,0:T(8,128)(4,1)S(1)} %broadcast_in_dim.52, bf16[8,64,3584]{2,1,0:T(8,128)(2,1)} %bitcast.45), kind=kLoop, calls=%fused_computation.23 | loop fusion | flops 3670016 | bytes 14680576 | tf_op jit(solution)/shard_map/jit(_where)/select_n | solution.py:73
  36.4 49.0 %all_to_all.31 = bf16[8,64,3584]{2,1,0:T(8,128)(2,1)} all-to-all(bf16[8,64,3584]{2,1,0:T(8,128)(2,1)} %get-tuple-element.31), channel_id=1, replica_groups=mesh['dp'=16,'expert'=8] {'expert'}, dimensions={0} | all-to-all | bytes 7340032 | tf_op jit(solution)/shard_map/all_to_all | solution.py:78
  85.5 4.5 %all-to-all-start.1 = ((bf16[8,64,3584]{2,1,0:T(8,128)(2,1)}), bf16[8,64,3584]{2,1,0:T(8,128)(2,1)}, u32[]{:S(2)}, u32[]{:S(2)}) async-start(bf16[8,64,3584]{2,1,0:T(8,128)(2,1)} %get-tuple-element.30), calls=%async_computation.1 | async-start | bytes 7340032 | tf_op jit(solution)/shard_map/all_to_all | solution.py:79
  90.1 9.6 %fusion.2 = f32[512,1024]{1,0:T(8,128)} fusion(bf16[512,3584]{1,0:T(8,128)(2,1)} %bitcast.47, bf16[1,3584,1024]{2,1,0:T(8,128)(2,1)} %param.11), kind=kOutput, calls=%fused_computation.11 | convolution fusion | flops 3758096384 | bytes 13107200 | tf_op jit(solution)/shard_map/dot_general | solution.py:28
  99.7 7.6 %fusion.6 = f32[512,1024]{1,0:T(8,128)} fusion(bf16[512,3584]{1,0:T(8,128)(2,1)S(1)} %bitcast.48, bf16[1,3584,1024]{2,1,0:T(8,128)(2,1)} %param.12), kind=kOutput, calls=%fused_computation.15 | convolution fusion | flops 3758096384 | bytes 13107200 | tf_op jit(solution)/shard_map/dot_general | solution.py:29
  107.3 25.0 %all-to-all-done.1 = bf16[8,64,3584]{2,1,0:T(8,128)(2,1)} async-done(((bf16[8,64,3584]{2,1,0:T(8,128)(2,1)}), bf16[8,64,3584]{2,1,0:T(8,128)(2,1)}, u32[]{:S(2)}, u32[]{:S(2)}) %all-to-all-start.1) | async-done | bytes 3670048 | tf_op jit(solution)/shard_map/all_to_all | solution.py:79
  132.3 10.2 %multiply_reduce_fusion = (bf16[512]{0:T(512)(128)(2,1)S(1)}, bf16[512,1024]{1,0:T(8,128)(2,1)S(1)}, bf16[512,1024]{1,0:T(8,128)(2,1)S(1)}, bf16[512,1024]{1,0:T(8,128)(2,1)S(1)}) fusion(f32[512,1024]{1,0:T(8,128)} %fusion.6, f32[512,1024]{1,0:T(8,128)} %fusion.2, f32[512]{0:T(512)S(1)} %reshape.128, bf16[512,3584]{1,0:T(8,128)(2,1)} %bitcast.5, ...), kind=kOutput, calls=%fused_computation.27 | convolution fusion | flops 3768057344 | bytes 18353152 | tf_op jit(solution)/shard_map/dot_general | solution.py:33
  142.5 8.8 %convolution_convert_fusion.1 = bf16[3584,1024]{0,1:T(8,128)(2,1)} fusion(bf16[512,1024]{1,0:T(8,128)(2,1)S(1)} %get-tuple-element.21, bf16[512,3584]{1,0:T(8,128)(2,1)} %bitcast.5, f32[512]{0:T(512)S(1)} %reshape.128), kind=kOutput, calls=%fused_computation.8 | convolution fusion | flops 3767271424 | bytes 12060672 | tf_op jit(solution)/shard_map/dot_general | solution.py:22
  151.3 11.4 %convolution_convert_fusion = bf16[3584,2048]{0,1:T(8,128)(2,1)} fusion(bf16[512,3584]{1,0:T(8,128)(2,1)S(1)} %bitcast.49, bf16[512,1024]{1,0:T(8,128)(2,1)S(1)} %get-tuple-element.26, bf16[512,1024]{1,0:T(8,128)(2,1)S(1)} %get-tuple-element.25), kind=kOutput, calls=%fused_computation.7 | convolution fusion | flops 7527727104 | bytes 20447232 | tf_op jit(solution)/shard_map/dot_general | solution.py:22
  162.7 23.4 %pad_maximum_fusion = bf16[3584,3072]{0,1:T(8,128)(2,1)} fusion(bf16[3584,1024]{0,1:T(8,128)(2,1)} %convolution_convert_fusion.1, bf16[3584,2048]{0,1:T(8,128)(2,1)} %convolution_convert_fusion), kind=kLoop, calls=%fused_computation.6 | loop fusion | flops 44040192 | bytes 44040192 | tf_op jit(solution)/shard_map/concatenate | solution.py:94
  186.1 28.7 %copy.31 = bf16[3584,3072]{1,0:T(8,128)(2,1)} copy(bf16[3584,3072]{0,1:T(8,128)(2,1)} %pad_maximum_fusion) | data formatting | bytes 44040192
  215.5 3.3 all-to-all-start.4
  218.8 6.6 %fusion = f32[512,3584]{1,0:T(8,128)S(1)} fusion(bf16[512,1024]{1,0:T(8,128)(2,1)} %copy-done.5, bf16[1,3584,1024]{2,1,0:T(8,128)(2,1)} %param.11), kind=kOutput, calls=%fused_computation.9 | convolution fusion | flops 3758096384 | bytes 15728640 | tf_op jit(solution)/shard_map/dot_general | solution.py:43
  225.4 10.2 %add_convert_fusion = bf16[512,3584]{1,0:T(8,128)(2,1)} fusion(f32[512,3584]{1,0:T(8,128)S(1)} %fusion, bf16[512,1024]{1,0:T(8,128)(2,1)S(1)} %get-tuple-element.26, bf16[1,3584,1024]{2,1,0:T(8,128)(2,1)} %param.12), kind=kOutput, calls=%fused_computation.20 | convolution fusion | flops 3761766400 | bytes 19398656 | tf_op jit(solution)/shard_map/dot_general | solution.py:46
  235.6 5.7 %all-to-all-start.3 = ((bf16[8,64,3584]{2,1,0:T(8,128)(2,1)}), bf16[8,64,3584]{2,1,0:T(8,128)(2,1)}, u32[]{:S(2)}, u32[]{:S(2)}) async-start(bf16[8,64,3584]{2,1,0:T(8,128)(2,1)} %bitcast.50), calls=%async_computation.3 | async-start | bytes 7340032 | tf_op jit(solution)/shard_map/all_to_all | solution.py:104
  241.4 1.9 gather_fusion.4
  244.1 54.3 %all-to-all-done.3 = bf16[8,64,3584]{2,1,0:T(8,128)(2,1)} async-done(((bf16[8,64,3584]{2,1,0:T(8,128)(2,1)}), bf16[8,64,3584]{2,1,0:T(8,128)(2,1)}, u32[]{:S(2)}, u32[]{:S(2)}) %all-to-all-start.3) | async-done | bytes 3670048 | tf_op jit(solution)/shard_map/all_to_all | solution.py:104
  298.4 6.0 %gather_fusion.3 = bf16[256,3584]{1,0:T(8,128)(2,1)S(1)} fusion(bf16[512,3584]{1,0:T(8,128)(2,1)} %bitcast.12, s32[1024]{0:T(1024)S(1)} %pad_clamp_fusion), kind=kCustom, calls=%fused_computation.3 | custom fusion | bytes 3671040 | tf_op jit(solution)/shard_map/gather | solution.py:111
  306.1 7.1 %reduce_sum.34 = bf16[128,3584]{1,0:T(8,128)(2,1)} reduce(bf16[128,2,3584]{2,1,0:T(2,128)(2,1)} %reshape.125, bf16[]{:T(256)} %constant.46.clone.1), dimensions={1}, to_apply=%region_4.5 | reduce | flops 458752 | bytes 2752514 | tf_op jit(solution)/shard_map/reduce_sum | solution.py:112
  313.2 92.3 %reduce-scatter.4.cloned.1.call-done = bf16[224,3072]{1,0:T(8,128)(2,1)} async-done(((bf16[3584,3072]{1,0:T(8,128)(2,1)}), bf16[224,3072]{1,0:T(8,128)(2,1)}) %reduce-scatter.4.cloned.1.call-update) | async-done | bytes 1376272
  (52 shorter events, 13.5 us)
Async XLA Ops:
  7.2 15.4 %copy-start = (bf16[128,3584]{1,0:T(8,128)(2,1)S(1)}, bf16[128,3584]{1,0:T(8,128)(2,1)}, u32[]{:S(2)}) copy-start(bf16[128,3584]{1,0:T(8,128)(2,1)} %param.7) | copy-start | bytes 2752516
  17.0 19.4 %all-to-all-start = ((bf16[8,1,64]{2,1,0:T(2,128)(2,1)}), bf16[8,1,64]{2,1,0:T(2,128)(2,1)S(1)}, u32[]{:S(2)}, u32[]{:S(2)}) async-start(bf16[8,1,64]{2,1,0:T(2,128)(2,1)} %all_to_all.25), calls=%async_computation | async-start | bytes 8192 | tf_op jit(solution)/shard_map/all_to_all | solution.py:80
  22.6 4.2 %copy-start.2 = (bf16[128,3584]{1,0:T(8,128)(2,1)S(1)}, bf16[128,3584]{1,0:T(8,128)(2,1)}, u32[]{:S(2)}) copy-start(bf16[128,3584]{1,0:T(8,128)(2,1)} %param.8) | copy-start | bytes 2752516
  85.5 46.9 %all-to-all-start.1 = ((bf16[8,64,3584]{2,1,0:T(8,128)(2,1)}), bf16[8,64,3584]{2,1,0:T(8,128)(2,1)}, u32[]{:S(2)}, u32[]{:S(2)}) async-start(bf16[8,64,3584]{2,1,0:T(8,128)(2,1)} %get-tuple-element.30), calls=%async_computation.1 | async-start | bytes 7340032 | tf_op jit(solution)/shard_map/all_to_all | solution.py:79
  90.0 315.5 %reduce-scatter.4.cloned.1.call-start = ((), (), s32[]{:S(2)}) async-start(), calls=%async_computation.6 | async-start | bytes 23396352
  90.1 9.6 %copy-start.3 = (bf16[8,64,3584]{2,1,0:T(8,128)(2,1)S(1)}, bf16[8,64,3584]{2,1,0:T(8,128)(2,1)}, u32[]{:S(2)}) copy-start(bf16[8,64,3584]{2,1,0:T(8,128)(2,1)} %all_to_all.31) | copy-start | bytes 11010052
  142.5 8.8 %copy-start.5 = (bf16[512,1024]{1,0:T(8,128)(2,1)}, bf16[512,1024]{1,0:T(8,128)(2,1)S(1)}, u32[]{:S(2)}) copy-start(bf16[512,1024]{1,0:T(8,128)(2,1)S(1)} %get-tuple-element.25) | copy-start | bytes 3145732
  142.5 8.8 %copy-start.4 = (bf16[8,64,3584]{2,1,0:T(8,128)(2,1)S(1)}, bf16[8,64,3584]{2,1,0:T(8,128)(2,1)}, u32[]{:S(2)}) copy-start(bf16[8,64,3584]{2,1,0:T(8,128)(2,1)} %all_to_all.31) | copy-start | bytes 11010052
  215.5 20.1 %all-to-all-start.4 = ((bf16[8,1,64]{2,1,0:T(2,128)(2,1)}), bf16[8,1,64]{2,1,0:T(2,128)(2,1)S(1)}, u32[]{:S(2)}, u32[]{:S(2)}) async-start(bf16[8,1,64]{2,1,0:T(2,128)(2,1)} %convert_element_type.73), calls=%async_computation.4 | async-start | bytes 8192 | tf_op jit(solution)/shard_map/all_to_all | solution.py:107
  235.6 62.8 %all-to-all-start.3 = ((bf16[8,64,3584]{2,1,0:T(8,128)(2,1)}), bf16[8,64,3584]{2,1,0:T(8,128)(2,1)}, u32[]{:S(2)}, u32[]{:S(2)}) async-start(bf16[8,64,3584]{2,1,0:T(8,128)(2,1)} %bitcast.50), calls=%async_computation.3 | async-start | bytes 7340032 | tf_op jit(solution)/shard_map/all_to_all | solution.py:104
  306.1 104.3 %copy-start.1 = (bf16[128,3584]{1,0:T(8,128)(2,1)S(1)}, bf16[128,3584]{1,0:T(8,128)(2,1)}, u32[]{:S(2)}) copy-start(bf16[128,3584]{1,0:T(8,128)(2,1)} %param.7) | copy-start | bytes 2752516
Sparse Core Ops, SparseCore 0:
  214.9 190.4 reduce-scatter.3
where the time goes:
time: 419 us; the launch traced here: 417 us
  waiting for transfers between devices  172 us (41%)
  matrix products  64.3 us (15%)
  local copies, waits for them, and re-layouts  61.5 us (15%)
  blocking collectives  49 us (12%)
  other arithmetic  37.6 us (9%)
  starting transfers between devices  19.1 us (5%)
  between operations  14.2 us (3%)
    unnamed x2, waiting for transfers between devices  92.3 us
    all_to_all x1, waiting for transfers between devices, local(): lax.all_to_all(row_grad.reshape(experts, CAP, D), 'expert', split_axis=0,...  54.3 us
    all_to_all x1, blocking collectives, local(): lax.all_to_all(send_tokens, 'expert', split_axis=0, concat_axis=0, tiled=...  49 us
    unnamed x21, local copies, waits for them, and re-layouts  33.6 us
    all_to_all x1, waiting for transfers between devices, local(): lax.all_to_all(send_grads, 'expert', split_axis=0, concat_axis=0, tiled=T...  25 us
    concatenate x1, other arithmetic, local(): jnp.concatenate([contract_rows(row_tokens, paired), contract_rows(weighte...  23.4 us
    dot_general x2, matrix products, contract_rows(): lax.dot_general(left_rows, right_rows, (((0,), (0,)), ((), ())), preferre...  20.2 us
    dot_general x1, matrix products, expert_rows(): jnp.dot(row_grads, down_weight, preferred_element_type=jnp.float32)  10.2 us
  transfers between devices with their start and end apart: 5, of which 3 were waited for; matrix products, arithmetic and copies ran while one was open for 16% of the time, Pallas kernels for 0%

commit v1 on v0

v1 whole, which is shorter than its diff:
```python
import functools

import jax
import jax.numpy as jnp
from jax import lax
from jax.experimental import pallas as pl
from jax.experimental.pallas import tpu as pltpu
from jax.sharding import PartitionSpec as P

D = 3584
FF = 1024
TOP = 2
CAP = 64
EXPERTS = 8
ROWS = EXPERTS * CAP
TOK = 128
EXTRA = 128
WIDE = D + EXTRA
TILE = 512
NT = D // TILE
NZ = 4
ZB = D // NZ
SUB = ZB // 4
HALF = FF // 2
BF = jnp.bfloat16
F32 = jnp.float32
FIRST = (((0,), (0,)), ((), ()))
LAST = (((1,), (1,)), ((), ()))
MB = 1 << 20


def params(limit=48):
    return pltpu.CompilerParams(vmem_limit_bytes=limit * MB)


def cost(flops, nbytes, trans=0):
    return pl.CostEstimate(flops=flops, bytes_accessed=nbytes, transcendentals=trans)


def place_kernel(routes_ref, tokens_ref, picks_ref, out_ref):
    @pl.when(pl.program_id(0) == 0)
    def _():
        routes = routes_ref[...]
        ids = lax.broadcasted_iota(jnp.int32, (TOK, EXPERTS), 1)
        first = (routes[:, 0:1] == ids).astype(F32).astype(BF)
        second = (routes[:, 1:2] == ids).astype(F32).astype(BF)
        row = lax.broadcasted_iota(jnp.int32, (TOK, TOK), 0)
        col = lax.broadcasted_iota(jnp.int32, (TOK, TOK), 1)
        before = (row < col).astype(F32).astype(BF)
        same = (row == col).astype(F32).astype(BF)
        rank = lax.dot_general(first + second, before, FIRST, preferred_element_type=F32)
        slot = lax.broadcasted_iota(jnp.int32, (CAP, TOK), 0).astype(F32)
        for k, named in enumerate((first, second)):
            named_t = lax.dot_general(named, same, FIRST, preferred_element_type=F32)
            for e in range(EXPERTS):
                hit = (slot == rank[e : e + 1, :]) & (named_t[e : e + 1, :] > 0.5)
                picks_ref[k, e * CAP : (e + 1) * CAP, :] = hit.astype(F32).astype(BF)

    both = picks_ref[0] + picks_ref[1]
    out_ref[...] = jnp.dot(both, tokens_ref[...], preferred_element_type=F32).astype(BF)


def place_tokens(routes, tokens):
    return pl.pallas_call(
        place_kernel,
        grid=(NT,),
        in_specs=[
            pl.BlockSpec((TOK, TOP), lambda i: (0, 0)),
            pl.BlockSpec((TOK, TILE), lambda i: (0, i)),
        ],
        out_specs=[
            pl.BlockSpec((TOP, ROWS, TOK), lambda i: (0, 0, 0)),
            pl.BlockSpec((ROWS, TILE), lambda i: (0, i)),
        ],
        out_shape=[
            jax.ShapeDtypeStruct((TOP, ROWS, TOK), BF),
            jax.ShapeDtypeStruct((ROWS, D), BF),
        ],
        compiler_params=params(),
        cost_estimate=cost(2 * ROWS * TOK * D, 5 * MB),
    )(routes, tokens)


def grads_kernel(picks_ref, probs_ref, grads_ref, out_ref):
    step = pl.program_id(0)

    @pl.when(step < NT)
    def _():
        both = picks_ref[0] + picks_ref[1]
        out_ref[...] = jnp.dot(both, grads_ref[...], preferred_element_type=F32).astype(BF)

    @pl.when(step == NT)
    def _():
        probs = probs_ref[...].astype(F32)
        p0 = jnp.broadcast_to(probs[:, 0:1], (TOK, EXTRA)).astype(BF)
        p1 = jnp.broadcast_to(probs[:, 1:2], (TOK, EXTRA)).astype(BF)
        spread = jnp.dot(picks_ref[0], p0, preferred_element_type=F32)
        spread = spread + jnp.dot(picks_ref[1], p1, preferred_element_type=F32)
        out_ref[:, :EXTRA] = spread.astype(BF)


def place_grads(picks, probs, grads):
    return pl.pallas_call(
        grads_kernel,
        grid=(NT + 1,),
        in_specs=[
            pl.BlockSpec((TOP, ROWS, TOK), lambda i: (0, 0, 0)),
            pl.BlockSpec((TOK, TOP), lambda i: (0, 0)),
            pl.BlockSpec((TOK, TILE), lambda i: (0, jnp.minimum(i, NT - 1))),
        ],
        out_specs=pl.BlockSpec((ROWS, TILE), lambda i: (0, i)),
        out_shape=jax.ShapeDtypeStruct((ROWS, WIDE), BF),
        compiler_params=params(),
        cost_estimate=cost(2 * ROWS * TOK * D, 5 * MB),
    )(picks, probs, grads)


def forward_kernel(x_ref, gate_ref, up_ref, hidden_ref, active_ref, slope_ref):
    x = x_ref[...]
    gate = jnp.dot(x, gate_ref[...], preferred_element_type=F32)
    up = jnp.dot(x, up_ref[...], preferred_element_type=F32)
    s = jax.nn.sigmoid(gate)
    active = gate * s
    hidden_ref[...] = (active * up).astype(BF)
    active_ref[...] = active
    slope_ref[...] = up * s * (1.0 + gate * (1.0 - s))


def forward(x, gate, up):
    n = 256
    return pl.pallas_call(
        forward_kernel,
        grid=(FF // n,),
        in_specs=[
            pl.BlockSpec((ROWS, D), lambda i: (0, 0)),
            pl.BlockSpec((D, n), lambda i: (0, i)),
            pl.BlockSpec((D, n), lambda i: (0, i)),
        ],
        out_specs=[pl.BlockSpec((ROWS, n), lambda i: (0, i))] * 3,
        out_shape=[
            jax.ShapeDtypeStruct((ROWS, FF), BF),
            jax.ShapeDtypeStruct((ROWS, FF), F32),
            jax.ShapeDtypeStruct((ROWS, FF), F32),
        ],
        compiler_params=params(),
        cost_estimate=cost(4 * ROWS * D * FF, 23 * MB, ROWS * FF),
    )(x, gate, up)


def backward_kernel(g_ref, down_ref, hidden_ref, active_ref, slope_ref, gg_ref, gu_ref, wg_ref, total):
    step = pl.program_id(0)
    back = jnp.dot(g_ref[:, :D], down_ref[...], preferred_element_type=F32)
    part = jnp.sum(back * hidden_ref[...].astype(F32), axis=1, keepdims=True)

    @pl.when(step == 0)
    def _():
        total[...] = jnp.zeros_like(total)

    total[...] += jnp.broadcast_to(part, total.shape)
    scaled = g_ref[:, D : D + 1].astype(F32) * back
    gg_ref[...] = (scaled * slope_ref[...]).astype(BF)
    gu_ref[...] = (scaled * active_ref[...]).astype(BF)
    wg_ref[...] = total[...].astype(BF)


def backward(g, down, hidden, active, slope):
    n = 256
    tile = pl.BlockSpec((ROWS, n), lambda i: (0, i))
    return pl.pallas_call(
        backward_kernel,
        grid=(FF // n,),
        in_specs=[
            pl.BlockSpec((ROWS, WIDE), lambda i: (0, 0)),
            pl.BlockSpec((D, n), lambda i: (0, i)),
            tile,
            tile,
            tile,
        ],
        out_specs=[tile, tile, pl.BlockSpec((ROWS, EXTRA), lambda i: (0, 0))],
        out_shape=[
            jax.ShapeDtypeStruct((ROWS, FF), BF),
            jax.ShapeDtypeStruct((ROWS, FF), BF),
            jax.ShapeDtypeStruct((ROWS, EXTRA), BF),
        ],
        scratch_shapes=[pltpu.VMEM((ROWS, EXTRA), F32)],
        compiler_params=params(),
        cost_estimate=cost(2 * ROWS * D * FF, 18 * MB),
    )(g, down, hidden, active, slope)


def rows_kernel(gg_ref, gu_ref, gate_ref, up_ref, wg_ref, out_ref):
    step = pl.program_id(0)

    @pl.when(step < NT)
    def _():
        grad = lax.dot_general(gg_ref[...], gate_ref[...], LAST, preferred_element_type=F32)
        grad = grad + lax.dot_general(gu_ref[...], up_ref[...], LAST, preferred_element_type=F32)
        out_ref[...] = grad.astype(BF)

    @pl.when(step == NT)
    def _():
        out_ref[:, :EXTRA] = wg_ref[...]


def row_grads(gg, gu, gate, up, wg):
    clamp = lambda i: (jnp.minimum(i, NT - 1), 0)
    return pl.pallas_call(
        rows_kernel,
        grid=(NT + 1,),
        in_specs=[
            pl.BlockSpec((ROWS, FF), lambda i: (0, 0)),
            pl.BlockSpec((ROWS, FF), lambda i: (0, 0)),
            pl.BlockSpec((TILE, FF), clamp),
            pl.BlockSpec((TILE, FF), clamp),
            pl.BlockSpec((ROWS, EXTRA), lambda i: (0, 0)),
        ],
        out_specs=pl.BlockSpec((ROWS, TILE), lambda i: (0, i)),
        out_shape=jax.ShapeDtypeStruct((ROWS, WIDE), BF),
        compiler_params=params(),
        cost_estimate=cost(4 * ROWS * D * FF, 21 * MB),
    )(gg, gu, gate, up, wg)


def partial_kernel(scaled, place_ref, x_ref, p_ref, h_ref, send_ref, keep_ref):
    x = x_ref[...]
    if scaled:
        x = (p_ref[:, 0:1].astype(F32) * x.astype(F32)).astype(BF)
    part = lax.dot_general(x, h_ref[...], FIRST, preferred_element_type=F32).astype(BF)
    odd = place_ref[2] == 1
    for j in range(2):
        even_rows = part[2 * j * SUB : (2 * j + 1) * SUB]
        odd_rows = part[(2 * j + 1) * SUB : (2 * j + 2) * SUB]
        rows = slice(j * SUB, (j + 1) * SUB)
        send_ref[0, rows, :] = jnp.where(odd, even_rows, odd_rows)
        keep_ref[0, rows, :] = jnp.where(odd, odd_rows, even_rows)


def partial(place, x, p, h, scaled):
    last = (p.shape[1] // EXTRA) - 1
    return pl.pallas_call(
        functools.partial(partial_kernel, scaled),
        grid_spec=pltpu.PrefetchScalarGridSpec(
            num_scalar_prefetch=1,
            grid=(2,),
            in_specs=[
                pl.BlockSpec((ROWS, ZB), lambda i, place: (0, place[i])),
                pl.BlockSpec((ROWS, EXTRA), lambda i, place: (0, last)),
                pl.BlockSpec((ROWS, HALF), lambda i, place: (0, i)),
            ],
            out_specs=[pl.BlockSpec((1, 2 * SUB, HALF), lambda i, place: (i, 0, 0))] * 2,
        ),
        out_shape=[jax.ShapeDtypeStruct((2, 2 * SUB, HALF), BF)] * 2,
        compiler_params=params(),
        cost_estimate=cost(2 * ROWS * ZB * FF, 5 * MB),
    )(place, x, p, h)


def combine_kernel(picks_ref, rows_ref, tokens_ref, weights_ref):
    step = pl.program_id(0)

    @pl.when(step < NT)
    def _():
        both = picks_ref[0] + picks_ref[1]
        tokens_ref[...] = lax.dot_general(
            both, rows_ref[...], FIRST, preferred_element_type=F32
        ).astype(BF)

    @pl.when(step == NT)
    def _():
        found = [
            lax.dot_general(
                picks_ref[k], rows_ref[:, :EXTRA], FIRST, preferred_element_type=F32
            )
            for k in range(TOP)
        ]
        lane = lax.broadcasted_iota(jnp.int32, (TOK, EXTRA), 1)
        weights_ref[...] = jnp.where(lane == 0, found[0], found[1]).astype(BF)[:, :TOP]


def combine(picks, rows):
    return pl.pallas_call(
        combine_kernel,
        grid=(NT + 1,),
        in_specs=[
            pl.BlockSpec((TOP, ROWS, TOK), lambda i: (0, 0, 0)),
            pl.BlockSpec((ROWS, TILE), lambda i: (0, i)),
        ],
        out_specs=[
            pl.BlockSpec((TOK, TILE), lambda i: (0, jnp.minimum(i, NT - 1))),
            pl.BlockSpec((TOK, TOP), lambda i: (0, 0)),
        ],
        out_shape=[
            jax.ShapeDtypeStruct((TOK, D), BF),
            jax.ShapeDtypeStruct((TOK, TOP), BF),
        ],
        compiler_params=params(),
        cost_estimate=cost(2 * ROWS * TOK * D, 5 * MB),
    )(picks, rows)


def moves(f):
    pairs = []
    for z in range(NZ):
        for x in range(2):
            for c in range(2):
                tz, tx, tc = f(z, x, c)
                pairs.append((z * 4 + x * 2 + c, (tz % NZ) * 4 + tx * 2 + tc))
    return pairs


TO_CORE = moves(lambda z, x, c: (z, x, 1 - c))
TO_UP = moves(lambda z, x, c: (z + 1, x, c))
TO_DOWN = moves(lambda z, x, c: (z - 1, x, c))
TO_X = moves(lambda z, x, c: (z, 1 - x, c))


def add(*parts):
    total = parts[0].astype(F32)
    for part in parts[1:]:
        total = total + part.astype(F32)
    return total.astype(BF)


def summed(z, x, c, left, p, right, scaled):
    up = down = None
    for step in range(NZ):
        place = jnp.stack([(z - 1 - step) % NZ, (z + 1 + step) % NZ, c]).astype(jnp.int32)
        send, keep = partial(place, left, p, right, scaled)
        other = lax.ppermute(send, "dp", TO_CORE)
        if step == 0:
            up, down = add(keep[0], other[0]), add(keep[1], other[1])
        else:
            up, down = add(keep[0], other[0], up), add(keep[1], other[1], down)
        if step < NZ - 1:
            up = lax.ppermute(up, "dp", TO_UP)
            down = lax.ppermute(down, "dp", TO_DOWN)
    full = jnp.concatenate([up.reshape(2, SUB, HALF), down.reshape(2, SUB, HALF)], axis=2)
    mine = jnp.where(x == 0, full[0], full[1])
    away = lax.ppermute(jnp.where(x == 0, full[1], full[0]), "dp", TO_X)
    return add(mine, away)[None]


def exchange(rows):
    width = rows.shape[1]
    out = lax.all_to_all(
        rows.reshape(EXPERTS, CAP, width), "expert", split_axis=0, concat_axis=0, tiled=True
    )
    return out.reshape(ROWS, width)


def local(tokens, grad_out, routes, probs, w_gate, w_up, w_down):
    where = lax.axis_index("dp")
    z, x, c = where // 4, (where // 2) % 2, where % 2
    gate, up, down = w_gate[0], w_up[0], w_down[0]
    picks, send_tokens = place_tokens(routes, tokens)
    row_tokens = exchange(send_tokens)
    send_grads = place_grads(picks, probs, grad_out)
    row_grads_in = exchange(send_grads)
    hidden, active, slope = forward(row_tokens, gate, up)
    gg, gu, wg = backward(row_grads_in, down, hidden, active, slope)
    grad_down = summed(z, x, c, row_grads_in, row_grads_in, hidden, True)
    grad_gate = summed(z, x, c, row_tokens, row_grads_in, gg, False)
    grad_up = summed(z, x, c, row_tokens, row_grads_in, gu, False)
    returned = exchange(row_grads(gg, gu, gate, up, wg))
    grad_tokens, grad_weights = combine(picks, returned)
    return (grad_tokens, grad_weights, grad_gate, grad_up, grad_down)


def solution(mesh):
    spec = P(("dp", "expert"), None)
    weight = P("expert", None, None)
    out = P("expert", "dp", None)
    return jax.shard_map(
        local,
        mesh=mesh,
        in_specs=(spec, spec, spec, spec, weight, weight, weight),
        out_specs=(spec, spec, out, out, out),
        check_vma=False,
    )
```

time: 419 us -> 299 us (0.71)
  Pallas kernels: 0 us -> 88.9 us
  matrix products: 64.3 us -> 0 us
  waiting for transfers between devices: 172 us -> 113 us
  blocking collectives: 49 us -> 0 us
  local copies, waits for them, and re-layouts: 61.5 us -> 20.1 us
  starting transfers between devices: 19.1 us -> 53.4 us
  other arithmetic: 37.6 us -> 21.3 us
  between operations: 14.2 us -> 1.25 us
    unnamed x2 -> x0, waiting for transfers between devices: 92.3 us -> none
    pallas_call x0 -> x18, Pallas kernels: none -> 88.9 us  [the longest x12 43.7 us: partial(): pl.pallas_call(functools.partial(partial_kernel, scaled), grid_spec=pltpu...]
    dot_general x7 -> x0, matrix products: 64.3 us -> none  [the longest x2 20.2 us: contract_rows(): lax.dot_general(left_rows, right_rows, (((0,), (0,)), ((), ())), preferre...]
    all_to_all x1 -> x0, blocking collectives: 49 us -> none  [local(): lax.all_to_all(send_tokens, 'expert', split_axis=0, concat_axis=0, tiled=...]
    ppermute x0 -> x33, waiting for transfers between devices: none -> 44.6 us  [the longest x9 19.3 us: summed(): down = lax.ppermute(down, 'dp', TO_DOWN)]
    ppermute x0 -> x33, starting transfers between devices: none -> 38.7 us  [the longest x9 24.8 us: summed(): down = lax.ppermute(down, 'dp', TO_DOWN)]
    concatenate x2 -> x0, other arithmetic: 23.4 us -> none  [the longest x1 23.4 us: local(): jnp.concatenate([contract_rows(row_tokens, paired), contract_rows(weighte...]
    gather x5 -> x0, local copies, waits for them, and re-layouts: 20.9 us -> none  [the longest x1 6.04 us: local(): returned_rows.reshape(slot_rows, D)[slot_ids].reshape(tok_dev, TOP, D)]
  transfers between devices with their start and end apart: 5 -> 36, of which waited for: 3 -> 12; matrix products, arithmetic and copies ran while one was open for 16% -> 7% of each run, Pallas kernels for 0% -> 22%
where the time goes in v1:
time: 299 us; the launch traced here: 298 us
  waiting for transfers between devices  113 us (38%)
  Pallas kernels  88.9 us (30%)
  starting transfers between devices  53.4 us (18%)
  other arithmetic  21.3 us (7%)
  local copies, waits for them, and re-layouts  20.1 us (7%)
    all_to_all x3, waiting for transfers between devices, exchange(): lax.all_to_all(rows.reshape(EXPERTS, CAP, width), 'expert', split_axis=0,...  68.3 us
    pallas_call x12, Pallas kernels, partial(): pl.pallas_call(functools.partial(partial_kernel, scaled), grid_spec=pltpu...  43.7 us
    ppermute x9, starting transfers between devices, summed(): down = lax.ppermute(down, 'dp', TO_DOWN)  24.8 us
    unnamed x77, local copies, waits for them, and re-layouts  20.1 us
    ppermute x9, waiting for transfers between devices, summed(): down = lax.ppermute(down, 'dp', TO_DOWN)  19.3 us
    convert_element_type x12, other arithmetic, add(): return total.astype(BF)  18 us
    all_to_all x3, starting transfers between devices, exchange(): lax.all_to_all(rows.reshape(EXPERTS, CAP, width), 'expert', split_axis=0,...  14.8 us
    ppermute x9, waiting for transfers between devices, summed(): up = lax.ppermute(up, 'dp', TO_UP)  13.5 us
  transfers between devices with their start and end apart: 36, of which 12 were waited for; matrix products, arithmetic and copies ran while one was open for 7% of the time, Pallas kernels for 22%

profile of v1, /device:TPU:0, one launch (start us, length us, event | category | flops | bytes accessed | tf_op | source)
XLA Modules:
  0.0 297.9 jit_solution(7725765649569008657)
XLA Ops:
  7.0 5.6 %all-to-all-start.1 = ((bf16[8,64,3584]{2,1,0:T(8,128)(2,1)}), bf16[8,64,3584]{2,1,0:T(8,128)(2,1)}, u32[]{:S(2)}, u32[]{:S(2)}) async-start(bf16[8,64,3584]{2,1,0:T(8,128)(2,1)} %bitcast.131), calls=%async_computation.1 | async-start | bytes 7340032 | tf_op jit(solution)/shard_map/all_to_all | solution.py:345
  17.6 39.0 %all-to-all-done.1 = bf16[8,64,3584]{2,1,0:T(8,128)(2,1)} async-done(((bf16[8,64,3584]{2,1,0:T(8,128)(2,1)}), bf16[8,64,3584]{2,1,0:T(8,128)(2,1)}, u32[]{:S(2)}, u32[]{:S(2)}) %all-to-all-start.1) | async-done | bytes 3670048 | tf_op jit(solution)/shard_map/all_to_all | solution.py:345
  56.6 4.5 %all-to-all-start = ((bf16[8,64,3712]{2,1,0:T(8,128)(2,1)}), bf16[8,64,3712]{2,1,0:T(8,128)(2,1)}, u32[]{:S(2)}, u32[]{:S(2)}) async-start(bf16[8,64,3712]{2,1,0:T(8,128)(2,1)} %bitcast.129), calls=%async_computation | async-start | bytes 7602176 | tf_op jit(solution)/shard_map/all_to_all | solution.py:345
  61.2 12.2 %shard_map.112 = (bf16[512,1024]{1,0:T(8,128)(2,1)S(1)}, f32[512,1024]{1,0:T(8,128)S(1)}, f32[512,1024]{1,0:T(8,128)S(1)}) custom-call(bf16[512,3584]{1,0:T(8,128)(2,1)} %bitcast.4.x_ref, bf16[3584,1024]{1,0:T(8,128)(2,1)} %bitcast.145, bf16[3584,1024]{1,0:T(8,128)(2,1)} %bitcast.147), custom_call_target="tpu_custom_call" | custom-call | flops 7516192768 | bytes 24117248 | tf_op jit(solution)/shard_map/pallas_call | solution.py:131
  76.1 29.3 %all-to-all-done = bf16[8,64,3712]{2,1,0:T(8,128)(2,1)} async-done(((bf16[8,64,3712]{2,1,0:T(8,128)(2,1)}), bf16[8,64,3712]{2,1,0:T(8,128)(2,1)}, u32[]{:S(2)}, u32[]{:S(2)}) %all-to-all-start) | async-done | bytes 3801120 | tf_op jit(solution)/shard_map/all_to_all | solution.py:345
  107.0 8.9 %shard_map.113 = (bf16[512,1024]{1,0:T(8,128)(2,1)S(1)}, bf16[512,1024]{1,0:T(8,128)(2,1)S(1)}, bf16[512,128]{1,0:T(8,128)(2,1)S(1)}) custom-call(bf16[512,3712]{1,0:T(8,128)(2,1)} %bitcast.1.g_ref.p_ref.x_ref, bf16[3584,1024]{1,0:T(8,128)(2,1)} %bitcast.132, bf16[512,1024]{1,0:T(8,128)(2,1)S(1)} %get-tuple-element.41.hidden_ref.h_ref, ...), custom_call_target="tpu_custom_call" | custom-call | flops 3758096384 | bytes 18874368 | tf_op jit(solution)/shard_map/pallas_call | solution.py:169
  115.9 3.9 %shard_map.119 = (bf16[2,448,512]{2,1,0:T(8,128)(2,1)}, bf16[2,448,512]{2,1,0:T(8,128)(2,1)S(1)}) custom-call(s32[3]{0:T(128)S(1)} %get-tuple-element.105.place_ref, bf16[512,3584]{1,0:T(8,128)(2,1)} %bitcast.4.x_ref, bf16[512,3712]{1,0:T(8,128)(2,1)} %bitcast.1.g_ref.p_ref.x_ref, bf16[512,1024]{1,0:T(8,128)(2,1)S(1)} %get-tuple-element.44.gg_ref.h_ref), custom_call_target="tpu_custom_call" | custom-call | flops 939524096 | bytes 5242880 | tf_op jit(solution)/shard_map/pallas_call | solution.py:240
  120.7 3.9 %shard_map.118 = (bf16[2,448,512]{2,1,0:T(8,128)(2,1)}, bf16[2,448,512]{2,1,0:T(8,128)(2,1)S(1)}) custom-call(s32[3]{0:T(128)S(1)} %get-tuple-element.104.place_ref, bf16[512,3584]{1,0:T(8,128)(2,1)} %bitcast.4.x_ref, bf16[512,3712]{1,0:T(8,128)(2,1)} %bitcast.1.g_ref.p_ref.x_ref, bf16[512,1024]{1,0:T(8,128)(2,1)S(1)} %get-tuple-element.44.gg_ref.h_ref), custom_call_target="tpu_custom_call" | custom-call | flops 939524096 | bytes 5242880 | tf_op jit(solution)/shard_map/pallas_call | solution.py:240
  126.1 3.9 %shard_map.123 = (bf16[2,448,512]{2,1,0:T(8,128)(2,1)}, bf16[2,448,512]{2,1,0:T(8,128)(2,1)S(1)}) custom-call(s32[3]{0:T(128)S(1)} %get-tuple-element.105.place_ref, bf16[512,3584]{1,0:T(8,128)(2,1)} %bitcast.4.x_ref, bf16[512,3712]{1,0:T(8,128)(2,1)} %bitcast.1.g_ref.p_ref.x_ref, bf16[512,1024]{1,0:T(8,128)(2,1)S(1)} %get-tuple-element.45.gu_ref.h_ref), custom_call_target="tpu_custom_call" | custom-call | flops 939524096 | bytes 5242880 | tf_op jit(solution)/shard_map/pallas_call | solution.py:240
  130.9 4.1 %shard_map.127 = (bf16[2,448,512]{2,1,0:T(8,128)(2,1)}, bf16[2,448,512]{2,1,0:T(8,128)(2,1)S(1)}) custom-call(s32[3]{0:T(128)S(1)} %get-tuple-element.105.place_ref, bf16[512,3712]{1,0:T(8,128)(2,1)} %bitcast.1.g_ref.p_ref.x_ref, bf16[512,3712]{1,0:T(8,128)(2,1)} %bitcast.1.g_ref.p_ref.x_ref, bf16[512,1024]{1,0:T(8,128)(2,1)S(1)} %get-tuple-element.41.hidden_ref.h_ref), custom_call_target="tpu_custom_call" | custom-call | flops 939524096 | bytes 5242880 | tf_op jit(solution)/shard_map/pallas_call | solution.py:240
  149.0 3.9 %shard_map.121 = (bf16[2,448,512]{2,1,0:T(8,128)(2,1)}, bf16[2,448,512]{2,1,0:T(8,128)(2,1)S(1)}) custom-call(s32[3]{0:T(128)S(1)} %get-tuple-element.103.place_ref, bf16[512,3584]{1,0:T(8,128)(2,1)} %bitcast.4.x_ref, bf16[512,3712]{1,0:T(8,128)(2,1)} %bitcast.1.g_ref.p_ref.x_ref, bf16[512,1024]{1,0:T(8,128)(2,1)S(1)} %get-tuple-element.45.gu_ref.h_ref), custom_call_target="tpu_custom_call" | custom-call | flops 939524096 | bytes 5242880 | tf_op jit(solution)/shard_map/pallas_call | solution.py:240
  163.5 7.3 %collective-permute-done.4 = bf16[448,512]{1,0:T(8,128)(2,1)S(1)} collective-permute-done((bf16[448,512]{1,0:T(8,128)(2,1)S(1)}, bf16[448,512]{1,0:T(8,128)(2,1)S(1)}, u32[]{:S(2)}, u32[]{:S(2)}) %collective-permute-start.4) | collective-permute-done | bytes 458784 | tf_op jit(solution)/shard_map/ppermute | solution.py:335
  172.9 4.1 %shard_map.125 = (bf16[2,448,512]{2,1,0:T(8,128)(2,1)}, bf16[2,448,512]{2,1,0:T(8,128)(2,1)S(1)}) custom-call(s32[3]{0:T(128)S(1)} %get-tuple-element.103.place_ref, bf16[512,3712]{1,0:T(8,128)(2,1)} %bitcast.1.g_ref.p_ref.x_ref, bf16[512,3712]{1,0:T(8,128)(2,1)} %bitcast.1.g_ref.p_ref.x_ref, bf16[512,1024]{1,0:T(8,128)(2,1)S(1)} %get-tuple-element.41.hidden_ref.h_ref), custom_call_target="tpu_custom_call" | custom-call | flops 939524096 | bytes 5242880 | tf_op jit(solution)/shard_map/pallas_call | solution.py:240
  177.9 3.9 %shard_map.116 = (bf16[2,448,512]{2,1,0:T(8,128)(2,1)}, bf16[2,448,512]{2,1,0:T(8,128)(2,1)S(1)}) custom-call(s32[3]{0:T(128)S(1)} %get-tuple-element.102.place_ref, bf16[512,3584]{1,0:T(8,128)(2,1)} %bitcast.4.x_ref, bf16[512,3712]{1,0:T(8,128)(2,1)} %bitcast.1.g_ref.p_ref.x_ref, bf16[512,1024]{1,0:T(8,128)(2,1)S(1)} %get-tuple-element.44.gg_ref.h_ref), custom_call_target="tpu_custom_call" | custom-call | flops 939524096 | bytes 5242880 | tf_op jit(solution)/shard_map/pallas_call | solution.py:240
  190.0 11.9 %shard_map.114 = bf16[512,3712]{1,0:T(8,128)(2,1)S(1)} custom-call(bf16[512,1024]{1,0:T(8,128)(2,1)S(1)} %get-tuple-element.44.gg_ref.h_ref, bf16[512,1024]{1,0:T(8,128)(2,1)S(1)} %get-tuple-element.45.gu_ref.h_ref, bf16[3584,1024]{1,0:T(8,128)(2,1)} %bitcast.146, bf16[3584,1024]{1,0:T(8,128)(2,1)} %bitcast.148, bf16[512,128]{1,0:T(8,128)(2,1)S(1)} %get-tuple-element.46.wg_ref), custom_call_target="tpu_custom_call" | custom-call | flops 7516192768 | bytes 22020096 | tf_op jit(solution)/shard_map/pallas_call | solution.py:207
  203.8 4.7 %all-to-all-start.2 = ((bf16[8,64,3712]{2,1,0:T(8,128)(2,1)}), bf16[8,64,3712]{2,1,0:T(8,128)(2,1)}, u32[]{:S(2)}, u32[]{:S(2)}) async-start(bf16[8,64,3712]{2,1,0:T(8,128)(2,1)} %bitcast.130), calls=%async_computation.2 | async-start | bytes 7602176 | tf_op jit(solution)/shard_map/all_to_all | solution.py:345
  215.1 6.1 %collective-permute-done.8 = bf16[448,512]{1,0:T(8,128)(2,1)S(1)} collective-permute-done((bf16[448,512]{1,0:T(8,128)(2,1)}, bf16[448,512]{1,0:T(8,128)(2,1)S(1)}, u32[]{:S(2)}, u32[]{:S(2)}) %collective-permute-start.8) | collective-permute-done | bytes 458784 | tf_op jit(solution)/shard_map/ppermute | solution.py:336
  241.6 4.1 %collective-permute-done.30 = bf16[448,512]{1,0:T(8,128)(2,1)S(1)} collective-permute-done((bf16[448,512]{1,0:T(8,128)(2,1)S(1)}, bf16[448,512]{1,0:T(8,128)(2,1)S(1)}, u32[]{:S(2)}, u32[]{:S(2)}) %collective-permute-start.30) | collective-permute-done | bytes 458784 | tf_op jit(solution)/shard_map/ppermute | solution.py:336
  245.7 4.7 %collective-permute-done.6 = bf16[448,512]{1,0:T(8,128)(2,1)S(1)} collective-permute-done((bf16[448,512]{1,0:T(8,128)(2,1)S(1)}, bf16[448,512]{1,0:T(8,128)(2,1)S(1)}, u32[]{:S(2)}, u32[]{:S(2)}) %collective-permute-start.6) | collective-permute-done | bytes 458784 | tf_op jit(solution)/shard_map/ppermute | solution.py:335
  257.1 3.8 %collective-permute-start.31 = (bf16[448,512]{1,0:T(8,128)(2,1)S(1)}, bf16[448,512]{1,0:T(8,128)(2,1)S(1)}, u32[]{:S(2)}, u32[]{:S(2)}) collective-permute-start(bf16[448,512]{1,0:T(8,128)(2,1)S(1)} %get-tuple-element.81), channel_id=1, source_target_pairs={{0,96},{8,104},{16,112},{24,120},{32,0},{40,8},{48,16},{56,24},{64... | collective-permute-start | bytes 1376264 | tf_op jit(solution)/shard_map/ppermute | solution.py:336
  268.7 4.0 %collective-permute-done.31 = bf16[448,512]{1,0:T(8,128)(2,1)S(1)} collective-permute-done((bf16[448,512]{1,0:T(8,128)(2,1)S(1)}, bf16[448,512]{1,0:T(8,128)(2,1)S(1)}, u32[]{:S(2)}, u32[]{:S(2)}) %collective-permute-start.31) | collective-permute-done | bytes 458784 | tf_op jit(solution)/shard_map/ppermute | solution.py:336
  277.0 7.8 %collective-permute-done.21 = bf16[224,1024]{1,0:T(8,128)(2,1)S(1)} collective-permute-done((bf16[224,1024]{1,0:T(8,128)(2,1)S(1)}, bf16[224,1024]{1,0:T(8,128)(2,1)S(1)}, u32[]{:S(2)}, u32[]{:S(2)}) %collective-permute-start.21) | collective-permute-done | bytes 458784 | tf_op jit(solution)/shard_map/ppermute | solution.py:339
  285.7 4.0 %collective-permute-done.32 = bf16[224,1024]{1,0:T(8,128)(2,1)S(1)} collective-permute-done((bf16[224,1024]{1,0:T(8,128)(2,1)S(1)}, bf16[224,1024]{1,0:T(8,128)(2,1)S(1)}, u32[]{:S(2)}, u32[]{:S(2)}) %collective-permute-start.32) | collective-permute-done | bytes 458784 | tf_op jit(solution)/shard_map/ppermute | solution.py:339
  290.6 6.6 %shard_map.115 = (bf16[128,3584]{1,0:T(8,128)(2,1)}, bf16[128,2]{1,0:T(8,128)(2,1)S(1)}) custom-call(bf16[2,512,128]{2,1,0:T(8,128)(2,1)S(1)} %get-tuple-element.39.picks_ref, bf16[512,3712]{1,0:T(8,128)(2,1)} %bitcast.8.rows_ref), custom_call_target="tpu_custom_call" | custom-call | flops 469762048 | bytes 5242880 | tf_op jit(solution)/shard_map/pallas_call | solution.py:281
  (163 shorter events, 104.5 us)
Async XLA Ops:
  7.0 49.5 %all-to-all-start.1 = ((bf16[8,64,3584]{2,1,0:T(8,128)(2,1)}), bf16[8,64,3584]{2,1,0:T(8,128)(2,1)}, u32[]{:S(2)}, u32[]{:S(2)}) async-start(bf16[8,64,3584]{2,1,0:T(8,128)(2,1)} %bitcast.131), calls=%async_computation.1 | async-start | bytes 7340032 | tf_op jit(solution)/shard_map/all_to_all | solution.py:345
  56.6 48.9 %all-to-all-start = ((bf16[8,64,3712]{2,1,0:T(8,128)(2,1)}), bf16[8,64,3712]{2,1,0:T(8,128)(2,1)}, u32[]{:S(2)}, u32[]{:S(2)}) async-start(bf16[8,64,3712]{2,1,0:T(8,128)(2,1)} %bitcast.129), calls=%async_computation | async-start | bytes 7602176 | tf_op jit(solution)/shard_map/all_to_all | solution.py:345
  120.7 32.2 %collective-permute-start.3 = (bf16[2,448,512]{2,1,0:T(8,128)(2,1)}, bf16[2,448,512]{2,1,0:T(8,128)(2,1)}, u32[]{:S(2)}, u32[]{:S(2)}) collective-permute-start(bf16[2,448,512]{2,1,0:T(8,128)(2,1)} %get-tuple-element.56), channel_id=1, source_target_pairs={{0,8},{8,0},{16,24},{24,16},{32,40},{40,32},{48,56},{56,48},{64,72... | collective-permute-start | bytes 2752520 | tf_op jit(solution)/shard_map/ppermute | solution.py:329
  125.6 29.3 %collective-permute-start.2 = (bf16[2,448,512]{2,1,0:T(8,128)(2,1)}, bf16[2,448,512]{2,1,0:T(8,128)(2,1)}, u32[]{:S(2)}, u32[]{:S(2)}) collective-permute-start(bf16[2,448,512]{2,1,0:T(8,128)(2,1)} %get-tuple-element.54), channel_id=1, source_target_pairs={{0,8},{8,0},{16,24},{24,16},{32,40},{40,32},{48,56},{56,48},{64,72... | collective-permute-start | bytes 2752520 | tf_op jit(solution)/shard_map/ppermute | solution.py:329
  130.9 24.5 %collective-permute-start.14 = (bf16[2,448,512]{2,1,0:T(8,128)(2,1)}, bf16[2,448,512]{2,1,0:T(8,128)(2,1)}, u32[]{:S(2)}, u32[]{:S(2)}) collective-permute-start(bf16[2,448,512]{2,1,0:T(8,128)(2,1)} %get-tuple-element.64), channel_id=1, source_target_pairs={{0,8},{8,0},{16,24},{24,16},{32,40},{40,32},{48,56},{56,48},{64,72... | collective-permute-start | bytes 2752520 | tf_op jit(solution)/shard_map/ppermute | solution.py:329
  135.9 21.5 %collective-permute-start.25 = (bf16[2,448,512]{2,1,0:T(8,128)(2,1)}, bf16[2,448,512]{2,1,0:T(8,128)(2,1)}, u32[]{:S(2)}, u32[]{:S(2)}) collective-permute-start(bf16[2,448,512]{2,1,0:T(8,128)(2,1)} %get-tuple-element.72), channel_id=1, source_target_pairs={{0,8},{8,0},{16,24},{24,16},{32,40},{40,32},{48,56},{56,48},{64,72... | collective-permute-start | bytes 2752520 | tf_op jit(solution)/shard_map/ppermute | solution.py:329
  140.6 22.8 %collective-permute-start.1 = (bf16[2,448,512]{2,1,0:T(8,128)(2,1)S(1)}, bf16[2,448,512]{2,1,0:T(8,128)(2,1)S(1)}, u32[]{:S(2)}, u32[]{:S(2)}) collective-permute-start(bf16[2,448,512]{2,1,0:T(8,128)(2,1)S(1)} %get-tuple-element.52), channel_id=1, source_target_pairs={{0,8},{8,0},{16,24},{24,16},{32,40},{40,32},{48,56},{56,48},{64,72... | collective-permute-start | bytes 2752520 | tf_op jit(solution)/shard_map/ppermute | solution.py:329
  152.9 31.7 %collective-permute-start.13 = (bf16[2,448,512]{2,1,0:T(8,128)(2,1)S(1)}, bf16[2,448,512]{2,1,0:T(8,128)(2,1)S(1)}, u32[]{:S(2)}, u32[]{:S(2)}) collective-permute-start(bf16[2,448,512]{2,1,0:T(8,128)(2,1)S(1)} %get-tuple-element.62), channel_id=1, source_target_pairs={{0,8},{8,0},{16,24},{24,16},{32,40},{40,32},{48,56},{56,48},{64,72... | collective-permute-start | bytes 2752520 | tf_op jit(solution)/shard_map/ppermute | solution.py:329
  154.9 29.7 %collective-permute-start.24 = (bf16[2,448,512]{2,1,0:T(8,128)(2,1)S(1)}, bf16[2,448,512]{2,1,0:T(8,128)(2,1)S(1)}, u32[]{:S(2)}, u32[]{:S(2)}) collective-permute-start(bf16[2,448,512]{2,1,0:T(8,128)(2,1)S(1)} %get-tuple-element.70), channel_id=1, source_target_pairs={{0,8},{8,0},{16,24},{24,16},{32,40},{40,32},{48,56},{56,48},{64,72... | collective-permute-start | bytes 2752520 | tf_op jit(solution)/shard_map/ppermute | solution.py:329
  163.4 21.7 %collective-permute-start.15 = (bf16[448,512]{1,0:T(8,128)(2,1)S(1)}, bf16[448,512]{1,0:T(8,128)(2,1)S(1)}, u32[]{:S(2)}, u32[]{:S(2)}) collective-permute-start(bf16[448,512]{1,0:T(8,128)(2,1)S(1)} %get-tuple-element.92), channel_id=1, source_target_pairs={{0,32},{8,40},{16,48},{24,56},{32,64},{40,72},{48,80},{56,88},{64,... | collective-permute-start | bytes 1376264 | tf_op jit(solution)/shard_map/ppermute | solution.py:335
  172.9 17.1 %collective-permute-start.26 = (bf16[448,512]{1,0:T(8,128)(2,1)S(1)}, bf16[448,512]{1,0:T(8,128)(2,1)S(1)}, u32[]{:S(2)}, u32[]{:S(2)}) collective-permute-start(bf16[448,512]{1,0:T(8,128)(2,1)S(1)} %get-tuple-element.84), channel_id=1, source_target_pairs={{0,32},{8,40},{16,48},{24,56},{32,64},{40,72},{48,80},{56,88},{64,... | collective-permute-start | bytes 1376264 | tf_op jit(solution)/shard_map/ppermute | solution.py:335
  184.6 41.7 %collective-permute-start = (bf16[2,448,512]{2,1,0:T(8,128)(2,1)}, bf16[2,448,512]{2,1,0:T(8,128)(2,1)}, u32[]{:S(2)}, u32[]{:S(2)}) collective-permute-start(bf16[2,448,512]{2,1,0:T(8,128)(2,1)} %get-tuple-element.50), channel_id=1, source_target_pairs={{0,8},{8,0},{16,24},{24,16},{32,40},{40,32},{48,56},{56,48},{64,72... | collective-permute-start | bytes 2752520 | tf_op jit(solution)/shard_map/ppermute | solution.py:329
  184.6 41.7 %collective-permute-start.12 = (bf16[2,448,512]{2,1,0:T(8,128)(2,1)}, bf16[2,448,512]{2,1,0:T(8,128)(2,1)}, u32[]{:S(2)}, u32[]{:S(2)}) collective-permute-start(bf16[2,448,512]{2,1,0:T(8,128)(2,1)} %get-tuple-element.60), channel_id=1, source_target_pairs={{0,8},{8,0},{16,24},{24,16},{32,40},{40,32},{48,56},{56,48},{64,72... | collective-permute-start | bytes 2752520 | tf_op jit(solution)/shard_map/ppermute | solution.py:329
  185.1 44.5 %collective-permute-start.23 = (bf16[2,448,512]{2,1,0:T(8,128)(2,1)}, bf16[2,448,512]{2,1,0:T(8,128)(2,1)}, u32[]{:S(2)}, u32[]{:S(2)}) collective-permute-start(bf16[2,448,512]{2,1,0:T(8,128)(2,1)} %get-tuple-element.68), channel_id=1, source_target_pairs={{0,8},{8,0},{16,24},{24,16},{32,40},{40,32},{48,56},{56,48},{64,72... | collective-permute-start | bytes 2752520 | tf_op jit(solution)/shard_map/ppermute | solution.py:329
  185.2 23.3 %collective-permute-start.29 = (bf16[448,512]{1,0:T(8,128)(2,1)}, bf16[448,512]{1,0:T(8,128)(2,1)}, u32[]{:S(2)}, u32[]{:S(2)}) collective-permute-start(bf16[448,512]{1,0:T(8,128)(2,1)} %get-tuple-element.85), channel_id=1, source_target_pairs={{0,96},{8,104},{16,112},{24,120},{32,0},{40,8},{48,16},{56,24},{64... | collective-permute-start | bytes 1376264 | tf_op jit(solution)/shard_map/ppermute | solution.py:336
  190.0 23.5 %collective-permute-start.5 = (bf16[448,512]{1,0:T(8,128)(2,1)}, bf16[448,512]{1,0:T(8,128)(2,1)}, u32[]{:S(2)}, u32[]{:S(2)}) collective-permute-start(bf16[448,512]{1,0:T(8,128)(2,1)} %get-tuple-element.98), channel_id=1, source_target_pairs={{0,32},{8,40},{16,48},{24,56},{32,64},{40,72},{48,80},{56,88},{64,... | collective-permute-start | bytes 1376264 | tf_op jit(solution)/shard_map/ppermute | solution.py:335
  203.8 86.8 %all-to-all-start.2 = ((bf16[8,64,3712]{2,1,0:T(8,128)(2,1)}), bf16[8,64,3712]{2,1,0:T(8,128)(2,1)}, u32[]{:S(2)}, u32[]{:S(2)}) async-start(bf16[8,64,3712]{2,1,0:T(8,128)(2,1)} %bitcast.130), calls=%async_computation.2 | async-start | bytes 7602176 | tf_op jit(solution)/shard_map/all_to_all | solution.py:345
  213.5 19.3 %collective-permute-start.16 = (bf16[448,512]{1,0:T(8,128)(2,1)S(1)}, bf16[448,512]{1,0:T(8,128)(2,1)S(1)}, u32[]{:S(2)}, u32[]{:S(2)}) collective-permute-start(bf16[448,512]{1,0:T(8,128)(2,1)S(1)} %get-tuple-element.90), channel_id=1, source_target_pairs={{0,32},{8,40},{16,48},{24,56},{32,64},{40,72},{48,80},{56,88},{64,... | collective-permute-start | bytes 1376264 | tf_op jit(solution)/shard_map/ppermute | solution.py:335
  226.4 19.3 %collective-permute-start.30 = (bf16[448,512]{1,0:T(8,128)(2,1)S(1)}, bf16[448,512]{1,0:T(8,128)(2,1)S(1)}, u32[]{:S(2)}, u32[]{:S(2)}) collective-permute-start(bf16[448,512]{1,0:T(8,128)(2,1)S(1)} %get-tuple-element.83), channel_id=1, source_target_pairs={{0,96},{8,104},{16,112},{24,120},{32,0},{40,8},{48,16},{56,24},{64... | collective-permute-start | bytes 1376264 | tf_op jit(solution)/shard_map/ppermute | solution.py:336
  229.6 20.8 %collective-permute-start.6 = (bf16[448,512]{1,0:T(8,128)(2,1)S(1)}, bf16[448,512]{1,0:T(8,128)(2,1)S(1)}, u32[]{:S(2)}, u32[]{:S(2)}) collective-permute-start(bf16[448,512]{1,0:T(8,128)(2,1)S(1)} %get-tuple-element.96), channel_id=1, source_target_pairs={{0,32},{8,40},{16,48},{24,56},{32,64},{40,72},{48,80},{56,88},{64,... | collective-permute-start | bytes 1376264 | tf_op jit(solution)/shard_map/ppermute | solution.py:335
  232.8 24.3 %collective-permute-start.11 = (bf16[2,448,512]{2,1,0:T(8,128)(2,1)S(1)}, bf16[2,448,512]{2,1,0:T(8,128)(2,1)S(1)}, u32[]{:S(2)}, u32[]{:S(2)}) collective-permute-start(bf16[2,448,512]{2,1,0:T(8,128)(2,1)S(1)} %get-tuple-element.58), channel_id=1, source_target_pairs={{0,8},{8,0},{16,24},{24,16},{32,40},{40,32},{48,56},{56,48},{64,72... | collective-permute-start | bytes 2752520 | tf_op jit(solution)/shard_map/ppermute | solution.py:329
  236.2 19.3 %collective-permute-start.9 = (bf16[448,512]{1,0:T(8,128)(2,1)S(1)}, bf16[448,512]{1,0:T(8,128)(2,1)S(1)}, u32[]{:S(2)}, u32[]{:S(2)}) collective-permute-start(bf16[448,512]{1,0:T(8,128)(2,1)S(1)} %get-tuple-element.97), channel_id=1, source_target_pairs={{0,96},{8,104},{16,112},{24,120},{32,0},{40,8},{48,16},{56,24},{64... | collective-permute-start | bytes 1376264 | tf_op jit(solution)/shard_map/ppermute | solution.py:336
  241.3 27.4 %collective-permute-start.22 = (bf16[2,448,512]{2,1,0:T(8,128)(2,1)S(1)}, bf16[2,448,512]{2,1,0:T(8,128)(2,1)S(1)}, u32[]{:S(2)}, u32[]{:S(2)}) collective-permute-start(bf16[2,448,512]{2,1,0:T(8,128)(2,1)S(1)} %get-tuple-element.66), channel_id=1, source_target_pairs={{0,8},{8,0},{16,24},{24,16},{32,40},{40,32},{48,56},{56,48},{64,72... | collective-permute-start | bytes 2752520 | tf_op jit(solution)/shard_map/ppermute | solution.py:329
  265.8 18.9 %collective-permute-start.21 = (bf16[224,1024]{1,0:T(8,128)(2,1)S(1)}, bf16[224,1024]{1,0:T(8,128)(2,1)S(1)}, u32[]{:S(2)}, u32[]{:S(2)}) collective-permute-start(bf16[224,1024]{1,0:T(8,128)(2,1)S(1)} %select_bitcast_fusion.1), channel_id=1, source_target_pairs={{0,16},{8,24},{16,0},{24,8},{32,48},{40,56},{48,32},{56,40},{64,80... | collective-permute-start | bytes 1376264 | tf_op jit(solution)/shard_map/ppermute | solution.py:339
  (49 other events, 427.3 us)

commit v2 on v1

--- a/solution.py
+++ b/solution.py
@@ -2,6 +2,7 @@
 
 import jax
 import jax.numpy as jnp
+import numpy as np
 from jax import lax
 from jax.experimental import pallas as pl
 from jax.experimental.pallas import tpu as pltpu
@@ -29,7 +30,7 @@
 MB = 1 << 20
 
 
-def params(limit=48):
+def params(limit=60):
     return pltpu.CompilerParams(vmem_limit_bytes=limit * MB)
 
 
@@ -147,7 +148,8 @@
     )(x, gate, up)
 
 
-def backward_kernel(g_ref, down_ref, hidden_ref, active_ref, slope_ref, gg_ref, gu_ref, wg_ref, total):
+def backward_kernel(g_ref, down_ref, hidden_ref, active_ref, slope_ref, *refs):
+    both_ref, wg_ref, total = refs[-3:]
     step = pl.program_id(0)
     back = jnp.dot(g_ref[:, :D], down_ref[...], preferred_element_type=F32)
     part = jnp.sum(back * hidden_ref[...].astype(F32), axis=1, keepdims=True)
@@ -158,12 +160,12 @@
 
     total[...] += jnp.broadcast_to(part, total.shape)
     scaled = g_ref[:, D : D + 1].astype(F32) * back
-    gg_ref[...] = (scaled * slope_ref[...]).astype(BF)
-    gu_ref[...] = (scaled * active_ref[...]).astype(BF)
+    both_ref[0] = (scaled * slope_ref[...]).astype(BF)
+    both_ref[1] = (scaled * active_ref[...]).astype(BF)
     wg_ref[...] = total[...].astype(BF)
 
 
-def backward(g, down, hidden, active, slope):
+def backward(g, down, hidden, active, slope, after=()):
     n = 256
     tile = pl.BlockSpec((ROWS, n), lambda i: (0, i))
     return pl.pallas_call(
@@ -175,26 +177,30 @@
             tile,
             tile,
             tile,
-        ],
-        out_specs=[tile, tile, pl.BlockSpec((ROWS, EXTRA), lambda i: (0, 0))],
+        ]
+        + [pl.BlockSpec(memory_space=pl.ANY)] * len(after),
+        out_specs=[
+            pl.BlockSpec((2, ROWS, n), lambda i: (0, 0, i)),
+            pl.BlockSpec((ROWS, EXTRA), lambda i: (0, 0)),
+        ],
         out_shape=[
-            jax.ShapeDtypeStruct((ROWS, FF), BF),
-            jax.ShapeDtypeStruct((ROWS, FF), BF),
+            jax.ShapeDtypeStruct((2, ROWS, FF), BF),
             jax.ShapeDtypeStruct((ROWS, EXTRA), BF),
         ],
         scratch_shapes=[pltpu.VMEM((ROWS, EXTRA), F32)],
         compiler_params=params(),
         cost_estimate=cost(2 * ROWS * D * FF, 18 * MB),
-    )(g, down, hidden, active, slope)
-
-
-def rows_kernel(gg_ref, gu_ref, gate_ref, up_ref, wg_ref, out_ref):
+    )(g, down, hidden, active, slope, *after)
+
+
+def rows_kernel(both_ref, gate_ref, up_ref, wg_ref, *refs):
+    out_ref = refs[-1]
     step = pl.program_id(0)
 
     @pl.when(step < NT)
     def _():
-        grad = lax.dot_general(gg_ref[...], gate_ref[...], LAST, preferred_element_type=F32)
-        grad = grad + lax.dot_general(gu_ref[...], up_ref[...], LAST, preferred_element_type=F32)
+        grad = lax.dot_general(both_ref[0], gate_ref[...], LAST, preferred_element_type=F32)
+        grad = grad + lax.dot_general(both_ref[1], up_ref[...], LAST, preferred_element_type=F32)
         out_ref[...] = grad.astype(BF)
 
     @pl.when(step == NT)
@@ -202,60 +208,64 @@
         out_ref[:, :EXTRA] = wg_ref[...]
 
 
-def row_grads(gg, gu, gate, up, wg):
+def row_grads(both, gate, up, wg, after=()):
     clamp = lambda i: (jnp.minimum(i, NT - 1), 0)
     return pl.pallas_call(
         rows_kernel,
         grid=(NT + 1,),
         in_specs=[
-            pl.BlockSpec((ROWS, FF), lambda i: (0, 0)),
-            pl.BlockSpec((ROWS, FF), lambda i: (0, 0)),
+            pl.BlockSpec((2, ROWS, FF), lambda i: (0, 0, 0)),
             pl.BlockSpec((TILE, FF), clamp),
             pl.BlockSpec((TILE, FF), clamp),
             pl.BlockSpec((ROWS, EXTRA), lambda i: (0, 0)),
-        ],
+        ]
+        + [pl.BlockSpec(memory_space=pl.ANY)] * len(after),
         out_specs=pl.BlockSpec((ROWS, TILE), lambda i: (0, i)),
         out_shape=jax.ShapeDtypeStruct((ROWS, WIDE), BF),
         compiler_params=params(),
         cost_estimate=cost(4 * ROWS * D * FF, 21 * MB),
-    )(gg, gu, gate, up, wg)
-
-
-def partial_kernel(scaled, place_ref, x_ref, p_ref, h_ref, send_ref, keep_ref):
+    )(both, gate, up, wg, *after)
+
+
+def turned_kernel(scaled, deps, place_ref, x_ref, p_ref, *refs):
+    send_ref, keep_ref, turned = refs[deps:]
     x = x_ref[...]
     if scaled:
         x = (p_ref[:, 0:1].astype(F32) * x.astype(F32)).astype(BF)
-    part = lax.dot_general(x, h_ref[...], FIRST, preferred_element_type=F32).astype(BF)
-    odd = place_ref[2] == 1
+    turned[...] = x.T
+    core = place_ref[8]
     for j in range(2):
-        even_rows = part[2 * j * SUB : (2 * j + 1) * SUB]
-        odd_rows = part[(2 * j + 1) * SUB : (2 * j + 2) * SUB]
         rows = slice(j * SUB, (j + 1) * SUB)
-        send_ref[0, rows, :] = jnp.where(odd, even_rows, odd_rows)
-        keep_ref[0, rows, :] = jnp.where(odd, odd_rows, even_rows)
-
-
-def partial(place, x, p, h, scaled):
+        far = pl.multiple_of((2 * j + 1 - core) * SUB, SUB)
+        near = pl.multiple_of((2 * j + core) * SUB, SUB)
+        send_ref[0, rows, :] = turned[pl.ds(far, SUB), :]
+        keep_ref[0, rows, :] = turned[pl.ds(near, SUB), :]
+
+
+def turned(place, x, p, scaled, after=()):
     last = (p.shape[1] // EXTRA) - 1
-    return pl.pallas_call(
-        functools.partial(partial_kernel, scaled),
+    send, keep = pl.pallas_call(
+        functools.partial(turned_kernel, scaled, len(after)),
         grid_spec=pltpu.PrefetchScalarGridSpec(
             num_scalar_prefetch=1,
-            grid=(2,),
+            grid=(NZ,),
             in_specs=[
-                pl.BlockSpec((ROWS, ZB), lambda i, place: (0, place[i])),
+                pl.BlockSpec((ROWS, ZB), lambda i, place: (0, i)),
                 pl.BlockSpec((ROWS, EXTRA), lambda i, place: (0, last)),
-                pl.BlockSpec((ROWS, HALF), lambda i, place: (0, i)),
-            ],
-            out_specs=[pl.BlockSpec((1, 2 * SUB, HALF), lambda i, place: (i, 0, 0))] * 2,
+            ]
+            + [pl.BlockSpec(memory_space=pl.ANY)] * len(after),
+            out_specs=[pl.BlockSpec((1, 2 * SUB, ROWS), lambda i, place: (i, 0, 0))] * 2,
+            scratch_shapes=[pltpu.VMEM((ZB, ROWS), BF)],
         ),
-        out_shape=[jax.ShapeDtypeStruct((2, 2 * SUB, HALF), BF)] * 2,
-        compiler_params=params(),
-        cost_estimate=cost(2 * ROWS * ZB * FF, 5 * MB),
-    )(place, x, p, h)
-
-
-def combine_kernel(picks_ref, rows_ref, tokens_ref, weights_ref):
+        out_shape=[jax.ShapeDtypeStruct((NZ, 2 * SUB, ROWS), BF)] * 2,
+        compiler_params=params(),
+        cost_estimate=cost(ROWS * D, 8 * MB),
+    )(place, x, p, *after)
+    return keep, lax.ppermute(send, "dp", TO_CORE)
+
+
+def combine_kernel(picks_ref, rows_ref, *refs):
+    tokens_ref, weights_ref = refs[-2:]
     step = pl.program_id(0)
 
     @pl.when(step < NT)
@@ -277,14 +287,15 @@
         weights_ref[...] = jnp.where(lane == 0, found[0], found[1]).astype(BF)[:, :TOP]
 
 
-def combine(picks, rows):
+def combine(picks, rows, after=()):
     return pl.pallas_call(
         combine_kernel,
         grid=(NT + 1,),
         in_specs=[
             pl.BlockSpec((TOP, ROWS, TOK), lambda i: (0, 0, 0)),
             pl.BlockSpec((ROWS, TILE), lambda i: (0, i)),
-        ],
+        ]
+        + [pl.BlockSpec(memory_space=pl.ANY)] * len(after),
         out_specs=[
             pl.BlockSpec((TOK, TILE), lambda i: (0, jnp.minimum(i, NT - 1))),
             pl.BlockSpec((TOK, TOP), lambda i: (0, 0)),
@@ -295,7 +306,7 @@
         ],
         compiler_params=params(),
         cost_estimate=cost(2 * ROWS * TOK * D, 5 * MB),
-    )(picks, rows)
+    )(picks, rows, *after)
 
 
 def moves(f):
@@ -321,23 +332,80 @@
     return total.astype(BF)
 
 
-def summed(z, x, c, left, p, right, scaled):
-    up = down = None
-    for step in range(NZ):
-        place = jnp.stack([(z - 1 - step) % NZ, (z + 1 + step) % NZ, c]).astype(jnp.int32)
-        send, keep = partial(place, left, p, right, scaled)
-        other = lax.ppermute(send, "dp", TO_CORE)
-        if step == 0:
-            up, down = add(keep[0], other[0]), add(keep[1], other[1])
-        else:
-            up, down = add(keep[0], other[0], up), add(keep[1], other[1], down)
-        if step < NZ - 1:
-            up = lax.ppermute(up, "dp", TO_UP)
-            down = lax.ppermute(down, "dp", TO_DOWN)
-    full = jnp.concatenate([up.reshape(2, SUB, HALF), down.reshape(2, SUB, HALF)], axis=2)
-    mine = jnp.where(x == 0, full[0], full[1])
-    away = lax.ppermute(jnp.where(x == 0, full[1], full[0]), "dp", TO_X)
-    return add(mine, away)[None]
+def step_kernel(moved, last, place_ref, left_a, left_b, right_a, right_b, *refs):
+    way = pl.program_id(0) // 2
+    rights = [r[0] if len(r.shape) == 3 else r[...] for r in (right_a, right_b)]
+    total = jnp.dot(left_a[0], rights[0], preferred_element_type=F32)
+    total = total + jnp.dot(left_b[0], rights[1], preferred_element_type=F32)
+    if last:
+        mine_ref, away_ref, full = refs[-3:]
+        for k in range(2):
+
+            @pl.when(way == k)
+            def _():
+                full[...] = (total + refs[k][...].astype(F32)).astype(BF)
+
+        x = place_ref[9]
+        mine_ref[0] = full[pl.ds(pl.multiple_of(x * SUB, SUB), SUB), :]
+        away_ref[0] = full[pl.ds(pl.multiple_of((1 - x) * SUB, SUB), SUB), :]
+    else:
+        for k, out_ref in enumerate(refs[-2:]):
+
+            @pl.when(way == k)
+            def _():
+                out_ref[...] = (total + refs[k][...].astype(F32) if moved else total).astype(BF)
+
+
+def ring_step(place, step, lefts, rights, moved=(), after=()):
+    if rights[0].ndim == 3:
+        width = rights[0].shape[2]
+        n = width // 2
+        right = pl.BlockSpec((1, ROWS, n), lambda i, place: (i // 2, 0, i % 2))
+    else:
+        width = rights[0].shape[1] // 2
+        n = width // 2
+        right = pl.BlockSpec((ROWS, n), lambda i, place: (0, i))
+    left = pl.BlockSpec((1, 2 * SUB, ROWS), lambda i, place: (place[2 * step + i // 2], 0, 0))
+    up = pl.BlockSpec((2 * SUB, n), lambda i, place: (0, jnp.minimum(i, 1)))
+    down = pl.BlockSpec((2 * SUB, n), lambda i, place: (0, jnp.maximum(i - 2, 0)))
+    last = step == NZ - 1
+    if last:
+        out_specs = [pl.BlockSpec((1, SUB, n), lambda i, place: (i // 2, 0, i % 2))] * 2
+        out_shape = [jax.ShapeDtypeStruct((2, SUB, width), BF)] * 2
+        scratch = [pltpu.VMEM((2 * SUB, n), BF)]
+    else:
+        out_specs = [up, down]
+        out_shape = [jax.ShapeDtypeStruct((2 * SUB, width), BF)] * 2
+        scratch = []
+    first, second = pl.pallas_call(
+        functools.partial(step_kernel, len(moved) > 0, last),
+        grid_spec=pltpu.PrefetchScalarGridSpec(
+            num_scalar_prefetch=1,
+            grid=(4,),
+            in_specs=[left, left, right, right]
+            + [up, down][: len(moved)]
+            + [pl.BlockSpec(memory_space=pl.ANY)] * len(after),
+            out_specs=out_specs,
+            scratch_shapes=scratch,
+        ),
+        out_shape=out_shape,
+        compiler_params=params(),
+        cost_estimate=cost(1 if width == FF else 40_000_000_000, 1),
+    )(place, *lefts, *rights, *moved, *after)
+    if last:
+        return first, lax.ppermute(second, "dp", TO_X)
+    return lax.ppermute(first, "dp", TO_UP), lax.ppermute(second, "dp", TO_DOWN), first
+
+
+PLACES = np.array(
+    [
+        [v for s in range(NZ) for v in ((z - 1 - s) % NZ, (z + 1 + s) % NZ)] + [c, x]
+        for z in range(NZ)
+        for x in range(2)
+        for c in range(2)
+    ],
+    np.int32,
+)
 
 
 def exchange(rows):
@@ -349,20 +417,34 @@
 
 
 def local(tokens, grad_out, routes, probs, w_gate, w_up, w_down):
-    where = lax.axis_index("dp")
-    z, x, c = where // 4, (where // 2) % 2, where % 2
+    place = lax.dynamic_index_in_dim(jnp.asarray(PLACES), lax.axis_index("dp"), 0, keepdims=False)
     gate, up, down = w_gate[0], w_up[0], w_down[0]
     picks, send_tokens = place_tokens(routes, tokens)
     row_tokens = exchange(send_tokens)
     send_grads = place_grads(picks, probs, grad_out)
     row_grads_in = exchange(send_grads)
     hidden, active, slope = forward(row_tokens, gate, up)
-    gg, gu, wg = backward(row_grads_in, down, hidden, active, slope)
-    grad_down = summed(z, x, c, row_grads_in, row_grads_in, hidden, True)
-    grad_gate = summed(z, x, c, row_tokens, row_grads_in, gg, False)
-    grad_up = summed(z, x, c, row_tokens, row_grads_in, gu, False)
-    returned = exchange(row_grads(gg, gu, gate, up, wg))
-    grad_tokens, grad_weights = combine(picks, returned)
+    lefts = turned(place, row_tokens, row_tokens, False, after=(hidden,))
+    hiddens = (hidden, lax.ppermute(hidden, "dp", TO_CORE))
+    both, wg = backward(
+        row_grads_in, down, hidden, active, slope, after=(lefts[0], lefts[1], hiddens[1])
+    )
+    boths = (both, lax.ppermute(both, "dp", TO_CORE))
+    dlefts = turned(place, row_grads_in, row_grads_in, True, after=(both,))
+    *moved, done = ring_step(place, 0, lefts, boths, after=dlefts[:1])
+    *dmoved, done = ring_step(place, 0, dlefts, hiddens, after=(done,))
+    sent_rows = row_grads(both, gate, up, wg, after=(done,))
+    returned = exchange(sent_rows)
+    *moved, done = ring_step(place, 1, lefts, boths, moved, after=(sent_rows,))
+    *dmoved, done = ring_step(place, 1, dlefts, hiddens, dmoved, after=(done,))
+    *moved, done = ring_step(place, 2, lefts, boths, moved, after=(done,))
+    *dmoved, done = ring_step(place, 2, dlefts, hiddens, dmoved, after=(done,))
+    mine, away = ring_step(place, 3, lefts, boths, moved, after=(done,))
+    grad_tokens, grad_weights = combine(picks, returned, after=(mine,))
+    dmine, daway = ring_step(place, 3, dlefts, hiddens, dmoved, after=(grad_tokens,))
+    grad_gate = add(mine[0], away[0])[None]
+    grad_up = add(mine[1], away[1])[None]
+    grad_down = jnp.concatenate([add(dmine[0], daway[0]), add(dmine[1], daway[1])], axis=1)[None]
     return (grad_tokens, grad_weights, grad_gate, grad_up, grad_down)
 
 

time: 299 us -> 267 us (0.89)
  Pallas kernels: 88.9 us -> 121 us
  waiting for transfers between devices: 113 us -> 84.7 us
  other arithmetic: 21.3 us -> 2.22 us
  starting transfers between devices: 53.4 us -> 39.7 us
    pallas_call x13 -> x11, Pallas kernels: 55.6 us -> 77 us  [the longest x8 51.6 us: ring_step(): pl.pallas_call(functools.partial(step_kernel, len(moved) > 0, last), grid...]
    ppermute x33 -> x18, waiting for transfers between devices: 44.6 us -> 24.7 us  [the longest x6 17.2 us: ring_step(): lax.ppermute(first, 'dp', TO_UP)]
    convert_element_type x12 -> x2, other arithmetic: 18 us -> 1.39 us  [add(): return total.astype(BF)]
    ppermute x33 -> x18, starting transfers between devices: 38.7 us -> 24.9 us  [the longest x6 18.4 us: ring_step(): lax.ppermute(second, 'dp', TO_DOWN)]
    all_to_all x3, waiting for transfers between devices: 68.3 us -> 60 us  [exchange(): lax.all_to_all(rows.reshape(EXPERTS, CAP, width), 'expert', split_axis=0,...]
    unnamed x77 -> x43, local copies, waits for them, and re-layouts: 20.1 us -> 16.1 us
    pallas_call x1, Pallas kernels: 2.62 us -> 6.43 us  [place_tokens(): pl.pallas_call(place_kernel, grid=(NT,), in_specs=[pl.BlockSpec((TOK, TOP...]
    pallas_call x1, Pallas kernels: 2.9 us -> 6.65 us  [place_grads(): pl.pallas_call(grads_kernel, grid=(NT + 1,), in_specs=[pl.BlockSpec((TOP,...]
  transfers between devices with their start and end apart: 36 -> 21, of which waited for: 12 -> 6; matrix products, arithmetic and copies ran while one was open for 7% -> 1% of each run, Pallas kernels for 22% -> 39%
where the time goes in v2:
time: 267 us; the launch traced here: 266 us
  Pallas kernels  121 us (45%)
  waiting for transfers between devices  84.7 us (32%)
  starting transfers between devices  39.7 us (15%)
  local copies, waits for them, and re-layouts  17.3 us (6%)
    all_to_all x3, waiting for transfers between devices, exchange(): lax.all_to_all(rows.reshape(EXPERTS, CAP, width), 'expert', split_axis=0,...  60 us
    pallas_call x8, Pallas kernels, ring_step(): pl.pallas_call(functools.partial(step_kernel, len(moved) > 0, last), grid...  51.6 us
    ppermute x6, starting transfers between devices, ring_step(): lax.ppermute(second, 'dp', TO_DOWN)  18.4 us
    ppermute x6, waiting for transfers between devices, ring_step(): lax.ppermute(first, 'dp', TO_UP)  17.2 us
    unnamed x43, local copies, waits for them, and re-layouts  16.1 us
    all_to_all x3, starting transfers between devices, exchange(): lax.all_to_all(rows.reshape(EXPERTS, CAP, width), 'expert', split_axis=0,...  14.9 us
    pallas_call x1, Pallas kernels, row_grads(): pl.pallas_call(rows_kernel, grid=(NT + 1,), in_specs=[pl.BlockSpec((2, RO...  13.6 us
    pallas_call x1, Pallas kernels, forward(): pl.pallas_call(forward_kernel, grid=(FF // n,), in_specs=[pl.BlockSpec((R...  13.3 us
  transfers between devices with their start and end apart: 21, of which 6 were waited for; matrix products, arithmetic and copies ran while one was open for 1% of the time, Pallas kernels for 39%

profile of v2, /device:TPU:0, one launch (start us, length us, event | category | flops | bytes accessed | tf_op | source)
XLA Modules:
  0.0 265.7 jit_solution(4999371326149325090)
XLA Ops:
  2.0 6.4 %shard_map.119 = (bf16[2,512,128]{2,1,0:T(8,128)(2,1)}, bf16[512,3584]{1,0:T(8,128)(2,1)}) custom-call(s32[128,2]{1,0:T(8,128)} %copy.13.routes_ref, bf16[128,3584]{1,0:T(8,128)(2,1)} %tokens_ref.1), custom_call_target="tpu_custom_call" | custom-call | flops 469762048 | bytes 5242880 | tf_op jit(solution)/shard_map/pallas_call | solution.py:65
  8.5 5.6 %all-to-all-start.1 = ((bf16[8,64,3584]{2,1,0:T(8,128)(2,1)}), bf16[8,64,3584]{2,1,0:T(8,128)(2,1)}, u32[]{:S(2)}, u32[]{:S(2)}) async-start(bf16[8,64,3584]{2,1,0:T(8,128)(2,1)} %bitcast.20), calls=%async_computation.1 | async-start | bytes 7340032 | tf_op jit(solution)/shard_map/all_to_all | solution.py:413
  14.8 6.7 %shard_map.120 = bf16[512,3712]{1,0:T(8,128)(2,1)} custom-call(bf16[2,512,128]{2,1,0:T(8,128)(2,1)} %get-tuple-element.34.picks_ref, bf16[128,2]{1,0:T(8,128)(2,1)} %copy.14.probs_ref, bf16[128,3584]{1,0:T(8,128)(2,1)} %grads_ref.1), custom_call_target="tpu_custom_call" | custom-call | flops 469762048 | bytes 5242880 | tf_op jit(solution)/shard_map/pallas_call | solution.py:104
  21.5 36.5 %all-to-all-done.1 = bf16[8,64,3584]{2,1,0:T(8,128)(2,1)} async-done(((bf16[8,64,3584]{2,1,0:T(8,128)(2,1)}), bf16[8,64,3584]{2,1,0:T(8,128)(2,1)}, u32[]{:S(2)}, u32[]{:S(2)}) %all-to-all-start.1) | async-done | bytes 3670048 | tf_op jit(solution)/shard_map/all_to_all | solution.py:413
  58.0 4.5 %all-to-all-start = ((bf16[8,64,3712]{2,1,0:T(8,128)(2,1)}), bf16[8,64,3712]{2,1,0:T(8,128)(2,1)}, u32[]{:S(2)}, u32[]{:S(2)}) async-start(bf16[8,64,3712]{2,1,0:T(8,128)(2,1)} %bitcast.17), calls=%async_computation | async-start | bytes 7602176 | tf_op jit(solution)/shard_map/all_to_all | solution.py:413
  63.8 13.3 %shard_map.121 = (bf16[512,1024]{1,0:T(8,128)(2,1)}, f32[512,1024]{1,0:T(8,128)}, f32[512,1024]{1,0:T(8,128)}) custom-call(bf16[512,3584]{1,0:T(8,128)(2,1)} %bitcast.4.x_ref.p_ref, bf16[3584,1024]{1,0:T(8,128)(2,1)} %bitcast.21, bf16[3584,1024]{1,0:T(8,128)(2,1)} %bitcast.23), custom_call_target="tpu_custom_call" | custom-call | flops 7516192768 | bytes 24117248 | tf_op jit(solution)/shard_map/pallas_call | solution.py:132
  77.1 5.8 %shard_map.122 = (bf16[4,448,512]{2,1,0:T(8,128)(2,1)}, bf16[4,448,512]{2,1,0:T(8,128)(2,1)}) custom-call(s32[10]{0:T(128)} %dynamic-slice_bitcast_fusion.place_ref, bf16[512,3584]{1,0:T(8,128)(2,1)} %bitcast.4.x_ref.p_ref, bf16[512,3584]{1,0:T(8,128)(2,1)} %bitcast.4.x_ref.p_ref, bf16[512,1024]{1,0:T(8,128)(2,1)} %get-tuple-element.36.refs_0_.hidden_ref.right_a), custom_call_target="tpu_custom_call" | custom-call | flops 1835008 | bytes 8388608 | tf_op jit(solution)/shard_map/pallas_call | solution.py:247
  83.5 23.4 %all-to-all-done = bf16[8,64,3712]{2,1,0:T(8,128)(2,1)} async-done(((bf16[8,64,3712]{2,1,0:T(8,128)(2,1)}), bf16[8,64,3712]{2,1,0:T(8,128)(2,1)}, u32[]{:S(2)}, u32[]{:S(2)}) %all-to-all-start) | async-done | bytes 3801120 | tf_op jit(solution)/shard_map/all_to_all | solution.py:413
  108.2 10.9 %shard_map.123 = (bf16[2,512,1024]{2,1,0:T(8,128)(2,1)}, bf16[512,128]{1,0:T(8,128)(2,1)}) custom-call(bf16[512,3712]{1,0:T(8,128)(2,1)} %bitcast.1.g_ref.x_ref.p_ref, bf16[3584,1024]{1,0:T(8,128)(2,1)} %bitcast.19, bf16[512,1024]{1,0:T(8,128)(2,1)} %get-tuple-element.36.refs_0_.hidden_ref.right_a, f32[512,1024]{1,0:T(8,128)} %get-tuple-element.37.active_ref, ...), custom_call_target="tpu_custom_call" | custom-call | flops 3758096384 | bytes 18874368 | tf_op jit(solution)/shard_map/pallas_call | solution.py:171
  119.0 6.0 %shard_map.124 = (bf16[4,448,512]{2,1,0:T(8,128)(2,1)}, bf16[4,448,512]{2,1,0:T(8,128)(2,1)}) custom-call(s32[10]{0:T(128)} %dynamic-slice_bitcast_fusion.place_ref, bf16[512,3712]{1,0:T(8,128)(2,1)} %bitcast.1.g_ref.x_ref.p_ref, bf16[512,3712]{1,0:T(8,128)(2,1)} %bitcast.1.g_ref.x_ref.p_ref, bf16[2,512,1024]{2,1,0:T(8,128)(2,1)} %get-tuple-element.41.refs_0_.right_a.both_ref), custom_call_target="tpu_custom_call" | custom-call | flops 1835008 | bytes 8388608 | tf_op jit(solution)/shard_map/pallas_call | solution.py:247
  126.8 6.9 %shard_map.125 = (bf16[448,1024]{1,0:T(8,128)(2,1)}, bf16[448,1024]{1,0:T(8,128)(2,1)}) custom-call(s32[10]{0:T(128)} %dynamic-slice_bitcast_fusion.place_ref, bf16[4,448,512]{2,1,0:T(8,128)(2,1)} %get-tuple-element.39.refs_0_.left_a, bf16[4,448,512]{2,1,0:T(8,128)(2,1)} %copy-done, bf16[2,512,1024]{2,1,0:T(8,128)(2,1)} %get-tuple-element.41.refs_0_.right_a.both_ref, ...), custom_call_target="tpu_custom_call" | custom-call | flops 1 | bytes 1 | tf_op jit(solution)/shard_map/pallas_call | solution.py:380
  139.1 5.5 %shard_map.126 = (bf16[448,512]{1,0:T(8,128)(2,1)}, bf16[448,512]{1,0:T(8,128)(2,1)}) custom-call(s32[10]{0:T(128)} %dynamic-slice_bitcast_fusion.place_ref, bf16[4,448,512]{2,1,0:T(8,128)(2,1)} %get-tuple-element.43.refs_0_.left_a, bf16[4,448,512]{2,1,0:T(8,128)(2,1)} %copy-done.13, bf16[512,1024]{1,0:T(8,128)(2,1)} %get-tuple-element.36.refs_0_.hidden_ref.right_a, ...), custom_call_target="tpu_custom_call" | custom-call | flops 40000000000 | bytes 1 | tf_op jit(solution)/shard_map/pallas_call | solution.py:380
  147.9 13.6 %shard_map.127.refs_2_ = bf16[512,3712]{1,0:T(8,128)(2,1)} custom-call(bf16[2,512,1024]{2,1,0:T(8,128)(2,1)} %get-tuple-element.41.refs_0_.right_a.both_ref, bf16[3584,1024]{1,0:T(8,128)(2,1)} %bitcast.22, bf16[3584,1024]{1,0:T(8,128)(2,1)} %bitcast.24, bf16[512,128]{1,0:T(8,128)(2,1)} %get-tuple-element.42.wg_ref, bf16[448,512]{1,0:T(8,128)(2,1)} %get-tuple-element.46.refs_0_), custom_call_target="tpu_custom_call" | custom-call | flops 7516192768 | bytes 22020096 | tf_op jit(solution)/shard_map/pallas_call | solution.py:213
  163.4 7.2 %shard_map.128 = (bf16[448,1024]{1,0:T(8,128)(2,1)}, bf16[448,1024]{1,0:T(8,128)(2,1)}) custom-call(s32[10]{0:T(128)} %dynamic-slice_bitcast_fusion.place_ref, bf16[4,448,512]{2,1,0:T(8,128)(2,1)} %get-tuple-element.39.refs_0_.left_a, bf16[4,448,512]{2,1,0:T(8,128)(2,1)} %copy-done, bf16[2,512,1024]{2,1,0:T(8,128)(2,1)} %get-tuple-element.41.refs_0_.right_a.both_ref, ...), custom_call_target="tpu_custom_call" | custom-call | flops 1 | bytes 1 | tf_op jit(solution)/shard_map/pallas_call | solution.py:380
  175.4 5.7 %shard_map.129 = (bf16[448,512]{1,0:T(8,128)(2,1)}, bf16[448,512]{1,0:T(8,128)(2,1)}) custom-call(s32[10]{0:T(128)} %dynamic-slice_bitcast_fusion.place_ref, bf16[4,448,512]{2,1,0:T(8,128)(2,1)} %get-tuple-element.43.refs_0_.left_a, bf16[4,448,512]{2,1,0:T(8,128)(2,1)} %copy-done.13, bf16[512,1024]{1,0:T(8,128)(2,1)} %get-tuple-element.36.refs_0_.hidden_ref.right_a, ...), custom_call_target="tpu_custom_call" | custom-call | flops 40000000000 | bytes 1 | tf_op jit(solution)/shard_map/pallas_call | solution.py:380
  184.3 4.7 %all-to-all-start.2 = ((bf16[8,64,3712]{2,1,0:T(8,128)(2,1)}), bf16[8,64,3712]{2,1,0:T(8,128)(2,1)}, u32[]{:S(2)}, u32[]{:S(2)}) async-start(bf16[8,64,3712]{2,1,0:T(8,128)(2,1)} %bitcast.18), calls=%async_computation.2 | async-start | bytes 7602176 | tf_op jit(solution)/shard_map/all_to_all | solution.py:413
  189.0 6.3 %collective-permute-done.6.refs_0_ = bf16[448,1024]{1,0:T(8,128)(2,1)S(1)} collective-permute-done((bf16[448,1024]{1,0:T(8,128)(2,1)}, bf16[448,1024]{1,0:T(8,128)(2,1)S(1)}, u32[]{:S(2)}, u32[]{:S(2)}) %collective-permute-start.6) | collective-permute-done | bytes 917536 | tf_op jit(solution)/shard_map/ppermute | solution.py:397
  197.2 7.4 %shard_map.130 = (bf16[448,1024]{1,0:T(8,128)(2,1)}, bf16[448,1024]{1,0:T(8,128)(2,1)}) custom-call(s32[10]{0:T(128)} %dynamic-slice_bitcast_fusion.place_ref, bf16[4,448,512]{2,1,0:T(8,128)(2,1)} %get-tuple-element.39.refs_0_.left_a, bf16[4,448,512]{2,1,0:T(8,128)(2,1)} %copy-done, bf16[2,512,1024]{2,1,0:T(8,128)(2,1)} %get-tuple-element.41.refs_0_.right_a.both_ref, ...), custom_call_target="tpu_custom_call" | custom-call | flops 1 | bytes 1 | tf_op jit(solution)/shard_map/pallas_call | solution.py:380
  209.3 5.8 %shard_map.131 = (bf16[448,512]{1,0:T(8,128)(2,1)}, bf16[448,512]{1,0:T(8,128)(2,1)}) custom-call(s32[10]{0:T(128)} %dynamic-slice_bitcast_fusion.place_ref, bf16[4,448,512]{2,1,0:T(8,128)(2,1)} %get-tuple-element.43.refs_0_.left_a, bf16[4,448,512]{2,1,0:T(8,128)(2,1)} %copy-done.13, bf16[512,1024]{1,0:T(8,128)(2,1)} %get-tuple-element.36.refs_0_.hidden_ref.right_a, ...), custom_call_target="tpu_custom_call" | custom-call | flops 40000000000 | bytes 1 | tf_op jit(solution)/shard_map/pallas_call | solution.py:380
  218.4 10.9 %collective-permute-done.10.refs_0_ = bf16[448,1024]{1,0:T(8,128)(2,1)S(1)} collective-permute-done((bf16[448,1024]{1,0:T(8,128)(2,1)}, bf16[448,1024]{1,0:T(8,128)(2,1)S(1)}, u32[]{:S(2)}, u32[]{:S(2)}) %collective-permute-start.10) | collective-permute-done | bytes 917536 | tf_op jit(solution)/shard_map/ppermute | solution.py:397
  231.1 7.2 %shard_map.132 = (bf16[2,224,1024]{2,1,0:T(8,128)(2,1)}, bf16[2,224,1024]{2,1,0:T(8,128)(2,1)}) custom-call(s32[10]{0:T(128)} %dynamic-slice_bitcast_fusion.place_ref, bf16[4,448,512]{2,1,0:T(8,128)(2,1)} %get-tuple-element.39.refs_0_.left_a, bf16[4,448,512]{2,1,0:T(8,128)(2,1)} %copy-done, bf16[2,512,1024]{2,1,0:T(8,128)(2,1)} %get-tuple-element.41.refs_0_.right_a.both_ref, ...), custom_call_target="tpu_custom_call" | custom-call | flops 1 | bytes 1 | tf_op jit(solution)/shard_map/pallas_call | solution.py:380
  241.1 6.7 %shard_map.133 = (bf16[128,3584]{1,0:T(8,128)(2,1)}, bf16[128,2]{1,0:T(8,128)(2,1)}) custom-call(bf16[2,512,128]{2,1,0:T(8,128)(2,1)} %get-tuple-element.34.picks_ref, bf16[512,3712]{1,0:T(8,128)(2,1)} %bitcast.9.rows_ref, bf16[2,224,1024]{2,1,0:T(8,128)(2,1)} %get-tuple-element.56.refs_0_), custom_call_target="tpu_custom_call" | custom-call | flops 469762048 | bytes 5242880 | tf_op jit(solution)/shard_map/pallas_call | solution.py:291
  248.7 5.8 %shard_map.134 = (bf16[2,224,512]{2,1,0:T(8,128)(2,1)}, bf16[2,224,512]{2,1,0:T(8,128)(2,1)}) custom-call(s32[10]{0:T(128)} %dynamic-slice_bitcast_fusion.place_ref, bf16[4,448,512]{2,1,0:T(8,128)(2,1)} %get-tuple-element.43.refs_0_.left_a, bf16[4,448,512]{2,1,0:T(8,128)(2,1)} %copy-done.13, bf16[512,1024]{1,0:T(8,128)(2,1)} %get-tuple-element.36.refs_0_.hidden_ref.right_a, ...), custom_call_target="tpu_custom_call" | custom-call | flops 40000000000 | bytes 1 | tf_op jit(solution)/shard_map/pallas_call | solution.py:380
  258.6 6.1 %collective-permute-done.17 = bf16[2,224,512]{2,1,0:T(8,128)(2,1)S(1)} collective-permute-done((bf16[2,224,512]{2,1,0:T(8,128)(2,1)}, bf16[2,224,512]{2,1,0:T(8,128)(2,1)S(1)}, u32[]{:S(2)}, u32[]{:S(2)}) %collective-permute-start.17) | collective-permute-done | bytes 458784 | tf_op jit(solution)/shard_map/ppermute | solution.py:396
  (81 shorter events, 45.8 us)
Async XLA Ops:
  8.5 49.6 %all-to-all-start.1 = ((bf16[8,64,3584]{2,1,0:T(8,128)(2,1)}), bf16[8,64,3584]{2,1,0:T(8,128)(2,1)}, u32[]{:S(2)}, u32[]{:S(2)}) async-start(bf16[8,64,3584]{2,1,0:T(8,128)(2,1)} %bitcast.20), calls=%async_computation.1 | async-start | bytes 7340032 | tf_op jit(solution)/shard_map/all_to_all | solution.py:413
  58.0 48.9 %all-to-all-start = ((bf16[8,64,3712]{2,1,0:T(8,128)(2,1)}), bf16[8,64,3712]{2,1,0:T(8,128)(2,1)}, u32[]{:S(2)}, u32[]{:S(2)}) async-start(bf16[8,64,3712]{2,1,0:T(8,128)(2,1)} %bitcast.17), calls=%async_computation | async-start | bytes 7602176 | tf_op jit(solution)/shard_map/all_to_all | solution.py:413
  83.0 24.0 %collective-permute-start = (bf16[4,448,512]{2,1,0:T(8,128)(2,1)}, bf16[4,448,512]{2,1,0:T(8,128)(2,1)S(1)}, u32[]{:S(2)}, u32[]{:S(2)}) collective-permute-start(bf16[4,448,512]{2,1,0:T(8,128)(2,1)} %get-tuple-element.40), channel_id=1, source_target_pairs={{0,8},{8,0},{16,24},{24,16},{32,40},{40,32},{48,56},{56,48},{64,72... | collective-permute-start | bytes 5505032 | tf_op jit(solution)/shard_map/ppermute | solution.py:264
  83.0 24.0 %collective-permute-start.1 = (bf16[512,1024]{1,0:T(8,128)(2,1)S(1)}, bf16[512,1024]{1,0:T(8,128)(2,1)}, u32[]{:S(2)}, u32[]{:S(2)}) collective-permute-start(bf16[512,1024]{1,0:T(8,128)(2,1)S(1)} %copy-done.2), channel_id=1, source_target_pairs={{0,8},{8,0},{16,24},{24,16},{32,40},{40,32},{48,56},{56,48},{64,72... | collective-permute-start | bytes 3145736 | tf_op jit(solution)/shard_map/ppermute | solution.py:428
  119.0 6.5 %collective-permute-start.3 = (bf16[2,512,1024]{2,1,0:T(8,128)(2,1)}, bf16[2,512,1024]{2,1,0:T(8,128)(2,1)S(1)}, u32[]{:S(2)}, u32[]{:S(2)}) collective-permute-start(bf16[2,512,1024]{2,1,0:T(8,128)(2,1)} %get-tuple-element.41.refs_0_.right_a.both_ref), channel_id=1, source_target_pairs={{0,8},{8,0},{16,24},{24,16},{32,40},{40,32},{48,56},{56,48},{64,72... | collective-permute-start | bytes 6291464 | tf_op jit(solution)/shard_map/ppermute | solution.py:432
  125.0 12.9 %collective-permute-start.2 = (bf16[4,448,512]{2,1,0:T(8,128)(2,1)}, bf16[4,448,512]{2,1,0:T(8,128)(2,1)S(1)}, u32[]{:S(2)}, u32[]{:S(2)}) collective-permute-start(bf16[4,448,512]{2,1,0:T(8,128)(2,1)} %get-tuple-element.44), channel_id=1, source_target_pairs={{0,8},{8,0},{16,24},{24,16},{32,40},{40,32},{48,56},{56,48},{64,72... | collective-permute-start | bytes 5505032 | tf_op jit(solution)/shard_map/ppermute | solution.py:264
  133.8 27.7 %collective-permute-start.4 = (bf16[448,1024]{1,0:T(8,128)(2,1)}, bf16[448,1024]{1,0:T(8,128)(2,1)S(1)}, u32[]{:S(2)}, u32[]{:S(2)}) collective-permute-start(bf16[448,1024]{1,0:T(8,128)(2,1)} %get-tuple-element.45.refs_0_), channel_id=1, source_target_pairs={{0,32},{8,40},{16,48},{24,56},{32,64},{40,72},{48,80},{56,88},{64,... | collective-permute-start | bytes 2752520 | tf_op jit(solution)/shard_map/ppermute | solution.py:397
  135.6 25.8 %collective-permute-start.5 = (bf16[448,1024]{1,0:T(8,128)(2,1)}, bf16[448,1024]{1,0:T(8,128)(2,1)S(1)}, u32[]{:S(2)}, u32[]{:S(2)}) collective-permute-start(bf16[448,1024]{1,0:T(8,128)(2,1)} %get-tuple-element.47), channel_id=1, source_target_pairs={{0,96},{8,104},{16,112},{24,120},{32,0},{40,8},{48,16},{56,24},{64... | collective-permute-start | bytes 2752520 | tf_op jit(solution)/shard_map/ppermute | solution.py:397
  144.7 29.2 %collective-permute-start.8 = (bf16[448,512]{1,0:T(8,128)(2,1)}, bf16[448,512]{1,0:T(8,128)(2,1)S(1)}, u32[]{:S(2)}, u32[]{:S(2)}) collective-permute-start(bf16[448,512]{1,0:T(8,128)(2,1)} %get-tuple-element.46.refs_0_), channel_id=1, source_target_pairs={{0,32},{8,40},{16,48},{24,56},{32,64},{40,72},{48,80},{56,88},{64,... | collective-permute-start | bytes 1376264 | tf_op jit(solution)/shard_map/ppermute | solution.py:397
  144.7 29.2 %collective-permute-start.9 = (bf16[448,512]{1,0:T(8,128)(2,1)}, bf16[448,512]{1,0:T(8,128)(2,1)S(1)}, u32[]{:S(2)}, u32[]{:S(2)}) collective-permute-start(bf16[448,512]{1,0:T(8,128)(2,1)} %get-tuple-element.50), channel_id=1, source_target_pairs={{0,96},{8,104},{16,112},{24,120},{32,0},{40,8},{48,16},{56,24},{64... | collective-permute-start | bytes 1376264 | tf_op jit(solution)/shard_map/ppermute | solution.py:397
  170.6 24.7 %collective-permute-start.6 = (bf16[448,1024]{1,0:T(8,128)(2,1)}, bf16[448,1024]{1,0:T(8,128)(2,1)S(1)}, u32[]{:S(2)}, u32[]{:S(2)}) collective-permute-start(bf16[448,1024]{1,0:T(8,128)(2,1)} %get-tuple-element.48.refs_2_), channel_id=1, source_target_pairs={{0,32},{8,40},{16,48},{24,56},{32,64},{40,72},{48,80},{56,88},{64,... | collective-permute-start | bytes 2752520 | tf_op jit(solution)/shard_map/ppermute | solution.py:397
  170.6 24.7 %collective-permute-start.7 = (bf16[448,1024]{1,0:T(8,128)(2,1)}, bf16[448,1024]{1,0:T(8,128)(2,1)S(1)}, u32[]{:S(2)}, u32[]{:S(2)}) collective-permute-start(bf16[448,1024]{1,0:T(8,128)(2,1)} %get-tuple-element.49), channel_id=1, source_target_pairs={{0,96},{8,104},{16,112},{24,120},{32,0},{40,8},{48,16},{56,24},{64... | collective-permute-start | bytes 2752520 | tf_op jit(solution)/shard_map/ppermute | solution.py:397
  181.0 26.8 %collective-permute-start.12 = (bf16[448,512]{1,0:T(8,128)(2,1)}, bf16[448,512]{1,0:T(8,128)(2,1)S(1)}, u32[]{:S(2)}, u32[]{:S(2)}) collective-permute-start(bf16[448,512]{1,0:T(8,128)(2,1)} %get-tuple-element.51.refs_2_), channel_id=1, source_target_pairs={{0,32},{8,40},{16,48},{24,56},{32,64},{40,72},{48,80},{56,88},{64,... | collective-permute-start | bytes 1376264 | tf_op jit(solution)/shard_map/ppermute | solution.py:397
  181.0 26.8 %collective-permute-start.13 = (bf16[448,512]{1,0:T(8,128)(2,1)}, bf16[448,512]{1,0:T(8,128)(2,1)S(1)}, u32[]{:S(2)}, u32[]{:S(2)}) collective-permute-start(bf16[448,512]{1,0:T(8,128)(2,1)} %get-tuple-element.54), channel_id=1, source_target_pairs={{0,96},{8,104},{16,112},{24,120},{32,0},{40,8},{48,16},{56,24},{64... | collective-permute-start | bytes 1376264 | tf_op jit(solution)/shard_map/ppermute | solution.py:397
  184.3 56.8 %all-to-all-start.2 = ((bf16[8,64,3712]{2,1,0:T(8,128)(2,1)}), bf16[8,64,3712]{2,1,0:T(8,128)(2,1)}, u32[]{:S(2)}, u32[]{:S(2)}) async-start(bf16[8,64,3712]{2,1,0:T(8,128)(2,1)} %bitcast.18), calls=%async_computation.2 | async-start | bytes 7602176 | tf_op jit(solution)/shard_map/all_to_all | solution.py:413
  204.6 24.7 %collective-permute-start.10 = (bf16[448,1024]{1,0:T(8,128)(2,1)}, bf16[448,1024]{1,0:T(8,128)(2,1)S(1)}, u32[]{:S(2)}, u32[]{:S(2)}) collective-permute-start(bf16[448,1024]{1,0:T(8,128)(2,1)} %get-tuple-element.52.refs_2_), channel_id=1, source_target_pairs={{0,32},{8,40},{16,48},{24,56},{32,64},{40,72},{48,80},{56,88},{64,... | collective-permute-start | bytes 2752520 | tf_op jit(solution)/shard_map/ppermute | solution.py:397
  204.6 24.7 %collective-permute-start.11 = (bf16[448,1024]{1,0:T(8,128)(2,1)}, bf16[448,1024]{1,0:T(8,128)(2,1)S(1)}, u32[]{:S(2)}, u32[]{:S(2)}) collective-permute-start(bf16[448,1024]{1,0:T(8,128)(2,1)} %get-tuple-element.53), channel_id=1, source_target_pairs={{0,96},{8,104},{16,112},{24,120},{32,0},{40,8},{48,16},{56,24},{64... | collective-permute-start | bytes 2752520 | tf_op jit(solution)/shard_map/ppermute | solution.py:397
  215.2 32.6 %collective-permute-start.15 = (bf16[448,512]{1,0:T(8,128)(2,1)}, bf16[448,512]{1,0:T(8,128)(2,1)S(1)}, u32[]{:S(2)}, u32[]{:S(2)}) collective-permute-start(bf16[448,512]{1,0:T(8,128)(2,1)} %get-tuple-element.55.refs_2_), channel_id=1, source_target_pairs={{0,32},{8,40},{16,48},{24,56},{32,64},{40,72},{48,80},{56,88},{64,... | collective-permute-start | bytes 1376264 | tf_op jit(solution)/shard_map/ppermute | solution.py:397
  215.2 32.6 %collective-permute-start.16 = (bf16[448,512]{1,0:T(8,128)(2,1)}, bf16[448,512]{1,0:T(8,128)(2,1)S(1)}, u32[]{:S(2)}, u32[]{:S(2)}) collective-permute-start(bf16[448,512]{1,0:T(8,128)(2,1)} %get-tuple-element.60), channel_id=1, source_target_pairs={{0,96},{8,104},{16,112},{24,120},{32,0},{40,8},{48,16},{56,24},{64... | collective-permute-start | bytes 1376264 | tf_op jit(solution)/shard_map/ppermute | solution.py:397
  238.3 19.0 %collective-permute-start.14 = (bf16[2,224,1024]{2,1,0:T(8,128)(2,1)}, bf16[2,224,1024]{2,1,0:T(8,128)(2,1)S(1)}, u32[]{:S(2)}, u32[]{:S(2)}) collective-permute-start(bf16[2,224,1024]{2,1,0:T(8,128)(2,1)} %get-tuple-element.59), channel_id=1, source_target_pairs={{0,16},{8,24},{16,0},{24,8},{32,48},{40,56},{48,32},{56,40},{64,80... | collective-permute-start | bytes 2752520 | tf_op jit(solution)/shard_map/ppermute | solution.py:396
  248.7 6.7 %copy-start.11 = (bf16[128,2]{1,0:T(8,128)(2,1)S(1)}, bf16[128,2]{1,0:T(8,128)(2,1)}, u32[]{:S(2)}) copy-start(bf16[128,2]{1,0:T(8,128)(2,1)} %get-tuple-element.64) | copy-start | bytes 1540
  248.7 8.7 %copy-start.3 = (bf16[2,224,1024]{2,1,0:T(8,128)(2,1)S(1)}, bf16[2,224,1024]{2,1,0:T(8,128)(2,1)}, u32[]{:S(2)}) copy-start(bf16[2,224,1024]{2,1,0:T(8,128)(2,1)} %get-tuple-element.56.refs_0_) | copy-start | bytes 2752516
  254.5 10.3 %copy-start.10 = (bf16[2,224,512]{2,1,0:T(8,128)(2,1)S(1)}, bf16[2,224,512]{2,1,0:T(8,128)(2,1)}, u32[]{:S(2)}) copy-start(bf16[2,224,512]{2,1,0:T(8,128)(2,1)} %get-tuple-element.61) | copy-start | bytes 1376260
  254.5 10.3 %collective-permute-start.17 = (bf16[2,224,512]{2,1,0:T(8,128)(2,1)}, bf16[2,224,512]{2,1,0:T(8,128)(2,1)S(1)}, u32[]{:S(2)}, u32[]{:S(2)}) collective-permute-start(bf16[2,224,512]{2,1,0:T(8,128)(2,1)} %get-tuple-element.62), channel_id=1, source_target_pairs={{0,16},{8,24},{16,0},{24,8},{32,48},{40,56},{48,32},{56,40},{64,80... | collective-permute-start | bytes 1376264 | tf_op jit(solution)/shard_map/ppermute | solution.py:396
  (17 other events, 25.6 us)

commit v3 on v2

--- a/solution.py
+++ b/solution.py
@@ -17,7 +17,7 @@
 TOK = 128
 EXTRA = 128
 WIDE = D + EXTRA
-TILE = 512
+TILE = 1792
 NT = D // TILE
 NZ = 4
 ZB = D // NZ
@@ -166,7 +166,7 @@
 
 
 def backward(g, down, hidden, active, slope, after=()):
-    n = 256
+    n = 512
     tile = pl.BlockSpec((ROWS, n), lambda i: (0, i))
     return pl.pallas_call(
         backward_kernel,
@@ -332,74 +332,77 @@
     return total.astype(BF)
 
 
-def step_kernel(moved, last, place_ref, left_a, left_b, right_a, right_b, *refs):
-    way = pl.program_id(0) // 2
-    rights = [r[0] if len(r.shape) == 3 else r[...] for r in (right_a, right_b)]
-    total = jnp.dot(left_a[0], rights[0], preferred_element_type=F32)
-    total = total + jnp.dot(left_b[0], rights[1], preferred_element_type=F32)
-    if last:
-        mine_ref, away_ref, full = refs[-3:]
-        for k in range(2):
-
-            @pl.when(way == k)
-            def _():
-                full[...] = (total + refs[k][...].astype(F32)).astype(BF)
-
-        x = place_ref[9]
-        mine_ref[0] = full[pl.ds(pl.multiple_of(x * SUB, SUB), SUB), :]
-        away_ref[0] = full[pl.ds(pl.multiple_of((1 - x) * SUB, SUB), SUB), :]
-    else:
-        for k, out_ref in enumerate(refs[-2:]):
-
-            @pl.when(way == k)
-            def _():
-                out_ref[...] = (total + refs[k][...].astype(F32) if moved else total).astype(BF)
-
-
-def ring_step(place, step, lefts, rights, moved=(), after=()):
-    if rights[0].ndim == 3:
-        width = rights[0].shape[2]
-        n = width // 2
-        right = pl.BlockSpec((1, ROWS, n), lambda i, place: (i // 2, 0, i % 2))
-    else:
-        width = rights[0].shape[1] // 2
-        n = width // 2
-        right = pl.BlockSpec((ROWS, n), lambda i, place: (0, i))
-    left = pl.BlockSpec((1, 2 * SUB, ROWS), lambda i, place: (place[2 * step + i // 2], 0, 0))
-    up = pl.BlockSpec((2 * SUB, n), lambda i, place: (0, jnp.minimum(i, 1)))
-    down = pl.BlockSpec((2 * SUB, n), lambda i, place: (0, jnp.maximum(i - 2, 0)))
-    last = step == NZ - 1
-    if last:
-        out_specs = [pl.BlockSpec((1, SUB, n), lambda i, place: (i // 2, 0, i % 2))] * 2
-        out_shape = [jax.ShapeDtypeStruct((2, SUB, width), BF)] * 2
-        scratch = [pltpu.VMEM((2 * SUB, n), BF)]
-    else:
-        out_specs = [up, down]
-        out_shape = [jax.ShapeDtypeStruct((2 * SUB, width), BF)] * 2
-        scratch = []
-    first, second = pl.pallas_call(
-        functools.partial(step_kernel, len(moved) > 0, last),
+def wide_kernel(place_ref, left_a, left_b, right_a, right_b, *refs):
+    total = jnp.dot(left_a[0], right_a[0], preferred_element_type=F32)
+    total = total + jnp.dot(left_b[0], right_b[0], preferred_element_type=F32)
+    for k, out_ref in enumerate(refs[-2:]):
+
+        @pl.when(pl.program_id(0) == k)
+        def _():
+            out_ref[...] = total.astype(BF)
+
+
+def wide_parts(place, step, lefts, rights, after=()):
+    left = pl.BlockSpec((1, 2 * SUB, ROWS), lambda i, place: (place[2 * step + i], 0, 0))
+    right = pl.BlockSpec((1, ROWS, FF), lambda i, place: (i, 0, 0))
+    return pl.pallas_call(
+        wide_kernel,
         grid_spec=pltpu.PrefetchScalarGridSpec(
             num_scalar_prefetch=1,
-            grid=(4,),
+            grid=(2,),
             in_specs=[left, left, right, right]
-            + [up, down][: len(moved)]
             + [pl.BlockSpec(memory_space=pl.ANY)] * len(after),
-            out_specs=out_specs,
-            scratch_shapes=scratch,
+            out_specs=[pl.BlockSpec((2 * SUB, FF), lambda i, place: (0, 0))] * 2,
         ),
-        out_shape=out_shape,
-        compiler_params=params(),
-        cost_estimate=cost(1 if width == FF else 40_000_000_000, 1),
-    )(place, *lefts, *rights, *moved, *after)
-    if last:
-        return first, lax.ppermute(second, "dp", TO_X)
-    return lax.ppermute(first, "dp", TO_UP), lax.ppermute(second, "dp", TO_DOWN), first
+        out_shape=[jax.ShapeDtypeStruct((2 * SUB, FF), BF)] * 2,
+        compiler_params=params(),
+        cost_estimate=cost(16 * SUB * ROWS * FF, 8 * MB),
+    )(place, *lefts, *rights, *after)
+
+
+def down_kernel(place_ref, left_a, left_b, right_a, right_b, *refs):
+    total = jnp.dot(left_a[0], right_a[...], preferred_element_type=F32)
+    total = total + jnp.dot(left_b[0], right_b[...], preferred_element_type=F32)
+    refs[-1][0] = total.astype(BF)
+
+
+def down_parts(place, entry, lefts, rights, after=()):
+    left = pl.BlockSpec((1, SUB, ROWS), lambda i, place: (i, place[entry], 0))
+    right = pl.BlockSpec((ROWS, FF), lambda i, place: (0, 0))
+    return pl.pallas_call(
+        down_kernel,
+        grid_spec=pltpu.PrefetchScalarGridSpec(
+            num_scalar_prefetch=1,
+            grid=(NZ,),
+            in_specs=[left, left, right, right]
+            + [pl.BlockSpec(memory_space=pl.ANY)] * len(after),
+            out_specs=pl.BlockSpec((1, SUB, FF), lambda i, place: (i, 0, 0)),
+        ),
+        out_shape=jax.ShapeDtypeStruct((NZ, SUB, FF), BF),
+        compiler_params=params(),
+        cost_estimate=cost(16 * SUB * ROWS * FF, 8 * MB),
+    )(place, *lefts, *rights, *after)
+
+
+def around(up, down):
+    return lax.ppermute(up, "dp", TO_UP), lax.ppermute(down, "dp", TO_DOWN)
+
+
+def at_x(x, rows):
+    return lax.dynamic_slice_in_dim(rows, x * SUB, SUB, 0)
+
+
+def down_add(place, step, parts, moved):
+    up = [lax.dynamic_index_in_dim(p, place[2 * step], 0, keepdims=False)[:, :HALF] for p in parts]
+    down = [
+        lax.dynamic_index_in_dim(p, place[2 * step + 1], 0, keepdims=False)[:, HALF:] for p in parts
+    ]
+    return add(*up, *moved[:1]), add(*down, *moved[1:])
 
 
 PLACES = np.array(
     [
-        [v for s in range(NZ) for v in ((z - 1 - s) % NZ, (z + 1 + s) % NZ)] + [c, x]
+        [v for s in range(NZ) for v in ((z - 1 - s) % NZ, (z + 1 + s) % NZ)] + [c, x, 1 - x]
         for z in range(NZ)
         for x in range(2)
         for c in range(2)
@@ -431,20 +434,34 @@
     )
     boths = (both, lax.ppermute(both, "dp", TO_CORE))
     dlefts = turned(place, row_grads_in, row_grads_in, True, after=(both,))
-    *moved, done = ring_step(place, 0, lefts, boths, after=dlefts[:1])
-    *dmoved, done = ring_step(place, 0, dlefts, hiddens, after=(done,))
-    sent_rows = row_grads(both, gate, up, wg, after=(done,))
+    x = place[9]
+    ring0 = wide_parts(place, 0, lefts, boths, after=dlefts[:1])
+    moved0 = around(*ring0)
+    far = down_parts(place, 10, dlefts, hiddens, after=ring0[:1])
+    far_in = lax.ppermute(far, "dp", TO_X)
+    parts1 = wide_parts(place, 1, lefts, boths, after=(far,))
+    near = down_parts(place, 9, dlefts, hiddens, after=parts1[:1])
+    ring1 = add(parts1[0], moved0[0]), add(parts1[1], moved0[1])
+    moved1 = around(*ring1)
+    sent_rows = row_grads(both, gate, up, wg, after=ring1 + (near,))
     returned = exchange(sent_rows)
-    *moved, done = ring_step(place, 1, lefts, boths, moved, after=(sent_rows,))
-    *dmoved, done = ring_step(place, 1, dlefts, hiddens, dmoved, after=(done,))
-    *moved, done = ring_step(place, 2, lefts, boths, moved, after=(done,))
-    *dmoved, done = ring_step(place, 2, dlefts, hiddens, dmoved, after=(done,))
-    mine, away = ring_step(place, 3, lefts, boths, moved, after=(done,))
-    grad_tokens, grad_weights = combine(picks, returned, after=(mine,))
-    dmine, daway = ring_step(place, 3, dlefts, hiddens, dmoved, after=(grad_tokens,))
-    grad_gate = add(mine[0], away[0])[None]
-    grad_up = add(mine[1], away[1])[None]
-    grad_down = jnp.concatenate([add(dmine[0], daway[0]), add(dmine[1], daway[1])], axis=1)[None]
+    parts2 = wide_parts(place, 2, lefts, boths, after=(sent_rows,))
+    down_pair = (near, far_in)
+    down_moved0 = around(*down_add(place, 0, down_pair, ()))
+    ring2 = add(parts2[0], moved1[0]), add(parts2[1], moved1[1])
+    moved2 = around(*ring2)
+    parts3 = wide_parts(place, 3, lefts, boths, after=ring2)
+    down_moved1 = around(*down_add(place, 1, down_pair, down_moved0))
+    down_moved2 = around(*down_add(place, 2, down_pair, down_moved1))
+    down_grad = jnp.concatenate(down_add(place, 3, down_pair, down_moved2), axis=1)
+    mine = [add(at_x(x, a), at_x(x, b)) for a, b in zip(parts3, moved2)]
+    away = jnp.stack([add(at_x(1 - x, a), at_x(1 - x, b)) for a, b in zip(parts3, moved2)])
+    came = lax.ppermute(away, "dp", TO_X)
+    grad_tokens, grad_weights = combine(picks, returned, after=(away,))
+    mine, grad_tokens = lax.optimization_barrier((mine, grad_tokens))
+    grad_gate = add(mine[0], came[0])[None]
+    grad_up = add(mine[1], came[1])[None]
+    grad_down = down_grad[None]
     return (grad_tokens, grad_weights, grad_gate, grad_up, grad_down)
 
 

time: 267 us -> 271 us (1.015)
  Pallas kernels: 121 us -> 98.1 us
  between operations: 0.75 us -> 16.7 us
  other arithmetic: 2.22 us -> 15.8 us
    pallas_call x8 -> x6, Pallas kernels: 51.6 us -> 37.9 us  [the longest x4 24.8 us: wide_parts(): pl.pallas_call(wide_kernel, grid_spec=pltpu.PrefetchScalarGridSpec(num_sc...]
    unnamed x43 -> x55, local copies, waits for them, and re-layouts: 16.1 us -> 7.52 us
    convert_element_type x2 -> x12, other arithmetic: 1.39 us -> 9.33 us  [add(): return total.astype(BF)]
    squeeze x1 -> x2, local copies, waits for them, and re-layouts: 1.21 us -> 5.45 us  [down_add(): lax.dynamic_index_in_dim(p, place[2 * step], 0, keepdims=False)[:, :HALF]]
    another operation x0 -> x3, other arithmetic: none -> 3.23 us  [local(): jnp.stack([add(at_x(1 - x, a), at_x(1 - x, b)) for a, b in zip(parts3, mo...]
  transfers between devices with their start and end apart: 21 -> 21, of which waited for: 6 -> 6; matrix products, arithmetic and copies ran while one was open for 1% -> 8% of each run, Pallas kernels for 39% -> 31%
where the time goes in v3:
time: 271 us; the launch traced here: 269 us
  Pallas kernels  98.1 us (36%)
  waiting for transfers between devices  85 us (31%)
  starting transfers between devices  38.8 us (14%)
  between operations  16.7 us (6%)
  other arithmetic  15.8 us (6%)
  local copies, waits for them, and re-layouts  14.8 us (5%)
    all_to_all x3, waiting for transfers between devices, exchange(): lax.all_to_all(rows.reshape(EXPERTS, CAP, width), 'expert', split_axis=0,...  62.6 us
    pallas_call x4, Pallas kernels, wide_parts(): pl.pallas_call(wide_kernel, grid_spec=pltpu.PrefetchScalarGridSpec(num_sc...  24.8 us
    ppermute x12, starting transfers between devices, around(): return (lax.ppermute(up, 'dp', TO_UP), lax.ppermute(down, 'dp', TO_DOWN))  19.5 us
    ppermute x12, waiting for transfers between devices, around(): return (lax.ppermute(up, 'dp', TO_UP), lax.ppermute(down, 'dp', TO_DOWN))  19 us
    all_to_all x3, starting transfers between devices, exchange(): lax.all_to_all(rows.reshape(EXPERTS, CAP, width), 'expert', split_axis=0,...  14.7 us
    pallas_call x1, Pallas kernels, forward(): pl.pallas_call(forward_kernel, grid=(FF // n,), in_specs=[pl.BlockSpec((R...  13.3 us
    pallas_call x1, Pallas kernels, row_grads(): pl.pallas_call(rows_kernel, grid=(NT + 1,), in_specs=[pl.BlockSpec((2, RO...  13.1 us
    pallas_call x2, Pallas kernels, down_parts(): pl.pallas_call(down_kernel, grid_spec=pltpu.PrefetchScalarGridSpec(num_sc...  13 us
  transfers between devices with their start and end apart: 21, of which 6 were waited for; matrix products, arithmetic and copies ran while one was open for 8% of the time, Pallas kernels for 31%

profile of v3, /device:TPU:0, one launch (start us, length us, event | category | flops | bytes accessed | tf_op | source)
XLA Modules:
  0.0 269.2 jit_solution(11402124986387181294)
XLA Ops:
  2.0 3.9 %shard_map.119 = (bf16[2,512,128]{2,1,0:T(8,128)(2,1)}, bf16[512,3584]{1,0:T(8,128)(2,1)}) custom-call(s32[128,2]{1,0:T(8,128)} %copy.13.routes_ref, bf16[128,3584]{1,0:T(8,128)(2,1)} %tokens_ref.1), custom_call_target="tpu_custom_call" | custom-call | flops 469762048 | bytes 5242880 | tf_op jit(solution)/shard_map/pallas_call | solution.py:65
  6.0 5.6 %all-to-all-start = ((bf16[8,64,3584]{2,1,0:T(8,128)(2,1)}), bf16[8,64,3584]{2,1,0:T(8,128)(2,1)}, u32[]{:S(2)}, u32[]{:S(2)}) async-start(bf16[8,64,3584]{2,1,0:T(8,128)(2,1)} %bitcast.76), calls=%async_computation | async-start | bytes 7340032 | tf_op jit(solution)/shard_map/all_to_all | solution.py:416
  12.3 4.0 %shard_map.122 = bf16[512,3712]{1,0:T(8,128)(2,1)} custom-call(bf16[2,512,128]{2,1,0:T(8,128)(2,1)} %get-tuple-element.33.picks_ref, bf16[128,2]{1,0:T(8,128)(2,1)} %copy.14.probs_ref, bf16[128,3584]{1,0:T(8,128)(2,1)} %grads_ref.1), custom_call_target="tpu_custom_call" | custom-call | flops 469762048 | bytes 5242880 | tf_op jit(solution)/shard_map/pallas_call | solution.py:104
  16.3 39.2 %all-to-all-done = bf16[8,64,3584]{2,1,0:T(8,128)(2,1)} async-done(((bf16[8,64,3584]{2,1,0:T(8,128)(2,1)}), bf16[8,64,3584]{2,1,0:T(8,128)(2,1)}, u32[]{:S(2)}, u32[]{:S(2)}) %all-to-all-start) | async-done | bytes 3670048 | tf_op jit(solution)/shard_map/all_to_all | solution.py:416
  55.5 4.5 %all-to-all-start.1 = ((bf16[8,64,3712]{2,1,0:T(8,128)(2,1)}), bf16[8,64,3712]{2,1,0:T(8,128)(2,1)}, u32[]{:S(2)}, u32[]{:S(2)}) async-start(bf16[8,64,3712]{2,1,0:T(8,128)(2,1)} %bitcast.74), calls=%async_computation.1 | async-start | bytes 7602176 | tf_op jit(solution)/shard_map/all_to_all | solution.py:416
  61.2 13.3 %shard_map.120 = (bf16[512,1024]{1,0:T(8,128)(2,1)}, f32[512,1024]{1,0:T(8,128)}, f32[512,1024]{1,0:T(8,128)}) custom-call(bf16[512,3584]{1,0:T(8,128)(2,1)} %bitcast.2.x_ref.p_ref, bf16[3584,1024]{1,0:T(8,128)(2,1)} %bitcast.77, bf16[3584,1024]{1,0:T(8,128)(2,1)} %bitcast.79), custom_call_target="tpu_custom_call" | custom-call | flops 7516192768 | bytes 24117248 | tf_op jit(solution)/shard_map/pallas_call | solution.py:132
  74.6 5.8 %shard_map.121 = (bf16[4,448,512]{2,1,0:T(8,128)(2,1)}, bf16[4,448,512]{2,1,0:T(8,128)(2,1)}) custom-call(s32[11]{0:T(128)} %get-tuple-element.81.place_ref, bf16[512,3584]{1,0:T(8,128)(2,1)} %bitcast.2.x_ref.p_ref, bf16[512,3584]{1,0:T(8,128)(2,1)} %bitcast.2.x_ref.p_ref, bf16[512,1024]{1,0:T(8,128)(2,1)} %get-tuple-element.30.refs_0_.hidden_ref.right_a), custom_call_target="tpu_custom_call" | custom-call | flops 1835008 | bytes 8388608 | tf_op jit(solution)/shard_map/pallas_call | solution.py:247
  80.9 23.4 %all-to-all-done.1 = bf16[8,64,3712]{2,1,0:T(8,128)(2,1)} async-done(((bf16[8,64,3712]{2,1,0:T(8,128)(2,1)}), bf16[8,64,3712]{2,1,0:T(8,128)(2,1)}, u32[]{:S(2)}, u32[]{:S(2)}) %all-to-all-start.1) | async-done | bytes 3801120 | tf_op jit(solution)/shard_map/all_to_all | solution.py:416
  105.6 9.9 %shard_map.123 = (bf16[2,512,1024]{2,1,0:T(8,128)(2,1)}, bf16[512,128]{1,0:T(8,128)(2,1)}) custom-call(bf16[512,3712]{1,0:T(8,128)(2,1)} %bitcast.6.g_ref.x_ref.p_ref, bf16[3584,1024]{1,0:T(8,128)(2,1)} %bitcast.75, bf16[512,1024]{1,0:T(8,128)(2,1)} %get-tuple-element.30.refs_0_.hidden_ref.right_a, f32[512,1024]{1,0:T(8,128)} %get-tuple-element.34.active_ref, ...), custom_call_target="tpu_custom_call" | custom-call | flops 3758096384 | bytes 18874368 | tf_op jit(solution)/shard_map/pallas_call | solution.py:171
  115.6 5.9 %shard_map.124 = (bf16[4,448,512]{2,1,0:T(8,128)(2,1)}, bf16[4,448,512]{2,1,0:T(8,128)(2,1)}) custom-call(s32[11]{0:T(128)} %get-tuple-element.81.place_ref, bf16[512,3712]{1,0:T(8,128)(2,1)} %bitcast.6.g_ref.x_ref.p_ref, bf16[512,3712]{1,0:T(8,128)(2,1)} %bitcast.6.g_ref.x_ref.p_ref, bf16[2,512,1024]{2,1,0:T(8,128)(2,1)} %get-tuple-element.36.refs_0_.right_a.both_ref), custom_call_target="tpu_custom_call" | custom-call | flops 1835008 | bytes 8388608 | tf_op jit(solution)/shard_map/pallas_call | solution.py:247
  123.4 6.2 %shard_map.125 = (bf16[448,1024]{1,0:T(8,128)(2,1)}, bf16[448,1024]{1,0:T(8,128)(2,1)}) custom-call(s32[11]{0:T(128)} %get-tuple-element.81.place_ref, bf16[4,448,512]{2,1,0:T(8,128)(2,1)} %get-tuple-element.31.refs_0_.left_a, bf16[4,448,512]{2,1,0:T(8,128)(2,1)} %copy-done, bf16[2,512,1024]{2,1,0:T(8,128)(2,1)} %get-tuple-element.36.refs_0_.right_a.both_ref, ...), custom_call_target="tpu_custom_call" | custom-call | flops 1879048192 | bytes 8388608 | tf_op jit(solution)/shard_map/pallas_call | solution.py:348
  151.3 6.5 %shard_map.126.refs_0_ = bf16[4,224,1024]{2,1,0:T(8,128)(2,1)} custom-call(s32[11]{0:T(128)} %get-tuple-element.81.place_ref, bf16[4,448,512]{2,1,0:T(8,128)(2,1)} %get-tuple-element.38.refs_0_.left_a, bf16[4,448,512]{2,1,0:T(8,128)(2,1)} %copy-done.3, bf16[512,1024]{1,0:T(8,128)(2,1)} %get-tuple-element.30.refs_0_.hidden_ref.right_a, ...), custom_call_target="tpu_custom_call" | custom-call | flops 1879048192 | bytes 8388608 | tf_op jit(solution)/shard_map/pallas_call | solution.py:372
  160.6 6.2 %shard_map.127 = (bf16[448,1024]{1,0:T(8,128)(2,1)}, bf16[448,1024]{1,0:T(8,128)(2,1)}) custom-call(s32[11]{0:T(128)} %get-tuple-element.81.place_ref, bf16[4,448,512]{2,1,0:T(8,128)(2,1)} %get-tuple-element.31.refs_0_.left_a, bf16[4,448,512]{2,1,0:T(8,128)(2,1)} %copy-done, bf16[2,512,1024]{2,1,0:T(8,128)(2,1)} %get-tuple-element.36.refs_0_.right_a.both_ref, ...), custom_call_target="tpu_custom_call" | custom-call | flops 1879048192 | bytes 8388608 | tf_op jit(solution)/shard_map/pallas_call | solution.py:348
  166.8 6.5 %shard_map.128.refs_2_ = bf16[4,224,1024]{2,1,0:T(8,128)(2,1)} custom-call(s32[11]{0:T(128)} %get-tuple-element.81.place_ref, bf16[4,448,512]{2,1,0:T(8,128)(2,1)} %get-tuple-element.38.refs_0_.left_a, bf16[4,448,512]{2,1,0:T(8,128)(2,1)} %copy-done.3, bf16[512,1024]{1,0:T(8,128)(2,1)} %get-tuple-element.30.refs_0_.hidden_ref.right_a, ...), custom_call_target="tpu_custom_call" | custom-call | flops 1879048192 | bytes 8388608 | tf_op jit(solution)/shard_map/pallas_call | solution.py:372
  173.3 3.8 %dynamic-slice_bitcast_fusion.15 = (bf16[224,1024]{1,0:T(8,128)(2,1)}, bf16[224,1024]{1,0:T(8,128)(2,1)}, bf16[224,1024]{1,0:T(8,128)(2,1)}, bf16[224,1024]{1,0:...) fusion(bf16[4,224,1024]{2,1,0:T(8,128)(2,1)} %shard_map.128.ref, ...), kind=kLoop, calls=%fused_computation.43 | loop fusion | bytes 7340064 | tf_op jit(solution)/shard_map/jit(dynamic_index_in_dim)/squeeze | solution.py:396
  184.1 13.1 %shard_map.129.refs_0_ = bf16[512,3712]{1,0:T(8,128)(2,1)} custom-call(bf16[2,512,1024]{2,1,0:T(8,128)(2,1)} %get-tuple-element.36.refs_0_.right_a.both_ref, bf16[3584,1024]{1,0:T(8,128)(2,1)} %bitcast.78, bf16[3584,1024]{1,0:T(8,128)(2,1)} %bitcast.80, bf16[512,128]{1,0:T(8,128)(2,1)} %get-tuple-element.37.wg_ref, ...), custom_call_target="tpu_custom_call" | custom-call | flops 7516192768 | bytes 22020096 | tf_op jit(solution)/shard_map/pallas_call | solution.py:213
  197.2 4.5 %all-to-all-start.2 = ((bf16[8,64,3712]{2,1,0:T(8,128)(2,1)}), bf16[8,64,3712]{2,1,0:T(8,128)(2,1)}, u32[]{:S(2)}, u32[]{:S(2)}) async-start(bf16[8,64,3712]{2,1,0:T(8,128)(2,1)} %bitcast.73), calls=%async_computation.2 | async-start | bytes 7602176 | tf_op jit(solution)/shard_map/all_to_all | solution.py:416
  201.7 6.3 %shard_map.130 = (bf16[448,1024]{1,0:T(8,128)(2,1)}, bf16[448,1024]{1,0:T(8,128)(2,1)}) custom-call(s32[11]{0:T(128)} %get-tuple-element.81.place_ref, bf16[4,448,512]{2,1,0:T(8,128)(2,1)} %get-tuple-element.31.refs_0_.left_a, bf16[4,448,512]{2,1,0:T(8,128)(2,1)} %copy-done, bf16[2,512,1024]{2,1,0:T(8,128)(2,1)} %get-tuple-element.36.refs_0_.right_a.both_ref, ...), custom_call_target="tpu_custom_call" | custom-call | flops 1879048192 | bytes 8388608 | tf_op jit(solution)/shard_map/pallas_call | solution.py:348
  219.8 6.2 %shard_map.131 = (bf16[448,1024]{1,0:T(8,128)(2,1)}, bf16[448,1024]{1,0:T(8,128)(2,1)}) custom-call(s32[11]{0:T(128)} %get-tuple-element.81.place_ref, bf16[4,448,512]{2,1,0:T(8,128)(2,1)} %get-tuple-element.31.refs_0_.left_a, bf16[4,448,512]{2,1,0:T(8,128)(2,1)} %copy-done, bf16[2,512,1024]{2,1,0:T(8,128)(2,1)} %get-tuple-element.36.refs_0_.right_a.both_ref, ...), custom_call_target="tpu_custom_call" | custom-call | flops 1879048192 | bytes 8388608 | tf_op jit(solution)/shard_map/pallas_call | solution.py:348
  226.1 11.9 %collective-permute-done.15 = bf16[224,512]{1,0:T(8,128)(2,1)S(1)} collective-permute-done((bf16[224,512]{1,0:T(8,128)(2,1)}, bf16[224,512]{1,0:T(8,128)(2,1)S(1)}, u32[]{:S(2)}, u32[]{:S(2)}) %collective-permute-start.15) | collective-permute-done | bytes 229408 | tf_op jit(solution)/shard_map/ppermute | solution.py:388
  238.1 3.7 %collective-permute-start.16 = (bf16[224,512]{1,0:T(8,128)(2,1)S(1)}, bf16[224,512]{1,0:T(8,128)(2,1)S(1)}, u32[]{:S(2)}, u32[]{:S(2)}) collective-permute-start(bf16[224,512]{1,0:T(8,128)(2,1)S(1)} %add_convert_fusion.10), channel_id=1, source_target_pairs={{0,96},{8,104},{16,112},{24,120},{32,0},{40,8},{48,16},{56,24},{64... | collective-permute-start | bytes 688136 | tf_op jit(solution)/shard_map/ppermute | solution.py:388
  253.2 3.8 %collective-permute-done.14 = bf16[224,512]{1,0:T(8,128)(2,1)S(1)} collective-permute-done((bf16[224,512]{1,0:T(8,128)(2,1)S(1)}, bf16[224,512]{1,0:T(8,128)(2,1)S(1)}, u32[]{:S(2)}, u32[]{:S(2)}) %collective-permute-start.14) | collective-permute-done | bytes 229408 | tf_op jit(solution)/shard_map/ppermute | solution.py:388
  257.9 4.1 %shard_map.132 = (bf16[128,3584]{1,0:T(8,128)(2,1)}, bf16[128,2]{1,0:T(8,128)(2,1)}) custom-call(bf16[2,512,128]{2,1,0:T(8,128)(2,1)} %get-tuple-element.33.picks_ref, bf16[512,3712]{1,0:T(8,128)(2,1)} %bitcast.10.rows_ref, bf16[2,224,1024]{2,1,0:T(8,128)(2,1)} %copy-done.7), custom_call_target="tpu_custom_call" | custom-call | flops 469762048 | bytes 5242880 | tf_op jit(solution)/shard_map/pallas_call | solution.py:291
  263.4 3.4 %collective-permute-done.10 = bf16[2,224,1024]{2,1,0:T(8,128)(2,1)} collective-permute-done((bf16[2,224,1024]{2,1,0:T(8,128)(2,1)S(1)}, bf16[2,224,1024]{2,1,0:T(8,128)(2,1)}, u32[]{:S(2)}, u32[]{:S(2)}) %collective-permute-start.10) | collective-permute-done | bytes 917536 | tf_op jit(solution)/shard_map/ppermute | solution.py:459
  (108 shorter events, 50.6 us)
Async XLA Ops:
  6.0 49.5 %all-to-all-start = ((bf16[8,64,3584]{2,1,0:T(8,128)(2,1)}), bf16[8,64,3584]{2,1,0:T(8,128)(2,1)}, u32[]{:S(2)}, u32[]{:S(2)}) async-start(bf16[8,64,3584]{2,1,0:T(8,128)(2,1)} %bitcast.76), calls=%async_computation | async-start | bytes 7340032 | tf_op jit(solution)/shard_map/all_to_all | solution.py:416
  55.5 48.9 %all-to-all-start.1 = ((bf16[8,64,3712]{2,1,0:T(8,128)(2,1)}), bf16[8,64,3712]{2,1,0:T(8,128)(2,1)}, u32[]{:S(2)}, u32[]{:S(2)}) async-start(bf16[8,64,3712]{2,1,0:T(8,128)(2,1)} %bitcast.74), calls=%async_computation.1 | async-start | bytes 7602176 | tf_op jit(solution)/shard_map/all_to_all | solution.py:416
  80.4 24.0 %collective-permute-start = (bf16[4,448,512]{2,1,0:T(8,128)(2,1)}, bf16[4,448,512]{2,1,0:T(8,128)(2,1)S(1)}, u32[]{:S(2)}, u32[]{:S(2)}) collective-permute-start(bf16[4,448,512]{2,1,0:T(8,128)(2,1)} %get-tuple-element.32), channel_id=1, source_target_pairs={{0,8},{8,0},{16,24},{24,16},{32,40},{40,32},{48,56},{56,48},{64,72... | collective-permute-start | bytes 5505032 | tf_op jit(solution)/shard_map/ppermute | solution.py:264
  80.4 24.0 %collective-permute-start.1 = (bf16[512,1024]{1,0:T(8,128)(2,1)S(1)}, bf16[512,1024]{1,0:T(8,128)(2,1)}, u32[]{:S(2)}, u32[]{:S(2)}) collective-permute-start(bf16[512,1024]{1,0:T(8,128)(2,1)S(1)} %copy-done.2), channel_id=1, source_target_pairs={{0,8},{8,0},{16,24},{24,16},{32,40},{40,32},{48,56},{56,48},{64,72... | collective-permute-start | bytes 3145736 | tf_op jit(solution)/shard_map/ppermute | solution.py:431
  115.6 6.5 %collective-permute-start.2 = (bf16[2,512,1024]{2,1,0:T(8,128)(2,1)}, bf16[2,512,1024]{2,1,0:T(8,128)(2,1)S(1)}, u32[]{:S(2)}, u32[]{:S(2)}) collective-permute-start(bf16[2,512,1024]{2,1,0:T(8,128)(2,1)} %get-tuple-element.36.refs_0_.right_a.both_ref), channel_id=1, source_target_pairs={{0,8},{8,0},{16,24},{24,16},{32,40},{40,32},{48,56},{56,48},{64,72... | collective-permute-start | bytes 6291464 | tf_op jit(solution)/shard_map/ppermute | solution.py:435
  121.5 28.5 %collective-permute-start.3 = (bf16[4,448,512]{2,1,0:T(8,128)(2,1)}, bf16[4,448,512]{2,1,0:T(8,128)(2,1)S(1)}, u32[]{:S(2)}, u32[]{:S(2)}) collective-permute-start(bf16[4,448,512]{2,1,0:T(8,128)(2,1)} %get-tuple-element.39), channel_id=1, source_target_pairs={{0,8},{8,0},{16,24},{24,16},{32,40},{40,32},{48,56},{56,48},{64,72... | collective-permute-start | bytes 5505032 | tf_op jit(solution)/shard_map/ppermute | solution.py:264
  129.6 47.5 %collective-permute-start.4 = (bf16[448,1024]{1,0:T(8,128)(2,1)}, bf16[448,1024]{1,0:T(8,128)(2,1)S(1)}, u32[]{:S(2)}, u32[]{:S(2)}) collective-permute-start(bf16[448,1024]{1,0:T(8,128)(2,1)} %get-tuple-element.40.refs_0_), channel_id=1, source_target_pairs={{0,32},{8,40},{16,48},{24,56},{32,64},{40,72},{48,80},{56,88},{64,... | collective-permute-start | bytes 2752520 | tf_op jit(solution)/shard_map/ppermute | solution.py:388
  147.9 30.5 %collective-permute-start.5 = (bf16[448,1024]{1,0:T(8,128)(2,1)}, bf16[448,1024]{1,0:T(8,128)(2,1)}, u32[]{:S(2)}, u32[]{:S(2)}) collective-permute-start(bf16[448,1024]{1,0:T(8,128)(2,1)} %get-tuple-element.43), channel_id=1, source_target_pairs={{0,96},{8,104},{16,112},{24,120},{32,0},{40,8},{48,16},{56,24},{64... | collective-permute-start | bytes 2752520 | tf_op jit(solution)/shard_map/ppermute | solution.py:388
  157.9 56.7 %collective-permute-start.11 = (bf16[4,224,1024]{2,1,0:T(8,128)(2,1)}, bf16[4,224,1024]{2,1,0:T(8,128)(2,1)S(1)}, u32[]{:S(2)}, u32[]{:S(2)}) collective-permute-start(bf16[4,224,1024]{2,1,0:T(8,128)(2,1)} %shard_map.126.refs_0_), channel_id=1, source_target_pairs={{0,16},{8,24},{16,0},{24,8},{32,48},{40,56},{48,32},{56,40},{64,80... | collective-permute-start | bytes 5505032 | tf_op jit(solution)/shard_map/ppermute | solution.py:441
  178.4 29.6 %collective-permute-start.6 = (bf16[448,1024]{1,0:T(8,128)(2,1)}, bf16[448,1024]{1,0:T(8,128)(2,1)S(1)}, u32[]{:S(2)}, u32[]{:S(2)}) collective-permute-start(bf16[448,1024]{1,0:T(8,128)(2,1)} %add_convert_fusion.3.refs_0_), channel_id=1, source_target_pairs={{0,32},{8,40},{16,48},{24,56},{32,64},{40,72},{48,80},{56,88},{64,... | collective-permute-start | bytes 2752520 | tf_op jit(solution)/shard_map/ppermute | solution.py:388
  180.8 28.9 %collective-permute-start.7 = (bf16[448,1024]{1,0:T(8,128)(2,1)}, bf16[448,1024]{1,0:T(8,128)(2,1)}, u32[]{:S(2)}, u32[]{:S(2)}) collective-permute-start(bf16[448,1024]{1,0:T(8,128)(2,1)} %add_convert_fusion.2.refs_1_), channel_id=1, source_target_pairs={{0,96},{8,104},{16,112},{24,120},{32,0},{40,8},{48,16},{56,24},{64... | collective-permute-start | bytes 2752520 | tf_op jit(solution)/shard_map/ppermute | solution.py:388
  197.2 60.7 %all-to-all-start.2 = ((bf16[8,64,3712]{2,1,0:T(8,128)(2,1)}), bf16[8,64,3712]{2,1,0:T(8,128)(2,1)}, u32[]{:S(2)}, u32[]{:S(2)}) async-start(bf16[8,64,3712]{2,1,0:T(8,128)(2,1)} %bitcast.73), calls=%async_computation.2 | async-start | bytes 7602176 | tf_op jit(solution)/shard_map/all_to_all | solution.py:416
  209.6 32.3 %collective-permute-start.8 = (bf16[448,1024]{1,0:T(8,128)(2,1)S(1)}, bf16[448,1024]{1,0:T(8,128)(2,1)}, u32[]{:S(2)}, u32[]{:S(2)}) collective-permute-start(bf16[448,1024]{1,0:T(8,128)(2,1)S(1)} %add_convert_fusion.1.refs_0_), channel_id=1, source_target_pairs={{0,32},{8,40},{16,48},{24,56},{32,64},{40,72},{48,80},{56,88},{64,... | collective-permute-start | bytes 2752520 | tf_op jit(solution)/shard_map/ppermute | solution.py:388
  211.5 32.0 %collective-permute-start.9 = (bf16[448,1024]{1,0:T(8,128)(2,1)S(1)}, bf16[448,1024]{1,0:T(8,128)(2,1)}, u32[]{:S(2)}, u32[]{:S(2)}) collective-permute-start(bf16[448,1024]{1,0:T(8,128)(2,1)S(1)} %add_convert_fusion.refs_1_), channel_id=1, source_target_pairs={{0,96},{8,104},{16,112},{24,120},{32,0},{40,8},{48,16},{56,24},{64... | collective-permute-start | bytes 2752520 | tf_op jit(solution)/shard_map/ppermute | solution.py:388
  217.0 20.9 %collective-permute-start.15 = (bf16[224,512]{1,0:T(8,128)(2,1)}, bf16[224,512]{1,0:T(8,128)(2,1)S(1)}, u32[]{:S(2)}, u32[]{:S(2)}) collective-permute-start(bf16[224,512]{1,0:T(8,128)(2,1)} %add_convert_fusion.11), channel_id=1, source_target_pairs={{0,96},{8,104},{16,112},{24,120},{32,0},{40,8},{48,16},{56,24},{64... | collective-permute-start | bytes 688136 | tf_op jit(solution)/shard_map/ppermute | solution.py:388
  217.9 20.1 %copy-start.14 = (bf16[224,1024]{1,0:T(8,128)(2,1)S(1)}, bf16[224,1024]{1,0:T(8,128)(2,1)}, u32[]{:S(2)}) copy-start(bf16[224,1024]{1,0:T(8,128)(2,1)} %get-tuple-element.60) | copy-start | bytes 1376260
  217.9 20.1 %copy-start.18 = (bf16[224,1024]{1,0:T(8,128)(2,1)S(1)}, bf16[224,1024]{1,0:T(8,128)(2,1)}, u32[]{:S(2)}) copy-start(bf16[224,1024]{1,0:T(8,128)(2,1)} %get-tuple-element.68) | copy-start | bytes 1376260
  217.9 23.8 %copy-start.17 = (bf16[224,1024]{1,0:T(8,128)(2,1)S(1)}, bf16[224,1024]{1,0:T(8,128)(2,1)}, u32[]{:S(2)}) copy-start(bf16[224,1024]{1,0:T(8,128)(2,1)} %get-tuple-element.72) | copy-start | bytes 1376260
  217.9 23.8 %collective-permute-start.12 = (bf16[224,512]{1,0:T(8,128)(2,1)}, bf16[224,512]{1,0:T(8,128)(2,1)S(1)}, u32[]{:S(2)}, u32[]{:S(2)}) collective-permute-start(bf16[224,512]{1,0:T(8,128)(2,1)} %add_convert_fusion.15), channel_id=1, source_target_pairs={{0,32},{8,40},{16,48},{24,56},{32,64},{40,72},{48,80},{56,88},{64,... | collective-permute-start | bytes 688136 | tf_op jit(solution)/shard_map/ppermute | solution.py:388
  238.1 8.1 %collective-permute-start.16 = (bf16[224,512]{1,0:T(8,128)(2,1)S(1)}, bf16[224,512]{1,0:T(8,128)(2,1)S(1)}, u32[]{:S(2)}, u32[]{:S(2)}) collective-permute-start(bf16[224,512]{1,0:T(8,128)(2,1)S(1)} %add_convert_fusion.10), channel_id=1, source_target_pairs={{0,96},{8,104},{16,112},{24,120},{32,0},{40,8},{48,16},{56,24},{64... | collective-permute-start | bytes 688136 | tf_op jit(solution)/shard_map/ppermute | solution.py:388
  241.8 7.7 %collective-permute-start.13 = (bf16[224,512]{1,0:T(8,128)(2,1)S(1)}, bf16[224,512]{1,0:T(8,128)(2,1)S(1)}, u32[]{:S(2)}, u32[]{:S(2)}) collective-permute-start(bf16[224,512]{1,0:T(8,128)(2,1)S(1)} %add_convert_fusion.14), channel_id=1, source_target_pairs={{0,32},{8,40},{16,48},{24,56},{32,64},{40,72},{48,80},{56,88},{64,... | collective-permute-start | bytes 688136 | tf_op jit(solution)/shard_map/ppermute | solution.py:388
  245.3 21.4 %collective-permute-start.10 = (bf16[2,224,1024]{2,1,0:T(8,128)(2,1)S(1)}, bf16[2,224,1024]{2,1,0:T(8,128)(2,1)}, u32[]{:S(2)}, u32[]{:S(2)}) collective-permute-start(bf16[2,224,1024]{2,1,0:T(8,128)(2,1)S(1)} %pad_maximum_fusion.refs_0_), channel_id=1, source_target_pairs={{0,16},{8,24},{16,0},{24,8},{32,48},{40,56},{48,32},{56,40},{64,80... | collective-permute-start | bytes 2752520 | tf_op jit(solution)/shard_map/ppermute | solution.py:459
  246.3 6.8 %collective-permute-start.17 = (bf16[224,512]{1,0:T(8,128)(2,1)S(1)}, bf16[224,512]{1,0:T(8,128)(2,1)S(1)}, u32[]{:S(2)}, u32[]{:S(2)}) collective-permute-start(bf16[224,512]{1,0:T(8,128)(2,1)S(1)} %add_convert_fusion.9), channel_id=1, source_target_pairs={{0,96},{8,104},{16,112},{24,120},{32,0},{40,8},{48,16},{56,24},{64... | collective-permute-start | bytes 688136 | tf_op jit(solution)/shard_map/ppermute | solution.py:388
  249.6 7.3 %collective-permute-start.14 = (bf16[224,512]{1,0:T(8,128)(2,1)S(1)}, bf16[224,512]{1,0:T(8,128)(2,1)S(1)}, u32[]{:S(2)}, u32[]{:S(2)}) collective-permute-start(bf16[224,512]{1,0:T(8,128)(2,1)S(1)} %add_convert_fusion.13), channel_id=1, source_target_pairs={{0,32},{8,40},{16,48},{24,56},{32,64},{40,72},{48,80},{56,88},{64,... | collective-permute-start | bytes 688136 | tf_op jit(solution)/shard_map/ppermute | solution.py:388
  (23 other events, 126.6 us)

commit v4 on v3

--- a/solution.py
+++ b/solution.py
@@ -38,6 +38,12 @@
     return pl.CostEstimate(flops=flops, bytes_accessed=nbytes, transcendentals=trans)
 
 
+SHORT = cost(1, 1)
+LONG = cost(25_000_000_000, 1)
+PRODUCT = cost(16 * SUB * ROWS * FF, 8 * MB)
+WIDE_COSTS = (PRODUCT, PRODUCT, cost(14_000_000_000, 1), SHORT)
+
+
 def place_kernel(routes_ref, tokens_ref, picks_ref, out_ref):
     @pl.when(pl.program_id(0) == 0)
     def _():
@@ -223,21 +229,22 @@
         out_specs=pl.BlockSpec((ROWS, TILE), lambda i: (0, i)),
         out_shape=jax.ShapeDtypeStruct((ROWS, WIDE), BF),
         compiler_params=params(),
-        cost_estimate=cost(4 * ROWS * D * FF, 21 * MB),
+        cost_estimate=SHORT,
     )(both, gate, up, wg, *after)
 
 
 def turned_kernel(scaled, deps, place_ref, x_ref, p_ref, *refs):
     send_ref, keep_ref, turned = refs[deps:]
-    x = x_ref[...]
+    rows_in = x_ref[...]
     if scaled:
-        x = (p_ref[:, 0:1].astype(F32) * x.astype(F32)).astype(BF)
-    turned[...] = x.T
-    core = place_ref[8]
+        rows_in = (p_ref[:, 0:1].astype(F32) * rows_in.astype(F32)).astype(BF)
+    turned[...] = rows_in.T
+    core, x = place_ref[8], place_ref[9]
     for j in range(2):
         rows = slice(j * SUB, (j + 1) * SUB)
-        far = pl.multiple_of((2 * j + 1 - core) * SUB, SUB)
-        near = pl.multiple_of((2 * j + core) * SUB, SUB)
+        block = 2 * (x + j - 2 * x * j)
+        far = pl.multiple_of((block + 1 - core) * SUB, SUB)
+        near = pl.multiple_of((block + core) * SUB, SUB)
         send_ref[0, rows, :] = turned[pl.ds(far, SUB), :]
         keep_ref[0, rows, :] = turned[pl.ds(near, SUB), :]
 
@@ -305,7 +312,7 @@
             jax.ShapeDtypeStruct((TOK, TOP), BF),
         ],
         compiler_params=params(),
-        cost_estimate=cost(2 * ROWS * TOK * D, 5 * MB),
+        cost_estimate=LONG,
     )(picks, rows, *after)
 
 
@@ -356,7 +363,7 @@
         ),
         out_shape=[jax.ShapeDtypeStruct((2 * SUB, FF), BF)] * 2,
         compiler_params=params(),
-        cost_estimate=cost(16 * SUB * ROWS * FF, 8 * MB),
+        cost_estimate=WIDE_COSTS[step],
     )(place, *lefts, *rights, *after)
 
 
@@ -366,19 +373,19 @@
     refs[-1][0] = total.astype(BF)
 
 
-def down_parts(place, entry, lefts, rights, after=()):
-    left = pl.BlockSpec((1, SUB, ROWS), lambda i, place: (i, place[entry], 0))
-    right = pl.BlockSpec((ROWS, FF), lambda i, place: (0, 0))
+def down_parts(place, which, lefts, rights, after=()):
+    left = pl.BlockSpec((1, SUB, ROWS), lambda i, place: (place[i], which, 0))
+    right = pl.BlockSpec((ROWS, HALF), lambda i, place: (0, i % 2))
     return pl.pallas_call(
         down_kernel,
         grid_spec=pltpu.PrefetchScalarGridSpec(
             num_scalar_prefetch=1,
-            grid=(NZ,),
+            grid=(2 * NZ,),
             in_specs=[left, left, right, right]
             + [pl.BlockSpec(memory_space=pl.ANY)] * len(after),
-            out_specs=pl.BlockSpec((1, SUB, FF), lambda i, place: (i, 0, 0)),
+            out_specs=pl.BlockSpec((1, SUB, HALF), lambda i, place: (i, 0, 0)),
         ),
-        out_shape=jax.ShapeDtypeStruct((NZ, SUB, FF), BF),
+        out_shape=jax.ShapeDtypeStruct((2 * NZ, SUB, HALF), BF),
         compiler_params=params(),
         cost_estimate=cost(16 * SUB * ROWS * FF, 8 * MB),
     )(place, *lefts, *rights, *after)
@@ -388,21 +395,87 @@
     return lax.ppermute(up, "dp", TO_UP), lax.ppermute(down, "dp", TO_DOWN)
 
 
-def at_x(x, rows):
-    return lax.dynamic_slice_in_dim(rows, x * SUB, SUB, 0)
-
-
-def down_add(place, step, parts, moved):
-    up = [lax.dynamic_index_in_dim(p, place[2 * step], 0, keepdims=False)[:, :HALF] for p in parts]
-    down = [
-        lax.dynamic_index_in_dim(p, place[2 * step + 1], 0, keepdims=False)[:, HALF:] for p in parts
+def wide_add_kernel(part_up, part_down, up_ref, down_ref, *refs):
+    refs[-2][...] = (part_up[...].astype(F32) + up_ref[...].astype(F32)).astype(BF)
+    refs[-1][...] = (part_down[...].astype(F32) + down_ref[...].astype(F32)).astype(BF)
+
+
+def wide_add(parts, moved, after=()):
+    spec = pl.BlockSpec((SUB, FF), lambda i: (i, 0))
+    return pl.pallas_call(
+        wide_add_kernel,
+        grid=(2,),
+        in_specs=[spec] * 4 + [pl.BlockSpec(memory_space=pl.ANY)] * len(after),
+        out_specs=[spec] * 2,
+        out_shape=[jax.ShapeDtypeStruct((2 * SUB, FF), BF)] * 2,
+        compiler_params=params(),
+        cost_estimate=SHORT,
+    )(*parts, *moved, *after)
+
+
+def wide_last_kernel(part_up, part_down, up_ref, down_ref, *refs):
+    mine_ref, away_ref = refs[-2:]
+    sums = [
+        (a[...].astype(F32) + b[...].astype(F32)).astype(BF)
+        for a, b in ((part_up, up_ref), (part_down, down_ref))
     ]
-    return add(*up, *moved[:1]), add(*down, *moved[1:])
+    for step, out_ref in enumerate((away_ref, mine_ref)):
+
+        @pl.when(pl.program_id(0) == step)
+        def _():
+            out_ref[0] = sums[0]
+            out_ref[1] = sums[1]
+
+
+def wide_last(parts, moved, after=()):
+    spec = pl.BlockSpec((SUB, FF), lambda i: (1 - i, 0))
+    out = pl.BlockSpec((2, SUB, FF), lambda i: (0, 0, 0))
+    return pl.pallas_call(
+        wide_last_kernel,
+        grid=(2,),
+        in_specs=[spec] * 4 + [pl.BlockSpec(memory_space=pl.ANY)] * len(after),
+        out_specs=[out] * 2,
+        out_shape=[jax.ShapeDtypeStruct((2, SUB, FF), BF)] * 2,
+        compiler_params=params(),
+        cost_estimate=SHORT,
+    )(*parts, *moved, *after)
+
+
+def down_add_kernel(moved, near_ref, far_ref, *refs):
+    sums = [near_ref[k].astype(F32) + far_ref[k].astype(F32) for k in range(2)]
+    if moved:
+        sums = [a + ref[...].astype(F32) for a, ref in zip(sums, refs)]
+    if len(refs[-1].shape) == 2 and refs[-1].shape[1] == FF:
+        refs[-1][:, :HALF] = sums[0].astype(BF)
+        refs[-1][:, HALF:] = sums[1].astype(BF)
+    else:
+        refs[-2][...] = sums[0].astype(BF)
+        refs[-1][...] = sums[1].astype(BF)
+
+
+def down_add(step, parts, moved=(), after=()):
+    pair = pl.BlockSpec((2, SUB, HALF), lambda i: (step, 0, 0))
+    one = pl.BlockSpec((SUB, HALF), lambda i: (0, 0))
+    whole = pl.BlockSpec((SUB, FF), lambda i: (0, 0))
+    last = step == NZ - 1
+    return pl.pallas_call(
+        functools.partial(down_add_kernel, len(moved) > 0),
+        grid=(1,),
+        in_specs=[pair] * 2
+        + [one] * len(moved)
+        + [pl.BlockSpec(memory_space=pl.ANY)] * len(after),
+        out_specs=[whole] if last else [one] * 2,
+        out_shape=[jax.ShapeDtypeStruct((SUB, FF), BF)]
+        if last
+        else [jax.ShapeDtypeStruct((SUB, HALF), BF)] * 2,
+        compiler_params=params(),
+        cost_estimate=LONG if step == 1 else SHORT,
+    )(*parts, *moved, *after)
 
 
 PLACES = np.array(
     [
-        [v for s in range(NZ) for v in ((z - 1 - s) % NZ, (z + 1 + s) % NZ)] + [c, x, 1 - x]
+        [v for s in range(NZ) for v in ((z - 1 - s) % NZ, (z + 1 + s) % NZ)] + [c, x]
         for z in range(NZ)
         for x in range(2)
         for c in range(2)
@@ -420,7 +493,7 @@
 
 
 def local(tokens, grad_out, routes, probs, w_gate, w_up, w_down):
-    place = lax.dynamic_index_in_dim(jnp.asarray(PLACES), lax.axis_index("dp"), 0, keepdims=False)
+    place = lax.dynamic_slice(PLACES.reshape(-1), (10 * lax.axis_index("dp"),), (10,))
     gate, up, down = w_gate[0], w_up[0], w_down[0]
     picks, send_tokens = place_tokens(routes, tokens)
     row_tokens = exchange(send_tokens)
@@ -434,31 +507,32 @@
     )
     boths = (both, lax.ppermute(both, "dp", TO_CORE))
     dlefts = turned(place, row_grads_in, row_grads_in, True, after=(both,))
-    x = place[9]
     ring0 = wide_parts(place, 0, lefts, boths, after=dlefts[:1])
     moved0 = around(*ring0)
-    far = down_parts(place, 10, dlefts, hiddens, after=ring0[:1])
+    far = down_parts(place, 1, dlefts, hiddens, after=ring0[:1])
     far_in = lax.ppermute(far, "dp", TO_X)
     parts1 = wide_parts(place, 1, lefts, boths, after=(far,))
-    near = down_parts(place, 9, dlefts, hiddens, after=parts1[:1])
-    ring1 = add(parts1[0], moved0[0]), add(parts1[1], moved0[1])
+    near = down_parts(place, 0, dlefts, hiddens, after=parts1[:1])
+    ring1 = wide_add(parts1, moved0, after=(near,))
     moved1 = around(*ring1)
-    sent_rows = row_grads(both, gate, up, wg, after=ring1 + (near,))
+    sent_rows = row_grads(both, gate, up, wg, after=ring1)
     returned = exchange(sent_rows)
     parts2 = wide_parts(place, 2, lefts, boths, after=(sent_rows,))
     down_pair = (near, far_in)
-    down_moved0 = around(*down_add(place, 0, down_pair, ()))
-    ring2 = add(parts2[0], moved1[0]), add(parts2[1], moved1[1])
+    down_ring0 = down_add(0, down_pair, after=parts2[:1])
+    down_moved0 = around(*down_ring0)
+    ring2 = wide_add(parts2, moved1, after=down_ring0)
     moved2 = around(*ring2)
     parts3 = wide_parts(place, 3, lefts, boths, after=ring2)
-    down_moved1 = around(*down_add(place, 1, down_pair, down_moved0))
-    down_moved2 = around(*down_add(place, 2, down_pair, down_moved1))
-    down_grad = jnp.concatenate(down_add(place, 3, down_pair, down_moved2), axis=1)
-    mine = [add(at_x(x, a), at_x(x, b)) for a, b in zip(parts3, moved2)]
-    away = jnp.stack([add(at_x(1 - x, a), at_x(1 - x, b)) for a, b in zip(parts3, moved2)])
+    down_ring1 = down_add(1, down_pair, down_moved0, after=parts3[:1])
+    down_moved1 = around(*down_ring1)
+    mine, away = wide_last(parts3, moved2, after=down_ring1)
     came = lax.ppermute(away, "dp", TO_X)
-    grad_tokens, grad_weights = combine(picks, returned, after=(away,))
-    mine, grad_tokens = lax.optimization_barrier((mine, grad_tokens))
+    down_ring2 = down_add(2, down_pair, down_moved1, after=(away,))
+    down_moved2 = around(*down_ring2)
+    grad_tokens, grad_weights = combine(picks, returned, after=down_ring2)
+    (down_grad,) = down_add(3, down_pair, down_moved2, after=(grad_tokens,))
+    mine, down_grad = lax.optimization_barrier((mine, down_grad))
     grad_gate = add(mine[0], came[0])[None]
     grad_up = add(mine[1], came[1])[None]
     grad_down = down_grad[None]

time: 271 us -> 254 us (0.937)
  Pallas kernels: 98.1 us -> 122 us
  between operations: 16.7 us -> 0.76 us
  other arithmetic: 15.8 us -> 1.27 us
  waiting for transfers between devices: 85 us -> 75.8 us
    pallas_call x0 -> x7, Pallas kernels: none -> 18.5 us  [the longest x4 8.6 us: down_add(): pl.pallas_call(functools.partial(down_add_kernel, len(moved) > 0), grid=(...]
    ppermute x12, waiting for transfers between devices: 19 us -> 9.03 us  [around(): return (lax.ppermute(up, 'dp', TO_UP), lax.ppermute(down, 'dp', TO_DOWN))]
    convert_element_type x12 -> x1, other arithmetic: 9.33 us -> 1.27 us  [add(): return total.astype(BF)]
    unnamed x55 -> x41, local copies, waits for them, and re-layouts: 7.52 us -> 13.8 us
    pallas_call x2, Pallas kernels: 13 us -> 19 us  [down_parts(): pl.pallas_call(down_kernel, grid_spec=pltpu.PrefetchScalarGridSpec(num_sc...]
    squeeze x2 -> x0, local copies, waits for them, and re-layouts: 5.45 us -> none  [down_add(): lax.dynamic_index_in_dim(p, place[2 * step], 0, keepdims=False)[:, :HALF]]
    broadcast_in_dim x2 -> x0, other arithmetic: 3.25 us -> none  [the longest x1 2.42 us: local(): grad_up = add(mine[1], came[1])[None]]
    another operation x3 -> x0, other arithmetic: 3.23 us -> none  [local(): jnp.stack([add(at_x(1 - x, a), at_x(1 - x, b)) for a, b in zip(parts3, mo...]
  transfers between devices with their start and end apart: 21 -> 21, of which waited for: 6 -> 5; matrix products, arithmetic and copies ran while one was open for 8% -> 1% of each run, Pallas kernels for 31% -> 43%
where the time goes in v4:
time: 254 us; the launch traced here: 253 us
  Pallas kernels  122 us (48%)
  waiting for transfers between devices  75.8 us (30%)
  starting transfers between devices  38.3 us (15%)
  local copies, waits for them, and re-layouts  14.3 us (6%)
    all_to_all x3, waiting for transfers between devices, exchange(): lax.all_to_all(rows.reshape(EXPERTS, CAP, width), 'expert', split_axis=0,...  63.2 us
    pallas_call x4, Pallas kernels, wide_parts(): pl.pallas_call(wide_kernel, grid_spec=pltpu.PrefetchScalarGridSpec(num_sc...  24.7 us
    pallas_call x2, Pallas kernels, down_parts(): pl.pallas_call(down_kernel, grid_spec=pltpu.PrefetchScalarGridSpec(num_sc...  19 us
    ppermute x12, starting transfers between devices, around(): return (lax.ppermute(up, 'dp', TO_UP), lax.ppermute(down, 'dp', TO_DOWN))  19 us
    all_to_all x3, starting transfers between devices, exchange(): lax.all_to_all(rows.reshape(EXPERTS, CAP, width), 'expert', split_axis=0,...  14.8 us
    unnamed x41, local copies, waits for them, and re-layouts  13.8 us
    pallas_call x1, Pallas kernels, forward(): pl.pallas_call(forward_kernel, grid=(FF // n,), in_specs=[pl.BlockSpec((R...  13.3 us
    pallas_call x1, Pallas kernels, row_grads(): pl.pallas_call(rows_kernel, grid=(NT + 1,), in_specs=[pl.BlockSpec((2, RO...  13.1 us
  transfers between devices with their start and end apart: 21, of which 5 were waited for; matrix products, arithmetic and copies ran while one was open for 1% of the time, Pallas kernels for 43%

profile of v4, /device:TPU:0, one launch (start us, length us, event | category | flops | bytes accessed | tf_op | source)
XLA Modules:
  0.0 252.9 jit_solution(1698835541141200437)
XLA Ops:
  2.0 3.9 %shard_map.119 = (bf16[2,512,128]{2,1,0:T(8,128)(2,1)}, bf16[512,3584]{1,0:T(8,128)(2,1)}) custom-call(s32[128,2]{1,0:T(8,128)} %copy.13.routes_ref, bf16[128,3584]{1,0:T(8,128)(2,1)} %tokens_ref.1), custom_call_target="tpu_custom_call" | custom-call | flops 469762048 | bytes 5242880 | tf_op jit(solution)/shard_map/pallas_call | solution.py:71
  6.0 5.6 %all-to-all-start.1 = ((bf16[8,64,3584]{2,1,0:T(8,128)(2,1)}), bf16[8,64,3584]{2,1,0:T(8,128)(2,1)}, u32[]{:S(2)}, u32[]{:S(2)}) async-start(bf16[8,64,3584]{2,1,0:T(8,128)(2,1)} %bitcast.17), calls=%async_computation.1 | async-start | bytes 7340032 | tf_op jit(solution)/shard_map/all_to_all | solution.py:489
  12.3 4.0 %shard_map.120 = bf16[512,3712]{1,0:T(8,128)(2,1)} custom-call(bf16[2,512,128]{2,1,0:T(8,128)(2,1)} %get-tuple-element.40.picks_ref, bf16[128,2]{1,0:T(8,128)(2,1)} %copy.14.probs_ref, bf16[128,3584]{1,0:T(8,128)(2,1)} %grads_ref.1), custom_call_target="tpu_custom_call" | custom-call | flops 469762048 | bytes 5242880 | tf_op jit(solution)/shard_map/pallas_call | solution.py:110
  16.3 39.2 %all-to-all-done.1 = bf16[8,64,3584]{2,1,0:T(8,128)(2,1)} async-done(((bf16[8,64,3584]{2,1,0:T(8,128)(2,1)}), bf16[8,64,3584]{2,1,0:T(8,128)(2,1)}, u32[]{:S(2)}, u32[]{:S(2)}) %all-to-all-start.1) | async-done | bytes 3670048 | tf_op jit(solution)/shard_map/all_to_all | solution.py:489
  55.5 4.7 %all-to-all-start = ((bf16[8,64,3712]{2,1,0:T(8,128)(2,1)}), bf16[8,64,3712]{2,1,0:T(8,128)(2,1)}, u32[]{:S(2)}, u32[]{:S(2)}) async-start(bf16[8,64,3712]{2,1,0:T(8,128)(2,1)} %bitcast.10), calls=%async_computation | async-start | bytes 7602176 | tf_op jit(solution)/shard_map/all_to_all | solution.py:489
  60.8 13.3 %shard_map.121 = (bf16[512,1024]{1,0:T(8,128)(2,1)}, f32[512,1024]{1,0:T(8,128)}, f32[512,1024]{1,0:T(8,128)}) custom-call(bf16[512,3584]{1,0:T(8,128)(2,1)} %bitcast.4.x_ref.p_ref, bf16[3584,1024]{1,0:T(8,128)(2,1)} %bitcast.13, bf16[3584,1024]{1,0:T(8,128)(2,1)} %bitcast.15), custom_call_target="tpu_custom_call" | custom-call | flops 7516192768 | bytes 24117248 | tf_op jit(solution)/shard_map/pallas_call | solution.py:138
  74.1 5.8 %shard_map.122 = (bf16[4,448,512]{2,1,0:T(8,128)(2,1)}, bf16[4,448,512]{2,1,0:T(8,128)(2,1)}) custom-call(s32[10]{0:T(128)} %dynamic_slice.3.place_ref, bf16[512,3584]{1,0:T(8,128)(2,1)} %bitcast.4.x_ref.p_ref, bf16[512,3584]{1,0:T(8,128)(2,1)} %bitcast.4.x_ref.p_ref, bf16[512,1024]{1,0:T(8,128)(2,1)} %get-tuple-element.42.refs_0_.hidden_ref.right_a), custom_call_target="tpu_custom_call" | custom-call | flops 1835008 | bytes 8388608 | tf_op jit(solution)/shard_map/pallas_call | solution.py:254
  80.5 24.1 %all-to-all-done = bf16[8,64,3712]{2,1,0:T(8,128)(2,1)} async-done(((bf16[8,64,3712]{2,1,0:T(8,128)(2,1)}), bf16[8,64,3712]{2,1,0:T(8,128)(2,1)}, u32[]{:S(2)}, u32[]{:S(2)}) %all-to-all-start) | async-done | bytes 3801120 | tf_op jit(solution)/shard_map/all_to_all | solution.py:489
  105.8 9.9 %shard_map.123 = (bf16[2,512,1024]{2,1,0:T(8,128)(2,1)}, bf16[512,128]{1,0:T(8,128)(2,1)}) custom-call(bf16[512,3712]{1,0:T(8,128)(2,1)} %bitcast.1.g_ref.x_ref.p_ref, bf16[3584,1024]{1,0:T(8,128)(2,1)} %bitcast.12, bf16[512,1024]{1,0:T(8,128)(2,1)} %get-tuple-element.42.refs_0_.hidden_ref.right_a, f32[512,1024]{1,0:T(8,128)} %get-tuple-element.43.active_ref, ...), custom_call_target="tpu_custom_call" | custom-call | flops 3758096384 | bytes 18874368 | tf_op jit(solution)/shard_map/pallas_call | solution.py:177
  115.7 6.0 %shard_map.124 = (bf16[4,448,512]{2,1,0:T(8,128)(2,1)}, bf16[4,448,512]{2,1,0:T(8,128)(2,1)}) custom-call(s32[10]{0:T(128)} %dynamic_slice.3.place_ref, bf16[512,3712]{1,0:T(8,128)(2,1)} %bitcast.1.g_ref.x_ref.p_ref, bf16[512,3712]{1,0:T(8,128)(2,1)} %bitcast.1.g_ref.x_ref.p_ref, bf16[2,512,1024]{2,1,0:T(8,128)(2,1)} %get-tuple-element.47.refs_0_.right_a.both_ref), custom_call_target="tpu_custom_call" | custom-call | flops 1835008 | bytes 8388608 | tf_op jit(solution)/shard_map/pallas_call | solution.py:254
  123.5 6.2 %shard_map.125 = (bf16[448,1024]{1,0:T(8,128)(2,1)}, bf16[448,1024]{1,0:T(8,128)(2,1)}) custom-call(s32[10]{0:T(128)} %dynamic_slice.3.place_ref, bf16[4,448,512]{2,1,0:T(8,128)(2,1)} %get-tuple-element.45.refs_0_.left_a, bf16[4,448,512]{2,1,0:T(8,128)(2,1)} %copy-done, bf16[2,512,1024]{2,1,0:T(8,128)(2,1)} %get-tuple-element.47.refs_0_.right_a.both_ref, ...), custom_call_target="tpu_custom_call" | custom-call | flops 1879048192 | bytes 8388608 | tf_op jit(solution)/shard_map/pallas_call | solution.py:355
  135.0 9.5 %shard_map.126.refs_0_ = bf16[8,224,512]{2,1,0:T(8,128)(2,1)} custom-call(s32[10]{0:T(128)} %dynamic_slice.3.place_ref, bf16[4,448,512]{2,1,0:T(8,128)(2,1)} %get-tuple-element.49.refs_0_.left_a, bf16[4,448,512]{2,1,0:T(8,128)(2,1)} %copy-done.4, bf16[512,1024]{1,0:T(8,128)(2,1)} %get-tuple-element.42.refs_0_.hidden_ref.right_a, ...), custom_call_target="tpu_custom_call" | custom-call | flops 1879048192 | bytes 8388608 | tf_op jit(solution)/shard_map/pallas_call | solution.py:379
  147.2 6.2 %shard_map.127 = (bf16[448,1024]{1,0:T(8,128)(2,1)}, bf16[448,1024]{1,0:T(8,128)(2,1)}) custom-call(s32[10]{0:T(128)} %dynamic_slice.3.place_ref, bf16[4,448,512]{2,1,0:T(8,128)(2,1)} %get-tuple-element.45.refs_0_.left_a, bf16[4,448,512]{2,1,0:T(8,128)(2,1)} %copy-done, bf16[2,512,1024]{2,1,0:T(8,128)(2,1)} %get-tuple-element.47.refs_0_.right_a.both_ref, ...), custom_call_target="tpu_custom_call" | custom-call | flops 1879048192 | bytes 8388608 | tf_op jit(solution)/shard_map/pallas_call | solution.py:355
  153.4 9.5 %shard_map.128.refs_0_.near_ref = bf16[8,224,512]{2,1,0:T(8,128)(2,1)} custom-call(s32[10]{0:T(128)} %dynamic_slice.3.place_ref, bf16[4,448,512]{2,1,0:T(8,128)(2,1)} %get-tuple-element.49.refs_0_.left_a, bf16[4,448,512]{2,1,0:T(8,128)(2,1)} %copy-done.4, bf16[512,1024]{1,0:T(8,128)(2,1)} %get-tuple-element.42.refs_0_.hidden_ref.right_a, ...), custom_call_target="tpu_custom_call" | custom-call | flops 1879048192 | bytes 8388608 | tf_op jit(solution)/shard_map/pallas_call | solution.py:379
  169.0 13.1 %shard_map.130.refs_0_ = bf16[512,3712]{1,0:T(8,128)(2,1)} custom-call(bf16[2,512,1024]{2,1,0:T(8,128)(2,1)} %get-tuple-element.47.refs_0_.right_a.both_ref, bf16[3584,1024]{1,0:T(8,128)(2,1)} %bitcast.14, bf16[3584,1024]{1,0:T(8,128)(2,1)} %bitcast.16, bf16[512,128]{1,0:T(8,128)(2,1)} %get-tuple-element.48.wg_ref, ...), custom_call_target="tpu_custom_call" | custom-call | flops 1 | bytes 1 | tf_op jit(solution)/shard_map/pallas_call | solution.py:219
  182.1 4.5 %all-to-all-start.2 = ((bf16[8,64,3712]{2,1,0:T(8,128)(2,1)}), bf16[8,64,3712]{2,1,0:T(8,128)(2,1)}, u32[]{:S(2)}, u32[]{:S(2)}) async-start(bf16[8,64,3712]{2,1,0:T(8,128)(2,1)} %bitcast.11), calls=%async_computation.2 | async-start | bytes 7602176 | tf_op jit(solution)/shard_map/all_to_all | solution.py:489
  186.6 6.2 %shard_map.131 = (bf16[448,1024]{1,0:T(8,128)(2,1)}, bf16[448,1024]{1,0:T(8,128)(2,1)}) custom-call(s32[10]{0:T(128)} %dynamic_slice.3.place_ref, bf16[4,448,512]{2,1,0:T(8,128)(2,1)} %get-tuple-element.45.refs_0_.left_a, bf16[4,448,512]{2,1,0:T(8,128)(2,1)} %copy-done, bf16[2,512,1024]{2,1,0:T(8,128)(2,1)} %get-tuple-element.47.refs_0_.right_a.both_ref, ...), custom_call_target="tpu_custom_call" | custom-call | flops 14000000000 | bytes 1 | tf_op jit(solution)/shard_map/pallas_call | solution.py:355
  203.3 3.2 %collective-permute-start.14 = (bf16[448,1024]{1,0:T(8,128)(2,1)}, bf16[448,1024]{1,0:T(8,128)(2,1)S(1)}, u32[]{:S(2)}, u32[]{:S(2)}) collective-permute-start(bf16[448,1024]{1,0:T(8,128)(2,1)} %get-tuple-element.62.refs_1_), channel_id=1, source_target_pairs={{0,96},{8,104},{16,112},{24,120},{32,0},{40,8},{48,16},{56,24},{64... | collective-permute-start | bytes 2752520 | tf_op jit(solution)/shard_map/ppermute | solution.py:395
  206.5 6.2 %shard_map.134 = (bf16[448,1024]{1,0:T(8,128)(2,1)}, bf16[448,1024]{1,0:T(8,128)(2,1)}) custom-call(s32[10]{0:T(128)} %dynamic_slice.3.place_ref, bf16[4,448,512]{2,1,0:T(8,128)(2,1)} %get-tuple-element.45.refs_0_.left_a, bf16[4,448,512]{2,1,0:T(8,128)(2,1)} %copy-done, bf16[2,512,1024]{2,1,0:T(8,128)(2,1)} %get-tuple-element.47.refs_0_.right_a.both_ref, ...), custom_call_target="tpu_custom_call" | custom-call | flops 1 | bytes 1 | tf_op jit(solution)/shard_map/pallas_call | solution.py:355
  215.7 3.2 %collective-permute-start.12 = (bf16[224,512]{1,0:T(8,128)(2,1)}, bf16[224,512]{1,0:T(8,128)(2,1)S(1)}, u32[]{:S(2)}, u32[]{:S(2)}) collective-permute-start(bf16[224,512]{1,0:T(8,128)(2,1)} %get-tuple-element.65.refs_1_), channel_id=1, source_target_pairs={{0,96},{8,104},{16,112},{24,120},{32,0},{40,8},{48,16},{56,24},{64... | collective-permute-start | bytes 688136 | tf_op jit(solution)/shard_map/ppermute | solution.py:395
  218.9 8.9 %collective-permute-done.13.up_ref = bf16[448,1024]{1,0:T(8,128)(2,1)S(1)} collective-permute-done((bf16[448,1024]{1,0:T(8,128)(2,1)}, bf16[448,1024]{1,0:T(8,128)(2,1)S(1)}, u32[]{:S(2)}, u32[]{:S(2)}) %collective-permute-start.13) | collective-permute-done | bytes 917536 | tf_op jit(solution)/shard_map/ppermute | solution.py:395
  229.0 3.7 %shard_map.136 = (bf16[2,224,1024]{2,1,0:T(8,128)(2,1)}, bf16[2,224,1024]{2,1,0:T(8,128)(2,1)}) custom-call(bf16[448,1024]{1,0:T(8,128)(2,1)} %get-tuple-element.63.refs_2_.part_up, bf16[448,1024]{1,0:T(8,128)(2,1)} %get-tuple-element.66.part_down, bf16[448,1024]{1,0:T(8,128)(2,1)} %copy-done.6, bf16[448,1024]{1,0:T(8,128)(2,1)} %copy-done.8, ...), custom_call_target="tpu_custom_call" | custom-call | flops 1 | bytes 1 | tf_op jit(solution)/shard_map/pallas_call | solution.py:433
  240.3 4.1 %shard_map.138 = (bf16[128,3584]{1,0:T(8,128)(2,1)}, bf16[128,2]{1,0:T(8,128)(2,1)}) custom-call(bf16[2,512,128]{2,1,0:T(8,128)(2,1)} %get-tuple-element.40.picks_ref, bf16[512,3712]{1,0:T(8,128)(2,1)} %bitcast.8.rows_ref, bf16[224,512]{1,0:T(8,128)(2,1)} %get-tuple-element.68.refs_0_, bf16[224,512]{1,0:T(8,128)(2,1)} %get-tuple-element.69.refs_1_), custom_call_target="tpu_custom_call" | custom-call | flops 24999999488 | bytes 1 | tf_op jit(solution)/shard_map/pallas_call | solution.py:298
  248.1 3.5 %collective-permute-done.17 = bf16[2,224,1024]{2,1,0:T(8,128)(2,1)S(1)} collective-permute-done((bf16[2,224,1024]{2,1,0:T(8,128)(2,1)}, bf16[2,224,1024]{2,1,0:T(8,128)(2,1)S(1)}, u32[]{:S(2)}, u32[]{:S(2)}) %collective-permute-start.17) | collective-permute-done | bytes 917536 | tf_op jit(solution)/shard_map/ppermute | solution.py:530
  (82 shorter events, 47.6 us)
Async XLA Ops:
  6.0 5.6 %copy-start.15 = (bf16[128,2]{0,1:T(2,128)(2,1)S(1)}, bf16[128,2]{0,1:T(2,128)(2,1)}, u32[]{:S(2)}) copy-start(bf16[128,2]{0,1:T(2,128)(2,1)} %param.11) | copy-start | bytes 1540
  6.0 49.5 %all-to-all-start.1 = ((bf16[8,64,3584]{2,1,0:T(8,128)(2,1)}), bf16[8,64,3584]{2,1,0:T(8,128)(2,1)}, u32[]{:S(2)}, u32[]{:S(2)}) async-start(bf16[8,64,3584]{2,1,0:T(8,128)(2,1)} %bitcast.17), calls=%async_computation.1 | async-start | bytes 7340032 | tf_op jit(solution)/shard_map/all_to_all | solution.py:489
  55.5 49.0 %all-to-all-start = ((bf16[8,64,3712]{2,1,0:T(8,128)(2,1)}), bf16[8,64,3712]{2,1,0:T(8,128)(2,1)}, u32[]{:S(2)}, u32[]{:S(2)}) async-start(bf16[8,64,3712]{2,1,0:T(8,128)(2,1)} %bitcast.10), calls=%async_computation | async-start | bytes 7602176 | tf_op jit(solution)/shard_map/all_to_all | solution.py:489
  74.1 5.8 %copy-start.2 = (bf16[512,1024]{1,0:T(8,128)(2,1)S(1)}, bf16[512,1024]{1,0:T(8,128)(2,1)}, u32[]{:S(2)}) copy-start(bf16[512,1024]{1,0:T(8,128)(2,1)} %get-tuple-element.42.refs_0_.hidden_ref.right_a) | copy-start | bytes 3145732
  79.9 24.6 %collective-permute-start = (bf16[4,448,512]{2,1,0:T(8,128)(2,1)}, bf16[4,448,512]{2,1,0:T(8,128)(2,1)S(1)}, u32[]{:S(2)}, u32[]{:S(2)}) collective-permute-start(bf16[4,448,512]{2,1,0:T(8,128)(2,1)} %get-tuple-element.46), channel_id=1, source_target_pairs={{0,8},{8,0},{16,24},{24,16},{32,40},{40,32},{48,56},{56,48},{64,72... | collective-permute-start | bytes 5505032 | tf_op jit(solution)/shard_map/ppermute | solution.py:271
  80.0 24.6 %collective-permute-start.1 = (bf16[512,1024]{1,0:T(8,128)(2,1)S(1)}, bf16[512,1024]{1,0:T(8,128)(2,1)}, u32[]{:S(2)}, u32[]{:S(2)}) collective-permute-start(bf16[512,1024]{1,0:T(8,128)(2,1)S(1)} %copy-done.2), channel_id=1, source_target_pairs={{0,8},{8,0},{16,24},{24,16},{32,40},{40,32},{48,56},{56,48},{64,72... | collective-permute-start | bytes 3145736 | tf_op jit(solution)/shard_map/ppermute | solution.py:504
  115.7 6.5 %collective-permute-start.2 = (bf16[2,512,1024]{2,1,0:T(8,128)(2,1)}, bf16[2,512,1024]{2,1,0:T(8,128)(2,1)S(1)}, u32[]{:S(2)}, u32[]{:S(2)}) collective-permute-start(bf16[2,512,1024]{2,1,0:T(8,128)(2,1)} %get-tuple-element.47.refs_0_.right_a.both_ref), channel_id=1, source_target_pairs={{0,8},{8,0},{16,24},{24,16},{32,40},{40,32},{48,56},{56,48},{64,72... | collective-permute-start | bytes 6291464 | tf_op jit(solution)/shard_map/ppermute | solution.py:508
  121.7 12.1 %collective-permute-start.3 = (bf16[4,448,512]{2,1,0:T(8,128)(2,1)}, bf16[4,448,512]{2,1,0:T(8,128)(2,1)S(1)}, u32[]{:S(2)}, u32[]{:S(2)}) collective-permute-start(bf16[4,448,512]{2,1,0:T(8,128)(2,1)} %get-tuple-element.50), channel_id=1, source_target_pairs={{0,8},{8,0},{16,24},{24,16},{32,40},{40,32},{48,56},{56,48},{64,72... | collective-permute-start | bytes 5505032 | tf_op jit(solution)/shard_map/ppermute | solution.py:271
  129.7 33.2 %collective-permute-start.4 = (bf16[448,1024]{1,0:T(8,128)(2,1)}, bf16[448,1024]{1,0:T(8,128)(2,1)S(1)}, u32[]{:S(2)}, u32[]{:S(2)}) collective-permute-start(bf16[448,1024]{1,0:T(8,128)(2,1)} %get-tuple-element.51.refs_0_), channel_id=1, source_target_pairs={{0,32},{8,40},{16,48},{24,56},{32,64},{40,72},{48,80},{56,88},{64,... | collective-permute-start | bytes 2752520 | tf_op jit(solution)/shard_map/ppermute | solution.py:395
  131.6 31.3 %collective-permute-start.5 = (bf16[448,1024]{1,0:T(8,128)(2,1)}, bf16[448,1024]{1,0:T(8,128)(2,1)}, u32[]{:S(2)}, u32[]{:S(2)}) collective-permute-start(bf16[448,1024]{1,0:T(8,128)(2,1)} %get-tuple-element.54), channel_id=1, source_target_pairs={{0,96},{8,104},{16,112},{24,120},{32,0},{40,8},{48,16},{56,24},{64... | collective-permute-start | bytes 2752520 | tf_op jit(solution)/shard_map/ppermute | solution.py:395
  144.5 48.3 %collective-permute-start.6 = (bf16[8,224,512]{2,1,0:T(8,128)(2,1)}, bf16[8,224,512]{2,1,0:T(8,128)(2,1)S(1)}, u32[]{:S(2)}, u32[]{:S(2)}) collective-permute-start(bf16[8,224,512]{2,1,0:T(8,128)(2,1)} %shard_map.126.refs_0_), channel_id=1, source_target_pairs={{0,16},{8,24},{16,0},{24,8},{32,48},{40,56},{48,32},{56,40},{64,80... | collective-permute-start | bytes 5505032 | tf_op jit(solution)/shard_map/ppermute | solution.py:513
  167.0 32.3 %collective-permute-start.10 = (bf16[448,1024]{1,0:T(8,128)(2,1)}, bf16[448,1024]{1,0:T(8,128)(2,1)S(1)}, u32[]{:S(2)}, u32[]{:S(2)}) collective-permute-start(bf16[448,1024]{1,0:T(8,128)(2,1)} %get-tuple-element.56.refs_1_), channel_id=1, source_target_pairs={{0,96},{8,104},{16,112},{24,120},{32,0},{40,8},{48,16},{56,24},{64... | collective-permute-start | bytes 2752520 | tf_op jit(solution)/shard_map/ppermute | solution.py:395
  169.0 30.3 %collective-permute-start.9 = (bf16[448,1024]{1,0:T(8,128)(2,1)}, bf16[448,1024]{1,0:T(8,128)(2,1)}, u32[]{:S(2)}, u32[]{:S(2)}) collective-permute-start(bf16[448,1024]{1,0:T(8,128)(2,1)} %get-tuple-element.55.refs_0_), channel_id=1, source_target_pairs={{0,32},{8,40},{16,48},{24,56},{32,64},{40,72},{48,80},{56,88},{64,... | collective-permute-start | bytes 2752520 | tf_op jit(solution)/shard_map/ppermute | solution.py:395
  182.1 58.2 %all-to-all-start.2 = ((bf16[8,64,3712]{2,1,0:T(8,128)(2,1)}), bf16[8,64,3712]{2,1,0:T(8,128)(2,1)}, u32[]{:S(2)}, u32[]{:S(2)}) async-start(bf16[8,64,3712]{2,1,0:T(8,128)(2,1)} %bitcast.11), calls=%async_computation.2 | async-start | bytes 7602176 | tf_op jit(solution)/shard_map/all_to_all | solution.py:489
  196.1 16.7 %collective-permute-start.7 = (bf16[224,512]{1,0:T(8,128)(2,1)}, bf16[224,512]{1,0:T(8,128)(2,1)S(1)}, u32[]{:S(2)}, u32[]{:S(2)}) collective-permute-start(bf16[224,512]{1,0:T(8,128)(2,1)} %get-tuple-element.58.refs_0_), channel_id=1, source_target_pairs={{0,32},{8,40},{16,48},{24,56},{32,64},{40,72},{48,80},{56,88},{64,... | collective-permute-start | bytes 688136 | tf_op jit(solution)/shard_map/ppermute | solution.py:395
  196.1 16.7 %collective-permute-start.8 = (bf16[224,512]{1,0:T(8,128)(2,1)}, bf16[224,512]{1,0:T(8,128)(2,1)S(1)}, u32[]{:S(2)}, u32[]{:S(2)}) collective-permute-start(bf16[224,512]{1,0:T(8,128)(2,1)} %get-tuple-element.59.refs_1_), channel_id=1, source_target_pairs={{0,96},{8,104},{16,112},{24,120},{32,0},{40,8},{48,16},{56,24},{64... | collective-permute-start | bytes 688136 | tf_op jit(solution)/shard_map/ppermute | solution.py:395
  203.3 24.5 %collective-permute-start.13 = (bf16[448,1024]{1,0:T(8,128)(2,1)}, bf16[448,1024]{1,0:T(8,128)(2,1)S(1)}, u32[]{:S(2)}, u32[]{:S(2)}) collective-permute-start(bf16[448,1024]{1,0:T(8,128)(2,1)} %get-tuple-element.61.refs_0_), channel_id=1, source_target_pairs={{0,32},{8,40},{16,48},{24,56},{32,64},{40,72},{48,80},{56,88},{64,... | collective-permute-start | bytes 2752520 | tf_op jit(solution)/shard_map/ppermute | solution.py:395
  203.3 24.5 %collective-permute-start.14 = (bf16[448,1024]{1,0:T(8,128)(2,1)}, bf16[448,1024]{1,0:T(8,128)(2,1)S(1)}, u32[]{:S(2)}, u32[]{:S(2)}) collective-permute-start(bf16[448,1024]{1,0:T(8,128)(2,1)} %get-tuple-element.62.refs_1_), channel_id=1, source_target_pairs={{0,96},{8,104},{16,112},{24,120},{32,0},{40,8},{48,16},{56,24},{64... | collective-permute-start | bytes 2752520 | tf_op jit(solution)/shard_map/ppermute | solution.py:395
  215.7 17.8 %collective-permute-start.11 = (bf16[224,512]{1,0:T(8,128)(2,1)}, bf16[224,512]{1,0:T(8,128)(2,1)S(1)}, u32[]{:S(2)}, u32[]{:S(2)}) collective-permute-start(bf16[224,512]{1,0:T(8,128)(2,1)} %get-tuple-element.64.refs_0_), channel_id=1, source_target_pairs={{0,32},{8,40},{16,48},{24,56},{32,64},{40,72},{48,80},{56,88},{64,... | collective-permute-start | bytes 688136 | tf_op jit(solution)/shard_map/ppermute | solution.py:395
  215.7 17.8 %collective-permute-start.12 = (bf16[224,512]{1,0:T(8,128)(2,1)}, bf16[224,512]{1,0:T(8,128)(2,1)S(1)}, u32[]{:S(2)}, u32[]{:S(2)}) collective-permute-start(bf16[224,512]{1,0:T(8,128)(2,1)} %get-tuple-element.65.refs_1_), channel_id=1, source_target_pairs={{0,96},{8,104},{16,112},{24,120},{32,0},{40,8},{48,16},{56,24},{64... | collective-permute-start | bytes 688136 | tf_op jit(solution)/shard_map/ppermute | solution.py:395
  232.7 18.9 %collective-permute-start.17 = (bf16[2,224,1024]{2,1,0:T(8,128)(2,1)}, bf16[2,224,1024]{2,1,0:T(8,128)(2,1)S(1)}, u32[]{:S(2)}, u32[]{:S(2)}) collective-permute-start(bf16[2,224,1024]{2,1,0:T(8,128)(2,1)} %get-tuple-element.67.refs_2_), channel_id=1, source_target_pairs={{0,16},{8,24},{16,0},{24,8},{32,48},{40,56},{48,32},{56,40},{64,80... | collective-permute-start | bytes 2752520 | tf_op jit(solution)/shard_map/ppermute | solution.py:530
  237.0 7.4 %collective-permute-start.15 = (bf16[224,512]{1,0:T(8,128)(2,1)}, bf16[224,512]{1,0:T(8,128)(2,1)S(1)}, u32[]{:S(2)}, u32[]{:S(2)}) collective-permute-start(bf16[224,512]{1,0:T(8,128)(2,1)} %get-tuple-element.68.refs_0_), channel_id=1, source_target_pairs={{0,32},{8,40},{16,48},{24,56},{32,64},{40,72},{48,80},{56,88},{64,... | collective-permute-start | bytes 688136 | tf_op jit(solution)/shard_map/ppermute | solution.py:395
  237.0 7.4 %collective-permute-start.16 = (bf16[224,512]{1,0:T(8,128)(2,1)}, bf16[224,512]{1,0:T(8,128)(2,1)S(1)}, u32[]{:S(2)}, u32[]{:S(2)}) collective-permute-start(bf16[224,512]{1,0:T(8,128)(2,1)} %get-tuple-element.69.refs_1_), channel_id=1, source_target_pairs={{0,96},{8,104},{16,112},{24,120},{32,0},{40,8},{48,16},{56,24},{64... | collective-permute-start | bytes 688136 | tf_op jit(solution)/shard_map/ppermute | solution.py:395
  245.2 6.4 %copy-start.5 = (bf16[2,224,1024]{2,1,0:T(8,128)(2,1)S(1)}, bf16[2,224,1024]{2,1,0:T(8,128)(2,1)}, u32[]{:S(2)}) copy-start(bf16[2,224,1024]{2,1,0:T(8,128)(2,1)} %get-tuple-element.73) | copy-start | bytes 2752516
  (16 other events, 20.3 us)

commit v5 on v4

--- a/solution.py
+++ b/solution.py
@@ -30,7 +30,7 @@
 MB = 1 << 20
 
 
-def params(limit=60):
+def params(limit=63):
     return pltpu.CompilerParams(vmem_limit_bytes=limit * MB)
 
 
@@ -47,20 +47,16 @@
 def place_kernel(routes_ref, tokens_ref, picks_ref, out_ref):
     @pl.when(pl.program_id(0) == 0)
     def _():
-        routes = routes_ref[...]
-        ids = lax.broadcasted_iota(jnp.int32, (TOK, EXPERTS), 1)
-        first = (routes[:, 0:1] == ids).astype(F32).astype(BF)
-        second = (routes[:, 1:2] == ids).astype(F32).astype(BF)
+        ids = lax.broadcasted_iota(jnp.int32, (EXPERTS, TOK), 0)
+        named = [(routes_ref[k : k + 1, :] == ids).astype(F32) for k in range(TOP)]
         row = lax.broadcasted_iota(jnp.int32, (TOK, TOK), 0)
         col = lax.broadcasted_iota(jnp.int32, (TOK, TOK), 1)
         before = (row < col).astype(F32).astype(BF)
-        same = (row == col).astype(F32).astype(BF)
-        rank = lax.dot_general(first + second, before, FIRST, preferred_element_type=F32)
+        rank = jnp.dot((named[0] + named[1]).astype(BF), before, preferred_element_type=F32)
         slot = lax.broadcasted_iota(jnp.int32, (CAP, TOK), 0).astype(F32)
-        for k, named in enumerate((first, second)):
-            named_t = lax.dot_general(named, same, FIRST, preferred_element_type=F32)
+        for k in range(TOP):
             for e in range(EXPERTS):
-                hit = (slot == rank[e : e + 1, :]) & (named_t[e : e + 1, :] > 0.5)
+                hit = (slot == rank[e : e + 1, :]) & (named[k][e : e + 1, :] > 0.5)
                 picks_ref[k, e * CAP : (e + 1) * CAP, :] = hit.astype(F32).astype(BF)
 
     both = picks_ref[0] + picks_ref[1]
@@ -72,7 +68,7 @@
         place_kernel,
         grid=(NT,),
         in_specs=[
-            pl.BlockSpec((TOK, TOP), lambda i: (0, 0)),
+            pl.BlockSpec((TOP, TOK), lambda i: (0, 0)),
             pl.BlockSpec((TOK, TILE), lambda i: (0, i)),
         ],
         out_specs=[
@@ -85,7 +81,7 @@
         ],
         compiler_params=params(),
         cost_estimate=cost(2 * ROWS * TOK * D, 5 * MB),
-    )(routes, tokens)
+    )(routes.T, tokens)
 
 
 def grads_kernel(picks_ref, probs_ref, grads_ref, out_ref):
@@ -98,11 +94,9 @@
 
     @pl.when(step == NT)
     def _():
-        probs = probs_ref[...].astype(F32)
-        p0 = jnp.broadcast_to(probs[:, 0:1], (TOK, EXTRA)).astype(BF)
-        p1 = jnp.broadcast_to(probs[:, 1:2], (TOK, EXTRA)).astype(BF)
-        spread = jnp.dot(picks_ref[0], p0, preferred_element_type=F32)
-        spread = spread + jnp.dot(picks_ref[1], p1, preferred_element_type=F32)
+        held = picks_ref[0] * probs_ref[0:1, :] + picks_ref[1] * probs_ref[1:2, :]
+        ones = jnp.ones((TOK, EXTRA), BF)
+        spread = jnp.dot(held, ones, preferred_element_type=F32)
         out_ref[:, :EXTRA] = spread.astype(BF)
 
 
@@ -112,14 +106,14 @@
         grid=(NT + 1,),
         in_specs=[
             pl.BlockSpec((TOP, ROWS, TOK), lambda i: (0, 0, 0)),
-            pl.BlockSpec((TOK, TOP), lambda i: (0, 0)),
+            pl.BlockSpec((TOP, TOK), lambda i: (0, 0)),
             pl.BlockSpec((TOK, TILE), lambda i: (0, jnp.minimum(i, NT - 1))),
         ],
         out_specs=pl.BlockSpec((ROWS, TILE), lambda i: (0, i)),
         out_shape=jax.ShapeDtypeStruct((ROWS, WIDE), BF),
         compiler_params=params(),
         cost_estimate=cost(2 * ROWS * TOK * D, 5 * MB),
-    )(picks, probs, grads)
+    )(picks, probs.T, grads)
 
 
 def forward_kernel(x_ref, gate_ref, up_ref, hidden_ref, active_ref, slope_ref):
@@ -284,14 +278,11 @@
 
     @pl.when(step == NT)
     def _():
-        found = [
-            lax.dot_general(
-                picks_ref[k], rows_ref[:, :EXTRA], FIRST, preferred_element_type=F32
+        for k in range(TOP):
+            found = lax.dot_general(
+                rows_ref[:, :EXTRA], picks_ref[k], FIRST, preferred_element_type=F32
             )
-            for k in range(TOP)
-        ]
-        lane = lax.broadcasted_iota(jnp.int32, (TOK, EXTRA), 1)
-        weights_ref[...] = jnp.where(lane == 0, found[0], found[1]).astype(BF)[:, :TOP]
+            weights_ref[k : k + 1, :] = found[0:1].astype(BF)
 
 
 def combine(picks, rows, after=()):
@@ -305,11 +296,11 @@
         + [pl.BlockSpec(memory_space=pl.ANY)] * len(after),
         out_specs=[
             pl.BlockSpec((TOK, TILE), lambda i: (0, jnp.minimum(i, NT - 1))),
-            pl.BlockSpec((TOK, TOP), lambda i: (0, 0)),
+            pl.BlockSpec((TOP, TOK), lambda i: (0, 0)),
         ],
         out_shape=[
             jax.ShapeDtypeStruct((TOK, D), BF),
-            jax.ShapeDtypeStruct((TOK, TOP), BF),
+            jax.ShapeDtypeStruct((TOP, TOK), BF),
         ],
         compiler_params=params(),
         cost_estimate=LONG,
@@ -367,28 +358,33 @@
     )(place, *lefts, *rights, *after)
 
 
-def down_kernel(place_ref, left_a, left_b, right_a, right_b, *refs):
-    total = jnp.dot(left_a[0], right_a[...], preferred_element_type=F32)
-    total = total + jnp.dot(left_b[0], right_b[...], preferred_element_type=F32)
-    refs[-1][0] = total.astype(BF)
-
-
-def down_parts(place, which, lefts, rights, after=()):
-    left = pl.BlockSpec((1, SUB, ROWS), lambda i, place: (place[i], which, 0))
-    right = pl.BlockSpec((ROWS, HALF), lambda i, place: (0, i % 2))
+def down_kernel(place_ref, left_a, left_b, left_c, left_d, right_a, right_b, *refs):
+    far_ref, near_ref = refs[-2:]
+    for way, (a, b) in enumerate(((left_a, left_b), (left_c, left_d))):
+        columns = slice(way * HALF, (way + 1) * HALF)
+        total = jnp.dot(a[0], right_a[:, columns], preferred_element_type=F32)
+        total = total + jnp.dot(b[0], right_b[:, columns], preferred_element_type=F32)
+        near_ref[way] = total[:SUB].astype(BF)
+        far_ref[way] = total[SUB:].astype(BF)
+
+
+def down_parts(place, lefts, rights, after=()):
+    up = pl.BlockSpec((1, 2 * SUB, ROWS), lambda i, place: (place[2 * i], 0, 0))
+    down = pl.BlockSpec((1, 2 * SUB, ROWS), lambda i, place: (place[2 * i + 1], 0, 0))
+    right = pl.BlockSpec((ROWS, FF), lambda i, place: (0, 0))
     return pl.pallas_call(
         down_kernel,
         grid_spec=pltpu.PrefetchScalarGridSpec(
             num_scalar_prefetch=1,
-            grid=(2 * NZ,),
-            in_specs=[left, left, right, right]
+            grid=(NZ,),
+            in_specs=[up, up, down, down, right, right]
             + [pl.BlockSpec(memory_space=pl.ANY)] * len(after),
-            out_specs=pl.BlockSpec((1, SUB, HALF), lambda i, place: (i, 0, 0)),
+            out_specs=[pl.BlockSpec((2, SUB, HALF), lambda i, place: (i, 0, 0))] * 2,
         ),
-        out_shape=jax.ShapeDtypeStruct((2 * NZ, SUB, HALF), BF),
-        compiler_params=params(),
-        cost_estimate=cost(16 * SUB * ROWS * FF, 8 * MB),
-    )(place, *lefts, *rights, *after)
+        out_shape=[jax.ShapeDtypeStruct((2 * NZ, SUB, HALF), BF)] * 2,
+        compiler_params=params(),
+        cost_estimate=PRODUCT,
+    )(place, *lefts, *lefts, *rights, *after)
 
 
 def around(up, down):
@@ -509,11 +505,10 @@
     dlefts = turned(place, row_grads_in, row_grads_in, True, after=(both,))
     ring0 = wide_parts(place, 0, lefts, boths, after=dlefts[:1])
     moved0 = around(*ring0)
-    far = down_parts(place, 1, dlefts, hiddens, after=ring0[:1])
+    far, near = down_parts(place, dlefts, hiddens, after=ring0[:1])
     far_in = lax.ppermute(far, "dp", TO_X)
     parts1 = wide_parts(place, 1, lefts, boths, after=(far,))
-    near = down_parts(place, 0, dlefts, hiddens, after=parts1[:1])
-    ring1 = wide_add(parts1, moved0, after=(near,))
+    ring1 = wide_add(parts1, moved0)
     moved1 = around(*ring1)
     sent_rows = row_grads(both, gate, up, wg, after=ring1)
     returned = exchange(sent_rows)
@@ -536,7 +531,7 @@
     grad_gate = add(mine[0], came[0])[None]
     grad_up = add(mine[1], came[1])[None]
     grad_down = down_grad[None]
-    return (grad_tokens, grad_weights, grad_gate, grad_up, grad_down)
+    return (grad_tokens, grad_weights.T, grad_gate, grad_up, grad_down)
 
 
 def solution(mesh):

time: 254 us -> 246 us (0.969)
  Pallas kernels: 122 us -> 112 us
  local copies, waits for them, and re-layouts: 14.3 us -> 4.76 us
  waiting for transfers between devices: 75.8 us -> 84.5 us
    pallas_call x2 -> x1, Pallas kernels: 19 us -> 9.08 us  [down_parts(): pl.pallas_call(down_kernel, grid_spec=pltpu.PrefetchScalarGridSpec(num_sc...]
    unnamed x41 -> x14, local copies, waits for them, and re-layouts: 13.8 us -> 4.17 us
    ppermute x1, waiting for transfers between devices: 0.01 us -> 3 us  [local(): far_in = lax.ppermute(far, 'dp', TO_X)]
    ppermute x1, waiting for transfers between devices: 3.48 us -> 6.25 us  [local(): came = lax.ppermute(away, 'dp', TO_X)]
  transfers between devices with their start and end apart: 21 -> 21, of which waited for: 5 -> 7; matrix products, arithmetic and copies ran while one was open for 1% -> 0% of each run, Pallas kernels for 43% -> 40%
where the time goes in v5:
time: 246 us; the launch traced here: 245 us
  Pallas kernels  112 us (46%)
  waiting for transfers between devices  84.5 us (34%)
  starting transfers between devices  40.3 us (16%)
  local copies, waits for them, and re-layouts  4.76 us (2%)
    all_to_all x3, waiting for transfers between devices, exchange(): lax.all_to_all(rows.reshape(EXPERTS, CAP, width), 'expert', split_axis=0,...  64.2 us
    pallas_call x4, Pallas kernels, wide_parts(): pl.pallas_call(wide_kernel, grid_spec=pltpu.PrefetchScalarGridSpec(num_sc...  25 us
    ppermute x12, starting transfers between devices, around(): return (lax.ppermute(up, 'dp', TO_UP), lax.ppermute(down, 'dp', TO_DOWN))  19.1 us
    all_to_all x3, starting transfers between devices, exchange(): lax.all_to_all(rows.reshape(EXPERTS, CAP, width), 'expert', split_axis=0,...  14.6 us
    pallas_call x1, Pallas kernels, forward(): pl.pallas_call(forward_kernel, grid=(FF // n,), in_specs=[pl.BlockSpec((R...  13.3 us
    pallas_call x1, Pallas kernels, row_grads(): pl.pallas_call(rows_kernel, grid=(NT + 1,), in_specs=[pl.BlockSpec((2, RO...  13.1 us
    pallas_call x2, Pallas kernels, turned(): pl.pallas_call(functools.partial(turned_kernel, scaled, len(after)), grid...  11.6 us
    ppermute x12, waiting for transfers between devices, around(): return (lax.ppermute(up, 'dp', TO_UP), lax.ppermute(down, 'dp', TO_DOWN))  11.1 us
  transfers between devices with their start and end apart: 21, of which 7 were waited for; matrix products, arithmetic and copies ran while one was open for 0% of the time, Pallas kernels for 40%

profile of v5, /device:TPU:0, one launch (start us, length us, event | category | flops | bytes accessed | tf_op | source)
XLA Modules:
  0.0 245.0 jit_solution(16632324050612171911)
XLA Ops:
  0.6 3.8 %shard_map.119 = (bf16[2,512,128]{2,1,0:T(8,128)(2,1)}, bf16[512,3584]{1,0:T(8,128)(2,1)}) custom-call(s32[2,128]{1,0:T(2,128)} %bitcast.23, bf16[128,3584]{1,0:T(8,128)(2,1)} %tokens_ref.1), custom_call_target="tpu_custom_call" | custom-call | flops 469762048 | bytes 5242880 | tf_op jit(solution)/shard_map/pallas_call | solution.py:67
  4.5 5.5 %all-to-all-start.1 = ((bf16[8,64,3584]{2,1,0:T(8,128)(2,1)}), bf16[8,64,3584]{2,1,0:T(8,128)(2,1)}, u32[]{:S(2)}, u32[]{:S(2)}) async-start(bf16[8,64,3584]{2,1,0:T(8,128)(2,1)} %bitcast.20), calls=%async_computation.1 | async-start | bytes 7340032 | tf_op jit(solution)/shard_map/all_to_all | solution.py:485
  9.9 3.9 %shard_map.120 = bf16[512,3712]{1,0:T(8,128)(2,1)} custom-call(bf16[2,512,128]{2,1,0:T(8,128)(2,1)} %get-tuple-element.42.picks_ref, bf16[2,128]{1,0:T(2,128)(2,1)} %bitcast.22, bf16[128,3584]{1,0:T(8,128)(2,1)} %grads_ref.1), custom_call_target="tpu_custom_call" | custom-call | flops 469762048 | bytes 5242880 | tf_op jit(solution)/shard_map/pallas_call | solution.py:104
  13.9 40.0 %all-to-all-done.1 = bf16[8,64,3584]{2,1,0:T(8,128)(2,1)} async-done(((bf16[8,64,3584]{2,1,0:T(8,128)(2,1)}), bf16[8,64,3584]{2,1,0:T(8,128)(2,1)}, u32[]{:S(2)}, u32[]{:S(2)}) %all-to-all-start.1) | async-done | bytes 3670048 | tf_op jit(solution)/shard_map/all_to_all | solution.py:485
  53.9 4.6 %all-to-all-start = ((bf16[8,64,3712]{2,1,0:T(8,128)(2,1)}), bf16[8,64,3712]{2,1,0:T(8,128)(2,1)}, u32[]{:S(2)}, u32[]{:S(2)}) async-start(bf16[8,64,3712]{2,1,0:T(8,128)(2,1)} %bitcast.13), calls=%async_computation | async-start | bytes 7602176 | tf_op jit(solution)/shard_map/all_to_all | solution.py:485
  59.1 13.3 %shard_map.121 = (bf16[512,1024]{1,0:T(8,128)(2,1)}, f32[512,1024]{1,0:T(8,128)}, f32[512,1024]{1,0:T(8,128)}) custom-call(bf16[512,3584]{1,0:T(8,128)(2,1)} %bitcast.6.x_ref.p_ref, bf16[3584,1024]{1,0:T(8,128)(2,1)} %bitcast.16, bf16[3584,1024]{1,0:T(8,128)(2,1)} %bitcast.18), custom_call_target="tpu_custom_call" | custom-call | flops 7516192768 | bytes 24117248 | tf_op jit(solution)/shard_map/pallas_call | solution.py:132
  72.5 5.7 %shard_map.122 = (bf16[4,448,512]{2,1,0:T(8,128)(2,1)}, bf16[4,448,512]{2,1,0:T(8,128)(2,1)}) custom-call(s32[10]{0:T(128)} %dynamic_slice.3.place_ref, bf16[512,3584]{1,0:T(8,128)(2,1)} %bitcast.6.x_ref.p_ref, bf16[512,3584]{1,0:T(8,128)(2,1)} %bitcast.6.x_ref.p_ref, bf16[512,1024]{1,0:T(8,128)(2,1)} %get-tuple-element.44.refs_0_.hidden_ref.right_a), custom_call_target="tpu_custom_call" | custom-call | flops 1835008 | bytes 8388608 | tf_op jit(solution)/shard_map/pallas_call | solution.py:248
  78.7 24.2 %all-to-all-done = bf16[8,64,3712]{2,1,0:T(8,128)(2,1)} async-done(((bf16[8,64,3712]{2,1,0:T(8,128)(2,1)}), bf16[8,64,3712]{2,1,0:T(8,128)(2,1)}, u32[]{:S(2)}, u32[]{:S(2)}) %all-to-all-start) | async-done | bytes 3801120 | tf_op jit(solution)/shard_map/all_to_all | solution.py:485
  102.9 10.0 %shard_map.123 = (bf16[2,512,1024]{2,1,0:T(8,128)(2,1)}, bf16[512,128]{1,0:T(8,128)(2,1)}) custom-call(bf16[512,3712]{1,0:T(8,128)(2,1)} %bitcast.3.g_ref.x_ref.p_ref, bf16[3584,1024]{1,0:T(8,128)(2,1)} %bitcast.15, bf16[512,1024]{1,0:T(8,128)(2,1)} %get-tuple-element.44.refs_0_.hidden_ref.right_a, f32[512,1024]{1,0:T(8,128)} %get-tuple-element.45.active_ref, ...), custom_call_target="tpu_custom_call" | custom-call | flops 3758096384 | bytes 18874368 | tf_op jit(solution)/shard_map/pallas_call | solution.py:171
  112.8 5.9 %shard_map.124 = (bf16[4,448,512]{2,1,0:T(8,128)(2,1)}, bf16[4,448,512]{2,1,0:T(8,128)(2,1)}) custom-call(s32[10]{0:T(128)} %dynamic_slice.3.place_ref, bf16[512,3712]{1,0:T(8,128)(2,1)} %bitcast.3.g_ref.x_ref.p_ref, bf16[512,3712]{1,0:T(8,128)(2,1)} %bitcast.3.g_ref.x_ref.p_ref, bf16[2,512,1024]{2,1,0:T(8,128)(2,1)} %get-tuple-element.49.refs_0_.right_a.both_ref), custom_call_target="tpu_custom_call" | custom-call | flops 1835008 | bytes 8388608 | tf_op jit(solution)/shard_map/pallas_call | solution.py:248
  119.3 6.2 %shard_map.125 = (bf16[448,1024]{1,0:T(8,128)(2,1)}, bf16[448,1024]{1,0:T(8,128)(2,1)}) custom-call(s32[10]{0:T(128)} %dynamic_slice.3.place_ref, bf16[4,448,512]{2,1,0:T(8,128)(2,1)} %get-tuple-element.47.refs_0_.left_a, bf16[4,448,512]{2,1,0:T(8,128)(2,1)} %collective-permute-done.refs_1_.left_b, ...), custom_call_target="tpu_custom_call" | custom-call | flops 1879048192 | bytes 8388608 | tf_op jit(solution)/shard_map/pallas_call | solution.py:346
  129.6 9.1 %shard_map.126 = (bf16[8,224,512]{2,1,0:T(8,128)(2,1)}, bf16[8,224,512]{2,1,0:T(8,128)(2,1)}) custom-call(s32[10]{0:T(128)} %dynamic_slice.3.place_ref, bf16[4,448,512]{2,1,0:T(8,128)(2,1)} %get-tuple-element.51.refs_0_.left_a.left_c, bf16[4,448,512]{2,1,0:T(8,128)(2,1)} %collective-permute-done.3.left_b.left_d, ...), custom_call_target="tpu_custom_call" | custom-call | flops 1879048192 | bytes 8388608 | tf_op jit(solution)/shard_map/pallas_call | solution.py:375
  141.4 6.3 %shard_map.127 = (bf16[448,1024]{1,0:T(8,128)(2,1)}, bf16[448,1024]{1,0:T(8,128)(2,1)}) custom-call(s32[10]{0:T(128)} %dynamic_slice.3.place_ref, bf16[4,448,512]{2,1,0:T(8,128)(2,1)} %get-tuple-element.47.refs_0_.left_a, bf16[4,448,512]{2,1,0:T(8,128)(2,1)} %collective-permute-done.refs_1_.left_b, ...), custom_call_target="tpu_custom_call" | custom-call | flops 1879048192 | bytes 8388608 | tf_op jit(solution)/shard_map/pallas_call | solution.py:346
  156.5 13.1 %shard_map.129.refs_0_ = bf16[512,3712]{1,0:T(8,128)(2,1)} custom-call(bf16[2,512,1024]{2,1,0:T(8,128)(2,1)} %get-tuple-element.49.refs_0_.right_a.both_ref, bf16[3584,1024]{1,0:T(8,128)(2,1)} %bitcast.17, bf16[3584,1024]{1,0:T(8,128)(2,1)} %bitcast.19, bf16[512,128]{1,0:T(8,128)(2,1)} %get-tuple-element.50.wg_ref, ...), custom_call_target="tpu_custom_call" | custom-call | flops 1 | bytes 1 | tf_op jit(solution)/shard_map/pallas_call | solution.py:213
  169.6 4.5 %all-to-all-start.2 = ((bf16[8,64,3712]{2,1,0:T(8,128)(2,1)}), bf16[8,64,3712]{2,1,0:T(8,128)(2,1)}, u32[]{:S(2)}, u32[]{:S(2)}) async-start(bf16[8,64,3712]{2,1,0:T(8,128)(2,1)} %bitcast.14), calls=%async_computation.2 | async-start | bytes 7602176 | tf_op jit(solution)/shard_map/all_to_all | solution.py:485
  174.1 6.3 %shard_map.130 = (bf16[448,1024]{1,0:T(8,128)(2,1)}, bf16[448,1024]{1,0:T(8,128)(2,1)}) custom-call(s32[10]{0:T(128)} %dynamic_slice.3.place_ref, bf16[4,448,512]{2,1,0:T(8,128)(2,1)} %get-tuple-element.47.refs_0_.left_a, bf16[4,448,512]{2,1,0:T(8,128)(2,1)} %collective-permute-done.refs_1_.left_b, ...), custom_call_target="tpu_custom_call" | custom-call | flops 14000000000 | bytes 1 | tf_op jit(solution)/shard_map/pallas_call | solution.py:346
  185.4 3.2 %collective-permute-start.8 = (bf16[224,512]{1,0:T(8,128)(2,1)}, bf16[224,512]{1,0:T(8,128)(2,1)}, u32[]{:S(2)}, u32[]{:S(2)}) collective-permute-start(bf16[224,512]{1,0:T(8,128)(2,1)} %get-tuple-element.63.refs_1_), channel_id=1, source_target_pairs={{0,96},{8,104},{16,112},{24,120},{32,0},{40,8},{48,16},{56,24},{64... | collective-permute-start | bytes 688136 | tf_op jit(solution)/shard_map/ppermute | solution.py:391
  192.6 3.2 %collective-permute-start.14 = (bf16[448,1024]{1,0:T(8,128)(2,1)}, bf16[448,1024]{1,0:T(8,128)(2,1)}, u32[]{:S(2)}, u32[]{:S(2)}) collective-permute-start(bf16[448,1024]{1,0:T(8,128)(2,1)} %get-tuple-element.66.refs_1_), channel_id=1, source_target_pairs={{0,96},{8,104},{16,112},{24,120},{32,0},{40,8},{48,16},{56,24},{64... | collective-permute-start | bytes 2752520 | tf_op jit(solution)/shard_map/ppermute | solution.py:391
  195.9 6.2 %shard_map.133 = (bf16[448,1024]{1,0:T(8,128)(2,1)}, bf16[448,1024]{1,0:T(8,128)(2,1)}) custom-call(s32[10]{0:T(128)} %dynamic_slice.3.place_ref, bf16[4,448,512]{2,1,0:T(8,128)(2,1)} %get-tuple-element.47.refs_0_.left_a, bf16[4,448,512]{2,1,0:T(8,128)(2,1)} %collective-permute-done.refs_1_.left_b, ...), custom_call_target="tpu_custom_call" | custom-call | flops 1 | bytes 1 | tf_op jit(solution)/shard_map/pallas_call | solution.py:346
  204.2 3.2 %collective-permute-start.12 = (bf16[224,512]{1,0:T(8,128)(2,1)}, bf16[224,512]{1,0:T(8,128)(2,1)}, u32[]{:S(2)}, u32[]{:S(2)}) collective-permute-start(bf16[224,512]{1,0:T(8,128)(2,1)} %get-tuple-element.69.refs_1_), channel_id=1, source_target_pairs={{0,96},{8,104},{16,112},{24,120},{32,0},{40,8},{48,16},{56,24},{64... | collective-permute-start | bytes 688136 | tf_op jit(solution)/shard_map/ppermute | solution.py:391
  207.5 8.3 %collective-permute-done.13.up_ref = bf16[448,1024]{1,0:T(8,128)(2,1)S(1)} collective-permute-done((bf16[448,1024]{1,0:T(8,128)(2,1)}, bf16[448,1024]{1,0:T(8,128)(2,1)S(1)}, u32[]{:S(2)}, u32[]{:S(2)}) %collective-permute-start.13) | collective-permute-done | bytes 917536 | tf_op jit(solution)/shard_map/ppermute | solution.py:391
  216.7 3.6 %shard_map.135 = (bf16[2,224,1024]{2,1,0:T(8,128)(2,1)}, bf16[2,224,1024]{2,1,0:T(8,128)(2,1)}) custom-call(bf16[448,1024]{1,0:T(8,128)(2,1)} %get-tuple-element.67.refs_2_.part_up, bf16[448,1024]{1,0:T(8,128)(2,1)} %get-tuple-element.70.part_down, bf16[448,1024]{1,0:T(8,128)(2,1)} %copy-done.2, bf16[448,1024]{1,0:T(8,128)(2,1)} %collective-permute-done.14.down_ref, ...), custom_call_target="tpu_custom_call" | custom-call | flops 1 | bytes 1 | tf_op jit(solution)/shard_map/pallas_call | solution.py:429
  228.5 4.1 %shard_map.137 = (bf16[128,3584]{1,0:T(8,128)(2,1)}, bf16[2,128]{1,0:T(2,128)(2,1)}) custom-call(bf16[2,512,128]{2,1,0:T(8,128)(2,1)} %get-tuple-element.42.picks_ref, bf16[512,3712]{1,0:T(8,128)(2,1)} %bitcast.10.rows_ref, bf16[224,512]{1,0:T(8,128)(2,1)} %get-tuple-element.72.refs_0_, bf16[224,512]{1,0:T(8,128)(2,1)} %get-tuple-element.73.refs_1_), custom_call_target="tpu_custom_call" | custom-call | flops 24999999488 | bytes 1 | tf_op jit(solution)/shard_map/pallas_call | solution.py:289
  236.3 6.2 %collective-permute-done.17 = bf16[2,224,1024]{2,1,0:T(8,128)(2,1)} collective-permute-done((bf16[2,224,1024]{2,1,0:T(8,128)(2,1)}, bf16[2,224,1024]{2,1,0:T(8,128)(2,1)}, u32[]{:S(2)}, u32[]{:S(2)}) %collective-permute-start.17) | collective-permute-done | bytes 917536 | tf_op jit(solution)/shard_map/ppermute | solution.py:525
  (54 shorter events, 43.6 us)
Async XLA Ops:
  4.5 49.4 %all-to-all-start.1 = ((bf16[8,64,3584]{2,1,0:T(8,128)(2,1)}), bf16[8,64,3584]{2,1,0:T(8,128)(2,1)}, u32[]{:S(2)}, u32[]{:S(2)}) async-start(bf16[8,64,3584]{2,1,0:T(8,128)(2,1)} %bitcast.20), calls=%async_computation.1 | async-start | bytes 7340032 | tf_op jit(solution)/shard_map/all_to_all | solution.py:485
  53.9 4.7 %copy-start.6 = (s32[160]{0:T(256)S(1)}, s32[160]{0:T(256)}, u32[]{:S(2)}) copy-start(s32[160]{0:T(256)} %constant.14.clone) | copy-start | bytes 1924
  53.9 49.0 %all-to-all-start = ((bf16[8,64,3712]{2,1,0:T(8,128)(2,1)}), bf16[8,64,3712]{2,1,0:T(8,128)(2,1)}, u32[]{:S(2)}, u32[]{:S(2)}) async-start(bf16[8,64,3712]{2,1,0:T(8,128)(2,1)} %bitcast.13), calls=%async_computation | async-start | bytes 7602176 | tf_op jit(solution)/shard_map/all_to_all | solution.py:485
  78.2 24.7 %collective-permute-start = (bf16[4,448,512]{2,1,0:T(8,128)(2,1)}, bf16[4,448,512]{2,1,0:T(8,128)(2,1)}, u32[]{:S(2)}, u32[]{:S(2)}) collective-permute-start(bf16[4,448,512]{2,1,0:T(8,128)(2,1)} %get-tuple-element.48), channel_id=1, source_target_pairs={{0,8},{8,0},{16,24},{24,16},{32,40},{40,32},{48,56},{56,48},{64,72... | collective-permute-start | bytes 5505032 | tf_op jit(solution)/shard_map/ppermute | solution.py:265
  78.2 24.7 %collective-permute-start.1 = (bf16[512,1024]{1,0:T(8,128)(2,1)}, bf16[512,1024]{1,0:T(8,128)(2,1)}, u32[]{:S(2)}, u32[]{:S(2)}) collective-permute-start(bf16[512,1024]{1,0:T(8,128)(2,1)} %get-tuple-element.44.refs_0_.hidden_ref.right_a), channel_id=1, source_target_pairs={{0,8},{8,0},{16,24},{24,16},{32,40},{40,32},{48,56},{56,48},{64,72... | collective-permute-start | bytes 3145736 | tf_op jit(solution)/shard_map/ppermute | solution.py:500
  112.8 6.4 %collective-permute-start.2 = (bf16[2,512,1024]{2,1,0:T(8,128)(2,1)}, bf16[2,512,1024]{2,1,0:T(8,128)(2,1)}, u32[]{:S(2)}, u32[]{:S(2)}) collective-permute-start(bf16[2,512,1024]{2,1,0:T(8,128)(2,1)} %get-tuple-element.49.refs_0_.right_a.both_ref), channel_id=1, source_target_pairs={{0,8},{8,0},{16,24},{24,16},{32,40},{40,32},{48,56},{56,48},{64,72... | collective-permute-start | bytes 6291464 | tf_op jit(solution)/shard_map/ppermute | solution.py:504
  118.8 10.8 %collective-permute-start.3 = (bf16[4,448,512]{2,1,0:T(8,128)(2,1)}, bf16[4,448,512]{2,1,0:T(8,128)(2,1)}, u32[]{:S(2)}, u32[]{:S(2)}) collective-permute-start(bf16[4,448,512]{2,1,0:T(8,128)(2,1)} %get-tuple-element.52), channel_id=1, source_target_pairs={{0,8},{8,0},{16,24},{24,16},{32,40},{40,32},{48,56},{56,48},{64,72... | collective-permute-start | bytes 5505032 | tf_op jit(solution)/shard_map/ppermute | solution.py:265
  125.5 24.8 %collective-permute-start.4 = (bf16[448,1024]{1,0:T(8,128)(2,1)}, bf16[448,1024]{1,0:T(8,128)(2,1)S(1)}, u32[]{:S(2)}, u32[]{:S(2)}) collective-permute-start(bf16[448,1024]{1,0:T(8,128)(2,1)} %get-tuple-element.53.refs_0_), channel_id=1, source_target_pairs={{0,32},{8,40},{16,48},{24,56},{32,64},{40,72},{48,80},{56,88},{64,... | collective-permute-start | bytes 2752520 | tf_op jit(solution)/shard_map/ppermute | solution.py:391
  127.4 22.9 %collective-permute-start.5 = (bf16[448,1024]{1,0:T(8,128)(2,1)}, bf16[448,1024]{1,0:T(8,128)(2,1)}, u32[]{:S(2)}, u32[]{:S(2)}) collective-permute-start(bf16[448,1024]{1,0:T(8,128)(2,1)} %get-tuple-element.57), channel_id=1, source_target_pairs={{0,96},{8,104},{16,112},{24,120},{32,0},{40,8},{48,16},{56,24},{64... | collective-permute-start | bytes 2752520 | tf_op jit(solution)/shard_map/ppermute | solution.py:391
  138.6 44.7 %collective-permute-start.6 = (bf16[8,224,512]{2,1,0:T(8,128)(2,1)}, bf16[8,224,512]{2,1,0:T(8,128)(2,1)}, u32[]{:S(2)}, u32[]{:S(2)}) collective-permute-start(bf16[8,224,512]{2,1,0:T(8,128)(2,1)} %get-tuple-element.54.refs_0_), channel_id=1, source_target_pairs={{0,16},{8,24},{16,0},{24,8},{32,48},{40,56},{48,32},{56,40},{64,80... | collective-permute-start | bytes 5505032 | tf_op jit(solution)/shard_map/ppermute | solution.py:509
  154.3 34.3 %collective-permute-start.10 = (bf16[448,1024]{1,0:T(8,128)(2,1)}, bf16[448,1024]{1,0:T(8,128)(2,1)S(1)}, u32[]{:S(2)}, u32[]{:S(2)}) collective-permute-start(bf16[448,1024]{1,0:T(8,128)(2,1)} %get-tuple-element.59.refs_1_), channel_id=1, source_target_pairs={{0,96},{8,104},{16,112},{24,120},{32,0},{40,8},{48,16},{56,24},{64... | collective-permute-start | bytes 2752520 | tf_op jit(solution)/shard_map/ppermute | solution.py:391
  156.5 32.1 %collective-permute-start.9 = (bf16[448,1024]{1,0:T(8,128)(2,1)}, bf16[448,1024]{1,0:T(8,128)(2,1)}, u32[]{:S(2)}, u32[]{:S(2)}) collective-permute-start(bf16[448,1024]{1,0:T(8,128)(2,1)} %get-tuple-element.58.refs_0_), channel_id=1, source_target_pairs={{0,32},{8,40},{16,48},{24,56},{32,64},{40,72},{48,80},{56,88},{64,... | collective-permute-start | bytes 2752520 | tf_op jit(solution)/shard_map/ppermute | solution.py:391
  169.6 58.9 %all-to-all-start.2 = ((bf16[8,64,3712]{2,1,0:T(8,128)(2,1)}), bf16[8,64,3712]{2,1,0:T(8,128)(2,1)}, u32[]{:S(2)}, u32[]{:S(2)}) async-start(bf16[8,64,3712]{2,1,0:T(8,128)(2,1)} %bitcast.14), calls=%async_computation.2 | async-start | bytes 7602176 | tf_op jit(solution)/shard_map/all_to_all | solution.py:485
  185.4 16.7 %collective-permute-start.7 = (bf16[224,512]{1,0:T(8,128)(2,1)}, bf16[224,512]{1,0:T(8,128)(2,1)}, u32[]{:S(2)}, u32[]{:S(2)}) collective-permute-start(bf16[224,512]{1,0:T(8,128)(2,1)} %get-tuple-element.62.refs_0_), channel_id=1, source_target_pairs={{0,32},{8,40},{16,48},{24,56},{32,64},{40,72},{48,80},{56,88},{64,... | collective-permute-start | bytes 688136 | tf_op jit(solution)/shard_map/ppermute | solution.py:391
  185.4 16.7 %collective-permute-start.8 = (bf16[224,512]{1,0:T(8,128)(2,1)}, bf16[224,512]{1,0:T(8,128)(2,1)}, u32[]{:S(2)}, u32[]{:S(2)}) collective-permute-start(bf16[224,512]{1,0:T(8,128)(2,1)} %get-tuple-element.63.refs_1_), channel_id=1, source_target_pairs={{0,96},{8,104},{16,112},{24,120},{32,0},{40,8},{48,16},{56,24},{64... | collective-permute-start | bytes 688136 | tf_op jit(solution)/shard_map/ppermute | solution.py:391
  188.6 0.9 copy-start.3
  192.6 23.1 %collective-permute-start.13 = (bf16[448,1024]{1,0:T(8,128)(2,1)}, bf16[448,1024]{1,0:T(8,128)(2,1)S(1)}, u32[]{:S(2)}, u32[]{:S(2)}) collective-permute-start(bf16[448,1024]{1,0:T(8,128)(2,1)} %get-tuple-element.65.refs_0_), channel_id=1, source_target_pairs={{0,32},{8,40},{16,48},{24,56},{32,64},{40,72},{48,80},{56,88},{64,... | collective-permute-start | bytes 2752520 | tf_op jit(solution)/shard_map/ppermute | solution.py:391
  192.6 23.1 %collective-permute-start.14 = (bf16[448,1024]{1,0:T(8,128)(2,1)}, bf16[448,1024]{1,0:T(8,128)(2,1)}, u32[]{:S(2)}, u32[]{:S(2)}) collective-permute-start(bf16[448,1024]{1,0:T(8,128)(2,1)} %get-tuple-element.66.refs_1_), channel_id=1, source_target_pairs={{0,96},{8,104},{16,112},{24,120},{32,0},{40,8},{48,16},{56,24},{64... | collective-permute-start | bytes 2752520 | tf_op jit(solution)/shard_map/ppermute | solution.py:391
  204.2 18.8 %collective-permute-start.11 = (bf16[224,512]{1,0:T(8,128)(2,1)}, bf16[224,512]{1,0:T(8,128)(2,1)}, u32[]{:S(2)}, u32[]{:S(2)}) collective-permute-start(bf16[224,512]{1,0:T(8,128)(2,1)} %get-tuple-element.68.refs_0_), channel_id=1, source_target_pairs={{0,32},{8,40},{16,48},{24,56},{32,64},{40,72},{48,80},{56,88},{64,... | collective-permute-start | bytes 688136 | tf_op jit(solution)/shard_map/ppermute | solution.py:391
  204.2 18.8 %collective-permute-start.12 = (bf16[224,512]{1,0:T(8,128)(2,1)}, bf16[224,512]{1,0:T(8,128)(2,1)}, u32[]{:S(2)}, u32[]{:S(2)}) collective-permute-start(bf16[224,512]{1,0:T(8,128)(2,1)} %get-tuple-element.69.refs_1_), channel_id=1, source_target_pairs={{0,96},{8,104},{16,112},{24,120},{32,0},{40,8},{48,16},{56,24},{64... | collective-permute-start | bytes 688136 | tf_op jit(solution)/shard_map/ppermute | solution.py:391
  220.3 22.3 %collective-permute-start.17 = (bf16[2,224,1024]{2,1,0:T(8,128)(2,1)}, bf16[2,224,1024]{2,1,0:T(8,128)(2,1)}, u32[]{:S(2)}, u32[]{:S(2)}) collective-permute-start(bf16[2,224,1024]{2,1,0:T(8,128)(2,1)} %get-tuple-element.71.refs_2_), channel_id=1, source_target_pairs={{0,16},{8,24},{16,0},{24,8},{32,48},{40,56},{48,32},{56,40},{64,80... | collective-permute-start | bytes 2752520 | tf_op jit(solution)/shard_map/ppermute | solution.py:525
  225.2 7.4 %collective-permute-start.15 = (bf16[224,512]{1,0:T(8,128)(2,1)}, bf16[224,512]{1,0:T(8,128)(2,1)S(1)}, u32[]{:S(2)}, u32[]{:S(2)}) collective-permute-start(bf16[224,512]{1,0:T(8,128)(2,1)} %get-tuple-element.72.refs_0_), channel_id=1, source_target_pairs={{0,32},{8,40},{16,48},{24,56},{32,64},{40,72},{48,80},{56,88},{64,... | collective-permute-start | bytes 688136 | tf_op jit(solution)/shard_map/ppermute | solution.py:391
  225.2 7.4 %collective-permute-start.16 = (bf16[224,512]{1,0:T(8,128)(2,1)}, bf16[224,512]{1,0:T(8,128)(2,1)S(1)}, u32[]{:S(2)}, u32[]{:S(2)}) collective-permute-start(bf16[224,512]{1,0:T(8,128)(2,1)} %get-tuple-element.73.refs_1_), channel_id=1, source_target_pairs={{0,96},{8,104},{16,112},{24,120},{32,0},{40,8},{48,16},{56,24},{64... | collective-permute-start | bytes 688136 | tf_op jit(solution)/shard_map/ppermute | solution.py:391
  234.0 8.5 %copy-start.1 = (bf16[2,224,1024]{2,1,0:T(8,128)(2,1)S(1)}, bf16[2,224,1024]{2,1,0:T(8,128)(2,1)}, u32[]{:S(2)}) copy-start(bf16[2,224,1024]{2,1,0:T(8,128)(2,1)} %get-tuple-element.77) | copy-start | bytes 2752516
  (4 other events, 3.2 us)

commit v6 on v5

--- a/solution.py
+++ b/solution.py
@@ -39,9 +39,10 @@
 
 
 SHORT = cost(1, 1)
-LONG = cost(25_000_000_000, 1)
+LONG = cost(40_000_000_000, 1)
 PRODUCT = cost(16 * SUB * ROWS * FF, 8 * MB)
-WIDE_COSTS = (PRODUCT, PRODUCT, cost(14_000_000_000, 1), SHORT)
+WIDE_COSTS = (PRODUCT, PRODUCT, cost(25_000_000_000, 1), SHORT)
+SUMS = cost(10_000_000_000, 1)
 
 
 def place_kernel(routes_ref, tokens_ref, picks_ref, out_ref):
@@ -303,7 +304,7 @@
             jax.ShapeDtypeStruct((TOP, TOK), BF),
         ],
         compiler_params=params(),
-        cost_estimate=LONG,
+        cost_estimate=SHORT,
     )(picks, rows, *after)
 
 
@@ -320,6 +321,7 @@
 TO_CORE = moves(lambda z, x, c: (z, x, 1 - c))
 TO_UP = moves(lambda z, x, c: (z + 1, x, c))
 TO_DOWN = moves(lambda z, x, c: (z - 1, x, c))
+TO_TWO = moves(lambda z, x, c: (z + 2, x, c))
 TO_X = moves(lambda z, x, c: (z, 1 - x, c))
 
 
@@ -358,33 +360,30 @@
     )(place, *lefts, *rights, *after)
 
 
-def down_kernel(place_ref, left_a, left_b, left_c, left_d, right_a, right_b, *refs):
+def down_kernel(place_ref, left_a, left_b, right_a, right_b, *refs):
     far_ref, near_ref = refs[-2:]
-    for way, (a, b) in enumerate(((left_a, left_b), (left_c, left_d))):
-        columns = slice(way * HALF, (way + 1) * HALF)
-        total = jnp.dot(a[0], right_a[:, columns], preferred_element_type=F32)
-        total = total + jnp.dot(b[0], right_b[:, columns], preferred_element_type=F32)
-        near_ref[way] = total[:SUB].astype(BF)
-        far_ref[way] = total[SUB:].astype(BF)
+    total = jnp.dot(left_a[0], right_a[...], preferred_element_type=F32)
+    total = total + jnp.dot(left_b[0], right_b[...], preferred_element_type=F32)
+    near_ref[0] = total[:SUB].astype(BF)
+    far_ref[0] = total[SUB:].astype(BF)
 
 
 def down_parts(place, lefts, rights, after=()):
-    up = pl.BlockSpec((1, 2 * SUB, ROWS), lambda i, place: (place[2 * i], 0, 0))
-    down = pl.BlockSpec((1, 2 * SUB, ROWS), lambda i, place: (place[2 * i + 1], 0, 0))
+    left = pl.BlockSpec((1, 2 * SUB, ROWS), lambda i, place: (place[i + 3 * (i // 3)], 0, 0))
     right = pl.BlockSpec((ROWS, FF), lambda i, place: (0, 0))
     return pl.pallas_call(
         down_kernel,
         grid_spec=pltpu.PrefetchScalarGridSpec(
             num_scalar_prefetch=1,
             grid=(NZ,),
-            in_specs=[up, up, down, down, right, right]
+            in_specs=[left, left, right, right]
             + [pl.BlockSpec(memory_space=pl.ANY)] * len(after),
-            out_specs=[pl.BlockSpec((2, SUB, HALF), lambda i, place: (i, 0, 0))] * 2,
+            out_specs=[pl.BlockSpec((1, SUB, FF), lambda i, place: (i, 0, 0))] * 2,
         ),
-        out_shape=[jax.ShapeDtypeStruct((2 * NZ, SUB, HALF), BF)] * 2,
+        out_shape=[jax.ShapeDtypeStruct((NZ, SUB, FF), BF)] * 2,
         compiler_params=params(),
         cost_estimate=PRODUCT,
-    )(place, *lefts, *lefts, *rights, *after)
+    )(place, *lefts, *rights, *after)
 
 
 def around(up, down):
@@ -437,36 +436,44 @@
     )(*parts, *moved, *after)
 
 
-def down_add_kernel(moved, near_ref, far_ref, *refs):
-    sums = [near_ref[k].astype(F32) + far_ref[k].astype(F32) for k in range(2)]
-    if moved:
-        sums = [a + ref[...].astype(F32) for a, ref in zip(sums, refs)]
-    if len(refs[-1].shape) == 2 and refs[-1].shape[1] == FF:
-        refs[-1][:, :HALF] = sums[0].astype(BF)
-        refs[-1][:, HALF:] = sums[1].astype(BF)
-    else:
-        refs[-2][...] = sums[0].astype(BF)
-        refs[-1][...] = sums[1].astype(BF)
-
-
-def down_add(step, parts, moved=(), after=()):
-    pair = pl.BlockSpec((2, SUB, HALF), lambda i: (step, 0, 0))
-    one = pl.BlockSpec((SUB, HALF), lambda i: (0, 0))
-    whole = pl.BlockSpec((SUB, FF), lambda i: (0, 0))
-    last = step == NZ - 1
-    return pl.pallas_call(
-        functools.partial(down_add_kernel, len(moved) > 0),
+def down_sums_kernel(near_ref, far_ref, *refs):
+    for k, out_ref in enumerate(refs[-3:]):
+        out_ref[...] = (near_ref[k].astype(F32) + far_ref[k].astype(F32)).astype(BF)
+
+
+def down_sums(near, far, after=()):
+    some = pl.BlockSpec((NZ - 1, SUB, FF), lambda i: (0, 0, 0))
+    return pl.pallas_call(
+        down_sums_kernel,
         grid=(1,),
-        in_specs=[pair] * 2
-        + [one] * len(moved)
-        + [pl.BlockSpec(memory_space=pl.ANY)] * len(after),
-        out_specs=[whole] if last else [one] * 2,
-        out_shape=[jax.ShapeDtypeStruct((SUB, FF), BF)]
-        if last
-        else [jax.ShapeDtypeStruct((SUB, HALF), BF)] * 2,
-        compiler_params=params(),
-        cost_estimate=LONG if step == 1 else SHORT,
-    )(*parts, *moved, *after)
+        in_specs=[some] * 2 + [pl.BlockSpec(memory_space=pl.ANY)] * len(after),
+        out_specs=[pl.BlockSpec((SUB, FF), lambda i: (0, 0))] * 3,
+        out_shape=[jax.ShapeDtypeStruct((SUB, FF), BF)] * 3,
+        compiler_params=params(),
+        cost_estimate=SUMS,
+    )(near, far, *after)
+
+
+def down_last_kernel(near_ref, far_ref, a_ref, b_ref, c_ref, *refs):
+    total = near_ref[0].astype(F32) + far_ref[0].astype(F32)
+    for ref in (a_ref, b_ref, c_ref):
+        total = total + ref[...].astype(F32)
+    refs[-1][...] = total.astype(BF)
+
+
+def down_last(near, far, came, after=()):
+    half = SUB // 2
+    own = pl.BlockSpec((1, half, FF), lambda i: (NZ - 1, i, 0))
+    spec = pl.BlockSpec((half, FF), lambda i: (i, 0))
+    return pl.pallas_call(
+        down_last_kernel,
+        grid=(2,),
+        in_specs=[own] * 2 + [spec] * 3 + [pl.BlockSpec(memory_space=pl.ANY)] * len(after),
+        out_specs=spec,
+        out_shape=jax.ShapeDtypeStruct((SUB, FF), BF),
+        compiler_params=params(),
+        cost_estimate=LONG,
+    )(near, far, *came, *after)
 
 
 PLACES = np.array(
@@ -513,20 +520,16 @@
     sent_rows = row_grads(both, gate, up, wg, after=ring1)
     returned = exchange(sent_rows)
     parts2 = wide_parts(place, 2, lefts, boths, after=(sent_rows,))
-    down_pair = (near, far_in)
-    down_ring0 = down_add(0, down_pair, after=parts2[:1])
-    down_moved0 = around(*down_ring0)
-    ring2 = wide_add(parts2, moved1, after=down_ring0)
+    ring2 = wide_add(parts2, moved1)
     moved2 = around(*ring2)
-    parts3 = wide_parts(place, 3, lefts, boths, after=ring2)
-    down_ring1 = down_add(1, down_pair, down_moved0, after=parts3[:1])
-    down_moved1 = around(*down_ring1)
-    mine, away = wide_last(parts3, moved2, after=down_ring1)
+    sums = down_sums(near, far_in, after=ring2)
+    ways = (TO_DOWN, TO_UP, TO_TWO)
+    down_came = [lax.ppermute(part, "dp", way) for part, way in zip(sums, ways)]
+    parts3 = wide_parts(place, 3, lefts, boths, after=sums)
+    mine, away = wide_last(parts3, moved2)
     came = lax.ppermute(away, "dp", TO_X)
-    down_ring2 = down_add(2, down_pair, down_moved1, after=(away,))
-    down_moved2 = around(*down_ring2)
-    grad_tokens, grad_weights = combine(picks, returned, after=down_ring2)
-    (down_grad,) = down_add(3, down_pair, down_moved2, after=(grad_tokens,))
+    grad_tokens, grad_weights = combine(picks, returned, after=(away,))
+    down_grad = down_last(near, far_in, down_came, after=(grad_tokens,))
     mine, down_grad = lax.optimization_barrier((mine, down_grad))
     grad_gate = add(mine[0], came[0])[None]
     grad_up = add(mine[1], came[1])[None]

time: 246 us -> 245 us (level)
  waiting for transfers between devices: 84.5 us -> 96.2 us
  starting transfers between devices: 40.3 us -> 34.1 us
  Pallas kernels: 112 us -> 108 us
    ppermute x12 -> x6, starting transfers between devices: 19.1 us -> 9.3 us  [around(): return (lax.ppermute(up, 'dp', TO_UP), lax.ppermute(down, 'dp', TO_DOWN))]
    all_to_all x3, waiting for transfers between devices: 64.2 us -> 70.1 us  [exchange(): lax.all_to_all(rows.reshape(EXPERTS, CAP, width), 'expert', split_axis=0,...]
    ppermute x1, waiting for transfers between devices: 6.25 us -> 11 us  [local(): came = lax.ppermute(away, 'dp', TO_X)]
    ppermute x0 -> x3, starting transfers between devices: none -> 3.62 us  [local(): down_came = [lax.ppermute(part, 'dp', way) for part, way in zip(sums, ways)]]
    ppermute x12 -> x6, waiting for transfers between devices: 11.1 us -> 14.4 us  [around(): return (lax.ppermute(up, 'dp', TO_UP), lax.ppermute(down, 'dp', TO_DOWN))]
    pallas_call x4 -> x2, Pallas kernels: 8.56 us -> 5.53 us  [the longest x1 2.93 us: down_sums(): pl.pallas_call(down_sums_kernel, grid=(1,), in_specs=[some] * 2 + [pl.Blo...]
    ppermute x1, waiting for transfers between devices: 3 us -> 0.01 us  [local(): far_in = lax.ppermute(far, 'dp', TO_X)]
  transfers between devices with their start and end apart: 21 -> 18, of which waited for: 7 -> 8; matrix products, arithmetic and copies ran while one was open for 0% -> 0% of each run, Pallas kernels for 40% -> 39%
where the time goes in v6:
time: 245 us; the launch traced here: 244 us
  Pallas kernels  108 us (44%)
  waiting for transfers between devices  96.2 us (39%)
  starting transfers between devices  34.1 us (14%)
  local copies, waits for them, and re-layouts  2.5 us (1%)
    all_to_all x3, waiting for transfers between devices, exchange(): lax.all_to_all(rows.reshape(EXPERTS, CAP, width), 'expert', split_axis=0,...  70.1 us
    pallas_call x4, Pallas kernels, wide_parts(): pl.pallas_call(wide_kernel, grid_spec=pltpu.PrefetchScalarGridSpec(num_sc...  24.9 us
    all_to_all x3, starting transfers between devices, exchange(): lax.all_to_all(rows.reshape(EXPERTS, CAP, width), 'expert', split_axis=0,...  14.6 us
    ppermute x6, waiting for transfers between devices, around(): return (lax.ppermute(up, 'dp', TO_UP), lax.ppermute(down, 'dp', TO_DOWN))  14.4 us
    pallas_call x1, Pallas kernels, forward(): pl.pallas_call(forward_kernel, grid=(FF // n,), in_specs=[pl.BlockSpec((R...  13.4 us
    pallas_call x1, Pallas kernels, row_grads(): pl.pallas_call(rows_kernel, grid=(NT + 1,), in_specs=[pl.BlockSpec((2, RO...  13.1 us
    pallas_call x2, Pallas kernels, turned(): pl.pallas_call(functools.partial(turned_kernel, scaled, len(after)), grid...  11.6 us
    ppermute x1, waiting for transfers between devices, local(): came = lax.ppermute(away, 'dp', TO_X)  11 us
  transfers between devices with their start and end apart: 18, of which 8 were waited for; matrix products, arithmetic and copies ran while one was open for 0% of the time, Pallas kernels for 39%

profile of v6, /device:TPU:0, one launch (start us, length us, event | category | flops | bytes accessed | tf_op | source)
XLA Modules:
  0.0 244.2 jit_solution(5492703699380086114)
XLA Ops:
  0.6 3.8 %shard_map.119 = (bf16[2,512,128]{2,1,0:T(8,128)(2,1)}, bf16[512,3584]{1,0:T(8,128)(2,1)}) custom-call(s32[2,128]{1,0:T(2,128)} %bitcast.22, bf16[128,3584]{1,0:T(8,128)(2,1)} %tokens_ref.1), custom_call_target="tpu_custom_call" | custom-call | flops 469762048 | bytes 5242880 | tf_op jit(solution)/shard_map/pallas_call | solution.py:68
  4.4 5.5 %all-to-all-start.1 = ((bf16[8,64,3584]{2,1,0:T(8,128)(2,1)}), bf16[8,64,3584]{2,1,0:T(8,128)(2,1)}, u32[]{:S(2)}, u32[]{:S(2)}) async-start(bf16[8,64,3584]{2,1,0:T(8,128)(2,1)} %bitcast.20), calls=%async_computation.1 | async-start | bytes 7340032 | tf_op jit(solution)/shard_map/all_to_all | solution.py:492
  9.9 3.9 %shard_map.120 = bf16[512,3712]{1,0:T(8,128)(2,1)} custom-call(bf16[2,512,128]{2,1,0:T(8,128)(2,1)} %get-tuple-element.39.picks_ref, bf16[2,128]{1,0:T(2,128)(2,1)} %bitcast.21, bf16[128,3584]{1,0:T(8,128)(2,1)} %grads_ref.1), custom_call_target="tpu_custom_call" | custom-call | flops 469762048 | bytes 5242880 | tf_op jit(solution)/shard_map/pallas_call | solution.py:105
  13.8 40.1 %all-to-all-done.1 = bf16[8,64,3584]{2,1,0:T(8,128)(2,1)} async-done(((bf16[8,64,3584]{2,1,0:T(8,128)(2,1)}), bf16[8,64,3584]{2,1,0:T(8,128)(2,1)}, u32[]{:S(2)}, u32[]{:S(2)}) %all-to-all-start.1) | async-done | bytes 3670048 | tf_op jit(solution)/shard_map/all_to_all | solution.py:492
  53.8 4.6 %all-to-all-start = ((bf16[8,64,3712]{2,1,0:T(8,128)(2,1)}), bf16[8,64,3712]{2,1,0:T(8,128)(2,1)}, u32[]{:S(2)}, u32[]{:S(2)}) async-start(bf16[8,64,3712]{2,1,0:T(8,128)(2,1)} %bitcast.13), calls=%async_computation | async-start | bytes 7602176 | tf_op jit(solution)/shard_map/all_to_all | solution.py:492
  59.1 13.4 %shard_map.121 = (bf16[512,1024]{1,0:T(8,128)(2,1)}, f32[512,1024]{1,0:T(8,128)}, f32[512,1024]{1,0:T(8,128)}) custom-call(bf16[512,3584]{1,0:T(8,128)(2,1)} %bitcast.6.x_ref.p_ref, bf16[3584,1024]{1,0:T(8,128)(2,1)} %bitcast.16, bf16[3584,1024]{1,0:T(8,128)(2,1)} %bitcast.18), custom_call_target="tpu_custom_call" | custom-call | flops 7516192768 | bytes 24117248 | tf_op jit(solution)/shard_map/pallas_call | solution.py:133
  72.4 5.6 %shard_map.122 = (bf16[4,448,512]{2,1,0:T(8,128)(2,1)}, bf16[4,448,512]{2,1,0:T(8,128)(2,1)}) custom-call(s32[10]{0:T(128)} %dynamic_slice.3.place_ref, bf16[512,3584]{1,0:T(8,128)(2,1)} %bitcast.6.x_ref.p_ref, bf16[512,3584]{1,0:T(8,128)(2,1)} %bitcast.6.x_ref.p_ref, bf16[512,1024]{1,0:T(8,128)(2,1)} %get-tuple-element.41.refs_0_.hidden_ref.right_a), custom_call_target="tpu_custom_call" | custom-call | flops 1835008 | bytes 8388608 | tf_op jit(solution)/shard_map/pallas_call | solution.py:249
  78.6 24.2 %all-to-all-done = bf16[8,64,3712]{2,1,0:T(8,128)(2,1)} async-done(((bf16[8,64,3712]{2,1,0:T(8,128)(2,1)}), bf16[8,64,3712]{2,1,0:T(8,128)(2,1)}, u32[]{:S(2)}, u32[]{:S(2)}) %all-to-all-start) | async-done | bytes 3801120 | tf_op jit(solution)/shard_map/all_to_all | solution.py:492
  102.8 10.0 %shard_map.123 = (bf16[2,512,1024]{2,1,0:T(8,128)(2,1)}, bf16[512,128]{1,0:T(8,128)(2,1)}) custom-call(bf16[512,3712]{1,0:T(8,128)(2,1)} %bitcast.3.g_ref.x_ref.p_ref, bf16[3584,1024]{1,0:T(8,128)(2,1)} %bitcast.15, bf16[512,1024]{1,0:T(8,128)(2,1)} %get-tuple-element.41.refs_0_.hidden_ref.right_a, f32[512,1024]{1,0:T(8,128)} %get-tuple-element.42.active_ref, ...), custom_call_target="tpu_custom_call" | custom-call | flops 3758096384 | bytes 18874368 | tf_op jit(solution)/shard_map/pallas_call | solution.py:172
  112.8 5.9 %shard_map.124 = (bf16[4,448,512]{2,1,0:T(8,128)(2,1)}, bf16[4,448,512]{2,1,0:T(8,128)(2,1)}) custom-call(s32[10]{0:T(128)} %dynamic_slice.3.place_ref, bf16[512,3712]{1,0:T(8,128)(2,1)} %bitcast.3.g_ref.x_ref.p_ref, bf16[512,3712]{1,0:T(8,128)(2,1)} %bitcast.3.g_ref.x_ref.p_ref, bf16[2,512,1024]{2,1,0:T(8,128)(2,1)} %get-tuple-element.46.refs_0_.right_a.both_ref), custom_call_target="tpu_custom_call" | custom-call | flops 1835008 | bytes 8388608 | tf_op jit(solution)/shard_map/pallas_call | solution.py:249
  119.2 6.2 %shard_map.125 = (bf16[448,1024]{1,0:T(8,128)(2,1)}, bf16[448,1024]{1,0:T(8,128)(2,1)}) custom-call(s32[10]{0:T(128)} %dynamic_slice.3.place_ref, bf16[4,448,512]{2,1,0:T(8,128)(2,1)} %get-tuple-element.44.refs_0_.left_a, bf16[4,448,512]{2,1,0:T(8,128)(2,1)} %collective-permute-done.refs_1_.left_b, ...), custom_call_target="tpu_custom_call" | custom-call | flops 1879048192 | bytes 8388608 | tf_op jit(solution)/shard_map/pallas_call | solution.py:348
  129.5 8.3 %shard_map.126 = (bf16[4,224,1024]{2,1,0:T(8,128)(2,1)}, bf16[4,224,1024]{2,1,0:T(8,128)(2,1)}) custom-call(s32[10]{0:T(128)} %dynamic_slice.3.place_ref, bf16[4,448,512]{2,1,0:T(8,128)(2,1)} %get-tuple-element.48.refs_0_.left_a, bf16[4,448,512]{2,1,0:T(8,128)(2,1)} %collective-permute-done.3.left_b, ...), custom_call_target="tpu_custom_call" | custom-call | flops 1879048192 | bytes 8388608 | tf_op jit(solution)/shard_map/pallas_call | solution.py:374
  140.6 6.2 %shard_map.127 = (bf16[448,1024]{1,0:T(8,128)(2,1)}, bf16[448,1024]{1,0:T(8,128)(2,1)}) custom-call(s32[10]{0:T(128)} %dynamic_slice.3.place_ref, bf16[4,448,512]{2,1,0:T(8,128)(2,1)} %get-tuple-element.44.refs_0_.left_a, bf16[4,448,512]{2,1,0:T(8,128)(2,1)} %collective-permute-done.refs_1_.left_b, ...), custom_call_target="tpu_custom_call" | custom-call | flops 1879048192 | bytes 8388608 | tf_op jit(solution)/shard_map/pallas_call | solution.py:348
  146.8 3.4 %collective-permute-done.4.up_ref = bf16[448,1024]{1,0:T(8,128)(2,1)S(1)} collective-permute-done((bf16[448,1024]{1,0:T(8,128)(2,1)}, bf16[448,1024]{1,0:T(8,128)(2,1)S(1)}, u32[]{:S(2)}, u32[]{:S(2)}) %collective-permute-start.4) | collective-permute-done | bytes 917536 | tf_op jit(solution)/shard_map/ppermute | solution.py:390
  151.2 3.1 %shard_map.128 = (bf16[448,1024]{1,0:T(8,128)(2,1)}, bf16[448,1024]{1,0:T(8,128)(2,1)}) custom-call(bf16[448,1024]{1,0:T(8,128)(2,1)} %get-tuple-element.52.part_up, bf16[448,1024]{1,0:T(8,128)(2,1)} %get-tuple-element.53.part_down, bf16[448,1024]{1,0:T(8,128)(2,1)} %copy-done.1, bf16[448,1024]{1,0:T(8,128)(2,1)} %collective-permute-done.5.down_ref), custom_call_target="tpu_custom_call" | custom-call | flops 1 | bytes 1 | tf_op jit(solution)/shard_map/pallas_call | solution.py:400
  157.5 13.1 %shard_map.129.refs_0_ = bf16[512,3712]{1,0:T(8,128)(2,1)} custom-call(bf16[2,512,1024]{2,1,0:T(8,128)(2,1)} %get-tuple-element.46.refs_0_.right_a.both_ref, bf16[3584,1024]{1,0:T(8,128)(2,1)} %bitcast.17, bf16[3584,1024]{1,0:T(8,128)(2,1)} %bitcast.19, bf16[512,128]{1,0:T(8,128)(2,1)} %get-tuple-element.47.wg_ref, ...), custom_call_target="tpu_custom_call" | custom-call | flops 1 | bytes 1 | tf_op jit(solution)/shard_map/pallas_call | solution.py:214
  170.6 4.5 %all-to-all-start.2 = ((bf16[8,64,3712]{2,1,0:T(8,128)(2,1)}), bf16[8,64,3712]{2,1,0:T(8,128)(2,1)}, u32[]{:S(2)}, u32[]{:S(2)}) async-start(bf16[8,64,3712]{2,1,0:T(8,128)(2,1)} %bitcast.14), calls=%async_computation.2 | async-start | bytes 7602176 | tf_op jit(solution)/shard_map/all_to_all | solution.py:492
  175.1 6.2 %shard_map.130 = (bf16[448,1024]{1,0:T(8,128)(2,1)}, bf16[448,1024]{1,0:T(8,128)(2,1)}) custom-call(s32[10]{0:T(128)} %dynamic_slice.3.place_ref, bf16[4,448,512]{2,1,0:T(8,128)(2,1)} %get-tuple-element.44.refs_0_.left_a, bf16[4,448,512]{2,1,0:T(8,128)(2,1)} %collective-permute-done.refs_1_.left_b, ...), custom_call_target="tpu_custom_call" | custom-call | flops 24999999488 | bytes 1 | tf_op jit(solution)/shard_map/pallas_call | solution.py:348
  194.0 6.2 %shard_map.133 = (bf16[448,1024]{1,0:T(8,128)(2,1)}, bf16[448,1024]{1,0:T(8,128)(2,1)}) custom-call(s32[10]{0:T(128)} %dynamic_slice.3.place_ref, bf16[4,448,512]{2,1,0:T(8,128)(2,1)} %get-tuple-element.44.refs_0_.left_a, bf16[4,448,512]{2,1,0:T(8,128)(2,1)} %collective-permute-done.refs_1_.left_b, ...), custom_call_target="tpu_custom_call" | custom-call | flops 1 | bytes 1 | tf_op jit(solution)/shard_map/pallas_call | solution.py:348
  200.2 8.7 %collective-permute-done.10.down_ref = bf16[448,1024]{1,0:T(8,128)(2,1)S(1)} collective-permute-done((bf16[448,1024]{1,0:T(8,128)(2,1)}, bf16[448,1024]{1,0:T(8,128)(2,1)S(1)}, u32[]{:S(2)}, u32[]{:S(2)}) %collective-permute-start.10) | collective-permute-done | bytes 917536 | tf_op jit(solution)/shard_map/ppermute | solution.py:390
  211.2 3.7 %shard_map.134 = (bf16[2,224,1024]{2,1,0:T(8,128)(2,1)}, bf16[2,224,1024]{2,1,0:T(8,128)(2,1)}) custom-call(bf16[448,1024]{1,0:T(8,128)(2,1)} %get-tuple-element.65.part_up, bf16[448,1024]{1,0:T(8,128)(2,1)} %get-tuple-element.66.part_down, bf16[448,1024]{1,0:T(8,128)(2,1)} %collective-permute-done.9.up_ref, bf16[448,1024]{1,0:T(8,128)(2,1)} %copy-done), custom_call_target="tpu_custom_call" | custom-call | flops 1 | bytes 1 | tf_op jit(solution)/shard_map/pallas_call | solution.py:428
  217.7 5.8 %all-to-all-done.2 = bf16[8,64,3712]{2,1,0:T(8,128)(2,1)} async-done(((bf16[8,64,3712]{2,1,0:T(8,128)(2,1)}), bf16[8,64,3712]{2,1,0:T(8,128)(2,1)}, u32[]{:S(2)}, u32[]{:S(2)}) %all-to-all-start.2) | async-done | bytes 3801120 | tf_op jit(solution)/shard_map/all_to_all | solution.py:492
  223.5 4.1 %shard_map.135 = (bf16[128,3584]{1,0:T(8,128)(2,1)}, bf16[2,128]{1,0:T(2,128)(2,1)}) custom-call(bf16[2,512,128]{2,1,0:T(8,128)(2,1)} %get-tuple-element.39.picks_ref, bf16[512,3712]{1,0:T(8,128)(2,1)} %bitcast.10.rows_ref, bf16[2,224,1024]{2,1,0:T(8,128)(2,1)} %get-tuple-element.67.refs_0_), custom_call_target="tpu_custom_call" | custom-call | flops 1 | bytes 1 | tf_op jit(solution)/shard_map/pallas_call | solution.py:290
  230.8 11.0 %collective-permute-done.14 = bf16[2,224,1024]{2,1,0:T(8,128)(2,1)} collective-permute-done((bf16[2,224,1024]{2,1,0:T(8,128)(2,1)}, bf16[2,224,1024]{2,1,0:T(8,128)(2,1)}, u32[]{:S(2)}, u32[]{:S(2)}) %collective-permute-start.14) | collective-permute-done | bytes 917536 | tf_op jit(solution)/shard_map/ppermute | solution.py:530
  (42 shorter events, 35.9 us)
Async XLA Ops:
  4.4 49.4 %all-to-all-start.1 = ((bf16[8,64,3584]{2,1,0:T(8,128)(2,1)}), bf16[8,64,3584]{2,1,0:T(8,128)(2,1)}, u32[]{:S(2)}, u32[]{:S(2)}) async-start(bf16[8,64,3584]{2,1,0:T(8,128)(2,1)} %bitcast.20), calls=%async_computation.1 | async-start | bytes 7340032 | tf_op jit(solution)/shard_map/all_to_all | solution.py:492
  53.8 4.7 %copy-start.4 = (s32[160]{0:T(256)S(1)}, s32[160]{0:T(256)}, u32[]{:S(2)}) copy-start(s32[160]{0:T(256)} %constant.14.clone) | copy-start | bytes 1924
  53.8 49.0 %all-to-all-start = ((bf16[8,64,3712]{2,1,0:T(8,128)(2,1)}), bf16[8,64,3712]{2,1,0:T(8,128)(2,1)}, u32[]{:S(2)}, u32[]{:S(2)}) async-start(bf16[8,64,3712]{2,1,0:T(8,128)(2,1)} %bitcast.13), calls=%async_computation | async-start | bytes 7602176 | tf_op jit(solution)/shard_map/all_to_all | solution.py:492
  78.1 24.7 %collective-permute-start = (bf16[4,448,512]{2,1,0:T(8,128)(2,1)}, bf16[4,448,512]{2,1,0:T(8,128)(2,1)}, u32[]{:S(2)}, u32[]{:S(2)}) collective-permute-start(bf16[4,448,512]{2,1,0:T(8,128)(2,1)} %get-tuple-element.45), channel_id=1, source_target_pairs={{0,8},{8,0},{16,24},{24,16},{32,40},{40,32},{48,56},{56,48},{64,72... | collective-permute-start | bytes 5505032 | tf_op jit(solution)/shard_map/ppermute | solution.py:266
  78.1 24.7 %collective-permute-start.1 = (bf16[512,1024]{1,0:T(8,128)(2,1)}, bf16[512,1024]{1,0:T(8,128)(2,1)}, u32[]{:S(2)}, u32[]{:S(2)}) collective-permute-start(bf16[512,1024]{1,0:T(8,128)(2,1)} %get-tuple-element.41.refs_0_.hidden_ref.right_a), channel_id=1, source_target_pairs={{0,8},{8,0},{16,24},{24,16},{32,40},{40,32},{48,56},{56,48},{64,72... | collective-permute-start | bytes 3145736 | tf_op jit(solution)/shard_map/ppermute | solution.py:507
  112.8 6.4 %collective-permute-start.2 = (bf16[2,512,1024]{2,1,0:T(8,128)(2,1)}, bf16[2,512,1024]{2,1,0:T(8,128)(2,1)}, u32[]{:S(2)}, u32[]{:S(2)}) collective-permute-start(bf16[2,512,1024]{2,1,0:T(8,128)(2,1)} %get-tuple-element.46.refs_0_.right_a.both_ref), channel_id=1, source_target_pairs={{0,8},{8,0},{16,24},{24,16},{32,40},{40,32},{48,56},{56,48},{64,72... | collective-permute-start | bytes 6291464 | tf_op jit(solution)/shard_map/ppermute | solution.py:511
  118.7 10.8 %collective-permute-start.3 = (bf16[4,448,512]{2,1,0:T(8,128)(2,1)}, bf16[4,448,512]{2,1,0:T(8,128)(2,1)}, u32[]{:S(2)}, u32[]{:S(2)}) collective-permute-start(bf16[4,448,512]{2,1,0:T(8,128)(2,1)} %get-tuple-element.49), channel_id=1, source_target_pairs={{0,8},{8,0},{16,24},{24,16},{32,40},{40,32},{48,56},{56,48},{64,72... | collective-permute-start | bytes 5505032 | tf_op jit(solution)/shard_map/ppermute | solution.py:266
  125.5 24.8 %collective-permute-start.4 = (bf16[448,1024]{1,0:T(8,128)(2,1)}, bf16[448,1024]{1,0:T(8,128)(2,1)S(1)}, u32[]{:S(2)}, u32[]{:S(2)}) collective-permute-start(bf16[448,1024]{1,0:T(8,128)(2,1)} %get-tuple-element.50.refs_0_), channel_id=1, source_target_pairs={{0,32},{8,40},{16,48},{24,56},{32,64},{40,72},{48,80},{56,88},{64,... | collective-permute-start | bytes 2752520 | tf_op jit(solution)/shard_map/ppermute | solution.py:390
  127.4 22.9 %collective-permute-start.5 = (bf16[448,1024]{1,0:T(8,128)(2,1)}, bf16[448,1024]{1,0:T(8,128)(2,1)}, u32[]{:S(2)}, u32[]{:S(2)}) collective-permute-start(bf16[448,1024]{1,0:T(8,128)(2,1)} %get-tuple-element.54), channel_id=1, source_target_pairs={{0,96},{8,104},{16,112},{24,120},{32,0},{40,8},{48,16},{56,24},{64... | collective-permute-start | bytes 2752520 | tf_op jit(solution)/shard_map/ppermute | solution.py:390
  137.9 49.6 %collective-permute-start.6 = (bf16[4,224,1024]{2,1,0:T(8,128)(2,1)}, bf16[4,224,1024]{2,1,0:T(8,128)(2,1)}, u32[]{:S(2)}, u32[]{:S(2)}) collective-permute-start(bf16[4,224,1024]{2,1,0:T(8,128)(2,1)} %get-tuple-element.51.refs_0_), channel_id=1, source_target_pairs={{0,16},{8,24},{16,0},{24,8},{32,48},{40,56},{48,32},{56,40},{64,80... | collective-permute-start | bytes 5505032 | tf_op jit(solution)/shard_map/ppermute | solution.py:516
  150.2 0.9 copy-start.1
  154.3 27.1 %collective-permute-start.7 = (bf16[448,1024]{1,0:T(8,128)(2,1)}, bf16[448,1024]{1,0:T(8,128)(2,1)S(1)}, u32[]{:S(2)}, u32[]{:S(2)}) collective-permute-start(bf16[448,1024]{1,0:T(8,128)(2,1)} %get-tuple-element.55.refs_0_), channel_id=1, source_target_pairs={{0,32},{8,40},{16,48},{24,56},{32,64},{40,72},{48,80},{56,88},{64,... | collective-permute-start | bytes 2752520 | tf_op jit(solution)/shard_map/ppermute | solution.py:390
  154.7 26.6 %collective-permute-start.8 = (bf16[448,1024]{1,0:T(8,128)(2,1)}, bf16[448,1024]{1,0:T(8,128)(2,1)}, u32[]{:S(2)}, u32[]{:S(2)}) collective-permute-start(bf16[448,1024]{1,0:T(8,128)(2,1)} %get-tuple-element.56.refs_1_), channel_id=1, source_target_pairs={{0,96},{8,104},{16,112},{24,120},{32,0},{40,8},{48,16},{56,24},{64... | collective-permute-start | bytes 2752520 | tf_op jit(solution)/shard_map/ppermute | solution.py:390
  170.6 52.9 %all-to-all-start.2 = ((bf16[8,64,3712]{2,1,0:T(8,128)(2,1)}), bf16[8,64,3712]{2,1,0:T(8,128)(2,1)}, u32[]{:S(2)}, u32[]{:S(2)}) async-start(bf16[8,64,3712]{2,1,0:T(8,128)(2,1)} %bitcast.14), calls=%async_computation.2 | async-start | bytes 7602176 | tf_op jit(solution)/shard_map/all_to_all | solution.py:492
  181.4 1.0 copy-start.2
  185.5 23.5 %collective-permute-start.10 = (bf16[448,1024]{1,0:T(8,128)(2,1)}, bf16[448,1024]{1,0:T(8,128)(2,1)S(1)}, u32[]{:S(2)}, u32[]{:S(2)}) collective-permute-start(bf16[448,1024]{1,0:T(8,128)(2,1)} %get-tuple-element.61.refs_1_), channel_id=1, source_target_pairs={{0,96},{8,104},{16,112},{24,120},{32,0},{40,8},{48,16},{56,24},{64... | collective-permute-start | bytes 2752520 | tf_op jit(solution)/shard_map/ppermute | solution.py:390
  186.4 24.8 %collective-permute-start.9 = (bf16[448,1024]{1,0:T(8,128)(2,1)}, bf16[448,1024]{1,0:T(8,128)(2,1)}, u32[]{:S(2)}, u32[]{:S(2)}) collective-permute-start(bf16[448,1024]{1,0:T(8,128)(2,1)} %get-tuple-element.60.refs_0_), channel_id=1, source_target_pairs={{0,32},{8,40},{16,48},{24,56},{32,64},{40,72},{48,80},{56,88},{64,... | collective-permute-start | bytes 2752520 | tf_op jit(solution)/shard_map/ppermute | solution.py:390
  190.4 37.2 %collective-permute-start.11 = (bf16[224,1024]{1,0:T(8,128)(2,1)}, bf16[224,1024]{1,0:T(8,128)(2,1)}, u32[]{:S(2)}, u32[]{:S(2)}) collective-permute-start(bf16[224,1024]{1,0:T(8,128)(2,1)} %get-tuple-element.62.refs_0_), channel_id=1, source_target_pairs={{0,96},{8,104},{16,112},{24,120},{32,0},{40,8},{48,16},{56,24},{64... | collective-permute-start | bytes 1376264 | tf_op jit(solution)/shard_map/ppermute | solution.py:527
  192.6 35.6 %collective-permute-start.12 = (bf16[224,1024]{1,0:T(8,128)(2,1)}, bf16[224,1024]{1,0:T(8,128)(2,1)}, u32[]{:S(2)}, u32[]{:S(2)}) collective-permute-start(bf16[224,1024]{1,0:T(8,128)(2,1)} %get-tuple-element.63.refs_1_), channel_id=1, source_target_pairs={{0,32},{8,40},{16,48},{24,56},{32,64},{40,72},{48,80},{56,88},{64,... | collective-permute-start | bytes 1376264 | tf_op jit(solution)/shard_map/ppermute | solution.py:527
  192.6 35.6 %collective-permute-start.13 = (bf16[224,1024]{1,0:T(8,128)(2,1)}, bf16[224,1024]{1,0:T(8,128)(2,1)}, u32[]{:S(2)}, u32[]{:S(2)}) collective-permute-start(bf16[224,1024]{1,0:T(8,128)(2,1)} %get-tuple-element.64.refs_2_), channel_id=1, source_target_pairs={{0,64},{8,72},{16,80},{24,88},{32,96},{40,104},{48,112},{56,120},{... | collective-permute-start | bytes 1376264 | tf_op jit(solution)/shard_map/ppermute | solution.py:527
  209.0 2.3 copy-start
  214.9 26.9 %collective-permute-start.14 = (bf16[2,224,1024]{2,1,0:T(8,128)(2,1)}, bf16[2,224,1024]{2,1,0:T(8,128)(2,1)}, u32[]{:S(2)}, u32[]{:S(2)}) collective-permute-start(bf16[2,224,1024]{2,1,0:T(8,128)(2,1)} %get-tuple-element.67.refs_0_), channel_id=1, source_target_pairs={{0,16},{8,24},{16,0},{24,8},{32,48},{40,56},{48,32},{56,40},{64,80... | collective-permute-start | bytes 2752520 | tf_op jit(solution)/shard_map/ppermute | solution.py:530
  228.2 13.6 %copy-start.3 = (bf16[2,224,1024]{2,1,0:T(8,128)(2,1)S(1)}, bf16[2,224,1024]{2,1,0:T(8,128)(2,1)}, u32[]{:S(2)}) copy-start(bf16[2,224,1024]{2,1,0:T(8,128)(2,1)} %get-tuple-element.71) | copy-start | bytes 2752516

commit v7 on v6

--- a/solution.py
+++ b/solution.py
@@ -31,7 +31,7 @@
 
 
 def params(limit=63):
-    return pltpu.CompilerParams(vmem_limit_bytes=limit * MB)
+    return pltpu.CompilerParams(vmem_limit_bytes=limit * MB + MB // 2)
 
 
 def cost(flops, nbytes, trans=0):
@@ -522,11 +522,11 @@
     parts2 = wide_parts(place, 2, lefts, boths, after=(sent_rows,))
     ring2 = wide_add(parts2, moved1)
     moved2 = around(*ring2)
-    sums = down_sums(near, far_in, after=ring2)
+    parts3 = wide_parts(place, 3, lefts, boths, after=ring2)
+    sums = down_sums(near, far_in, after=parts3)
     ways = (TO_DOWN, TO_UP, TO_TWO)
     down_came = [lax.ppermute(part, "dp", way) for part, way in zip(sums, ways)]
-    parts3 = wide_parts(place, 3, lefts, boths, after=sums)
-    mine, away = wide_last(parts3, moved2)
+    mine, away = wide_last(parts3, moved2, after=sums)
     came = lax.ppermute(away, "dp", TO_X)
     grad_tokens, grad_weights = combine(picks, returned, after=(away,))
     down_grad = down_last(near, far_in, down_came, after=(grad_tokens,))

time: 245 us -> 245 us (level)
    all_to_all x3, waiting for transfers between devices: 70.1 us -> 72.8 us  [exchange(): lax.all_to_all(rows.reshape(EXPERTS, CAP, width), 'expert', split_axis=0,...]
  transfers between devices with their start and end apart: 18 -> 18, of which waited for: 8 -> 6; matrix products, arithmetic and copies ran while one was open for 0% -> 0% of each run, Pallas kernels for 39% -> 39%
where the time goes in v7:
time: 245 us; the launch traced here: 244 us
  Pallas kernels  108 us (44%)
  waiting for transfers between devices  97.2 us (40%)
  starting transfers between devices  34.1 us (14%)
  other arithmetic  2.7 us (1%)
    all_to_all x3, waiting for transfers between devices, exchange(): lax.all_to_all(rows.reshape(EXPERTS, CAP, width), 'expert', split_axis=0,...  72.8 us
    pallas_call x4, Pallas kernels, wide_parts(): pl.pallas_call(wide_kernel, grid_spec=pltpu.PrefetchScalarGridSpec(num_sc...  24.9 us
    all_to_all x3, starting transfers between devices, exchange(): lax.all_to_all(rows.reshape(EXPERTS, CAP, width), 'expert', split_axis=0,...  14.6 us
    ppermute x6, waiting for transfers between devices, around(): return (lax.ppermute(up, 'dp', TO_UP), lax.ppermute(down, 'dp', TO_DOWN))  13.5 us
    pallas_call x1, Pallas kernels, forward(): pl.pallas_call(forward_kernel, grid=(FF // n,), in_specs=[pl.BlockSpec((R...  13.3 us
    pallas_call x1, Pallas kernels, row_grads(): pl.pallas_call(rows_kernel, grid=(NT + 1,), in_specs=[pl.BlockSpec((2, RO...  13.2 us
    pallas_call x2, Pallas kernels, turned(): pl.pallas_call(functools.partial(turned_kernel, scaled, len(after)), grid...  11.6 us
    ppermute x1, waiting for transfers between devices, local(): came = lax.ppermute(away, 'dp', TO_X)  10.9 us
  transfers between devices with their start and end apart: 18, of which 6 were waited for; matrix products, arithmetic and copies ran while one was open for 0% of the time, Pallas kernels for 39%

profile of v7, /device:TPU:0, one launch (start us, length us, event | category | flops | bytes accessed | tf_op | source)
XLA Modules:
  0.0 244.4 jit_solution(4944327462309747988)
XLA Ops:
  0.6 3.7 %shard_map.119 = (bf16[2,512,128]{2,1,0:T(8,128)(2,1)}, bf16[512,3584]{1,0:T(8,128)(2,1)}) custom-call(s32[2,128]{1,0:T(2,128)} %bitcast.22, bf16[128,3584]{1,0:T(8,128)(2,1)} %tokens_ref.1), custom_call_target="tpu_custom_call" | custom-call | flops 469762048 | bytes 5242880 | tf_op jit(solution)/shard_map/pallas_call | solution.py:68
  4.4 5.5 %all-to-all-start.1 = ((bf16[8,64,3584]{2,1,0:T(8,128)(2,1)}), bf16[8,64,3584]{2,1,0:T(8,128)(2,1)}, u32[]{:S(2)}, u32[]{:S(2)}) async-start(bf16[8,64,3584]{2,1,0:T(8,128)(2,1)} %bitcast.20), calls=%async_computation.1 | async-start | bytes 7340032 | tf_op jit(solution)/shard_map/all_to_all | solution.py:492
  9.9 3.9 %shard_map.120 = bf16[512,3712]{1,0:T(8,128)(2,1)} custom-call(bf16[2,512,128]{2,1,0:T(8,128)(2,1)} %get-tuple-element.39.picks_ref, bf16[2,128]{1,0:T(2,128)(2,1)} %bitcast.21, bf16[128,3584]{1,0:T(8,128)(2,1)} %grads_ref.1), custom_call_target="tpu_custom_call" | custom-call | flops 469762048 | bytes 5242880 | tf_op jit(solution)/shard_map/pallas_call | solution.py:105
  13.7 40.1 %all-to-all-done.1 = bf16[8,64,3584]{2,1,0:T(8,128)(2,1)} async-done(((bf16[8,64,3584]{2,1,0:T(8,128)(2,1)}), bf16[8,64,3584]{2,1,0:T(8,128)(2,1)}, u32[]{:S(2)}, u32[]{:S(2)}) %all-to-all-start.1) | async-done | bytes 3670048 | tf_op jit(solution)/shard_map/all_to_all | solution.py:492
  53.8 4.6 %all-to-all-start = ((bf16[8,64,3712]{2,1,0:T(8,128)(2,1)}), bf16[8,64,3712]{2,1,0:T(8,128)(2,1)}, u32[]{:S(2)}, u32[]{:S(2)}) async-start(bf16[8,64,3712]{2,1,0:T(8,128)(2,1)} %bitcast.13), calls=%async_computation | async-start | bytes 7602176 | tf_op jit(solution)/shard_map/all_to_all | solution.py:492
  59.0 13.3 %shard_map.121 = (bf16[512,1024]{1,0:T(8,128)(2,1)}, f32[512,1024]{1,0:T(8,128)}, f32[512,1024]{1,0:T(8,128)}) custom-call(bf16[512,3584]{1,0:T(8,128)(2,1)} %bitcast.6.x_ref.p_ref, bf16[3584,1024]{1,0:T(8,128)(2,1)} %bitcast.16, bf16[3584,1024]{1,0:T(8,128)(2,1)} %bitcast.18), custom_call_target="tpu_custom_call" | custom-call | flops 7516192768 | bytes 24117248 | tf_op jit(solution)/shard_map/pallas_call | solution.py:133
  72.4 5.7 %shard_map.122 = (bf16[4,448,512]{2,1,0:T(8,128)(2,1)}, bf16[4,448,512]{2,1,0:T(8,128)(2,1)}) custom-call(s32[10]{0:T(128)} %dynamic_slice.3.place_ref, bf16[512,3584]{1,0:T(8,128)(2,1)} %bitcast.6.x_ref.p_ref, bf16[512,3584]{1,0:T(8,128)(2,1)} %bitcast.6.x_ref.p_ref, bf16[512,1024]{1,0:T(8,128)(2,1)} %get-tuple-element.41.refs_0_.hidden_ref.right_a), custom_call_target="tpu_custom_call" | custom-call | flops 1835008 | bytes 8388608 | tf_op jit(solution)/shard_map/pallas_call | solution.py:249
  78.5 24.3 %all-to-all-done = bf16[8,64,3712]{2,1,0:T(8,128)(2,1)} async-done(((bf16[8,64,3712]{2,1,0:T(8,128)(2,1)}), bf16[8,64,3712]{2,1,0:T(8,128)(2,1)}, u32[]{:S(2)}, u32[]{:S(2)}) %all-to-all-start) | async-done | bytes 3801120 | tf_op jit(solution)/shard_map/all_to_all | solution.py:492
  102.8 10.0 %shard_map.123 = (bf16[2,512,1024]{2,1,0:T(8,128)(2,1)}, bf16[512,128]{1,0:T(8,128)(2,1)}) custom-call(bf16[512,3712]{1,0:T(8,128)(2,1)} %bitcast.3.g_ref.x_ref.p_ref, bf16[3584,1024]{1,0:T(8,128)(2,1)} %bitcast.15, bf16[512,1024]{1,0:T(8,128)(2,1)} %get-tuple-element.41.refs_0_.hidden_ref.right_a, f32[512,1024]{1,0:T(8,128)} %get-tuple-element.42.active_ref, ...), custom_call_target="tpu_custom_call" | custom-call | flops 3758096384 | bytes 18874368 | tf_op jit(solution)/shard_map/pallas_call | solution.py:172
  112.7 6.0 %shard_map.124 = (bf16[4,448,512]{2,1,0:T(8,128)(2,1)}, bf16[4,448,512]{2,1,0:T(8,128)(2,1)}) custom-call(s32[10]{0:T(128)} %dynamic_slice.3.place_ref, bf16[512,3712]{1,0:T(8,128)(2,1)} %bitcast.3.g_ref.x_ref.p_ref, bf16[512,3712]{1,0:T(8,128)(2,1)} %bitcast.3.g_ref.x_ref.p_ref, bf16[2,512,1024]{2,1,0:T(8,128)(2,1)} %get-tuple-element.46.refs_0_.right_a.both_ref), custom_call_target="tpu_custom_call" | custom-call | flops 1835008 | bytes 8388608 | tf_op jit(solution)/shard_map/pallas_call | solution.py:249
  119.2 6.2 %shard_map.125 = (bf16[448,1024]{1,0:T(8,128)(2,1)}, bf16[448,1024]{1,0:T(8,128)(2,1)}) custom-call(s32[10]{0:T(128)} %dynamic_slice.3.place_ref, bf16[4,448,512]{2,1,0:T(8,128)(2,1)} %get-tuple-element.44.refs_0_.left_a, bf16[4,448,512]{2,1,0:T(8,128)(2,1)} %collective-permute-done.refs_1_.left_b, ...), custom_call_target="tpu_custom_call" | custom-call | flops 1879048192 | bytes 8388608 | tf_op jit(solution)/shard_map/pallas_call | solution.py:348
  129.5 8.3 %shard_map.126 = (bf16[4,224,1024]{2,1,0:T(8,128)(2,1)}, bf16[4,224,1024]{2,1,0:T(8,128)(2,1)}) custom-call(s32[10]{0:T(128)} %dynamic_slice.3.place_ref, bf16[4,448,512]{2,1,0:T(8,128)(2,1)} %get-tuple-element.48.refs_0_.left_a, bf16[4,448,512]{2,1,0:T(8,128)(2,1)} %collective-permute-done.3.left_b, ...), custom_call_target="tpu_custom_call" | custom-call | flops 1879048192 | bytes 8388608 | tf_op jit(solution)/shard_map/pallas_call | solution.py:374
  140.5 6.2 %shard_map.127 = (bf16[448,1024]{1,0:T(8,128)(2,1)}, bf16[448,1024]{1,0:T(8,128)(2,1)}) custom-call(s32[10]{0:T(128)} %dynamic_slice.3.place_ref, bf16[4,448,512]{2,1,0:T(8,128)(2,1)} %get-tuple-element.44.refs_0_.left_a, bf16[4,448,512]{2,1,0:T(8,128)(2,1)} %collective-permute-done.refs_1_.left_b, ...), custom_call_target="tpu_custom_call" | custom-call | flops 1879048192 | bytes 8388608 | tf_op jit(solution)/shard_map/pallas_call | solution.py:348
  146.7 3.6 %collective-permute-done.4.up_ref = bf16[448,1024]{1,0:T(8,128)(2,1)} collective-permute-done((bf16[448,1024]{1,0:T(8,128)(2,1)}, bf16[448,1024]{1,0:T(8,128)(2,1)}, u32[]{:S(2)}, u32[]{:S(2)}) %collective-permute-start.4) | collective-permute-done | bytes 917536 | tf_op jit(solution)/shard_map/ppermute | solution.py:390
  156.6 13.2 %shard_map.129.refs_0_ = bf16[512,3712]{1,0:T(8,128)(2,1)} custom-call(bf16[2,512,1024]{2,1,0:T(8,128)(2,1)} %get-tuple-element.46.refs_0_.right_a.both_ref, bf16[3584,1024]{1,0:T(8,128)(2,1)} %bitcast.17, bf16[3584,1024]{1,0:T(8,128)(2,1)} %bitcast.19, bf16[512,128]{1,0:T(8,128)(2,1)} %get-tuple-element.47.wg_ref, ...), custom_call_target="tpu_custom_call" | custom-call | flops 1 | bytes 1 | tf_op jit(solution)/shard_map/pallas_call | solution.py:214
  169.8 4.5 %all-to-all-start.2 = ((bf16[8,64,3712]{2,1,0:T(8,128)(2,1)}), bf16[8,64,3712]{2,1,0:T(8,128)(2,1)}, u32[]{:S(2)}, u32[]{:S(2)}) async-start(bf16[8,64,3712]{2,1,0:T(8,128)(2,1)} %bitcast.14), calls=%async_computation.2 | async-start | bytes 7602176 | tf_op jit(solution)/shard_map/all_to_all | solution.py:492
  174.3 6.3 %shard_map.130 = (bf16[448,1024]{1,0:T(8,128)(2,1)}, bf16[448,1024]{1,0:T(8,128)(2,1)}) custom-call(s32[10]{0:T(128)} %dynamic_slice.3.place_ref, bf16[4,448,512]{2,1,0:T(8,128)(2,1)} %get-tuple-element.44.refs_0_.left_a, bf16[4,448,512]{2,1,0:T(8,128)(2,1)} %collective-permute-done.refs_1_.left_b, ...), custom_call_target="tpu_custom_call" | custom-call | flops 24999999488 | bytes 1 | tf_op jit(solution)/shard_map/pallas_call | solution.py:348
  183.7 3.2 %collective-permute-start.9 = (bf16[448,1024]{1,0:T(8,128)(2,1)}, bf16[448,1024]{1,0:T(8,128)(2,1)}, u32[]{:S(2)}, u32[]{:S(2)}) collective-permute-start(bf16[448,1024]{1,0:T(8,128)(2,1)} %get-tuple-element.60.refs_1_), channel_id=1, source_target_pairs={{0,96},{8,104},{16,112},{24,120},{32,0},{40,8},{48,16},{56,24},{64... | collective-permute-start | bytes 2752520 | tf_op jit(solution)/shard_map/ppermute | solution.py:390
  186.9 6.2 %shard_map.132 = (bf16[448,1024]{1,0:T(8,128)(2,1)}, bf16[448,1024]{1,0:T(8,128)(2,1)}) custom-call(s32[10]{0:T(128)} %dynamic_slice.3.place_ref, bf16[4,448,512]{2,1,0:T(8,128)(2,1)} %get-tuple-element.44.refs_0_.left_a, bf16[4,448,512]{2,1,0:T(8,128)(2,1)} %collective-permute-done.refs_1_.left_b, ...), custom_call_target="tpu_custom_call" | custom-call | flops 1 | bytes 1 | tf_op jit(solution)/shard_map/pallas_call | solution.py:348
  198.6 9.9 %collective-permute-done.8.up_ref = bf16[448,1024]{1,0:T(8,128)(2,1)} collective-permute-done((bf16[448,1024]{1,0:T(8,128)(2,1)}, bf16[448,1024]{1,0:T(8,128)(2,1)}, u32[]{:S(2)}, u32[]{:S(2)}) %collective-permute-start.8) | collective-permute-done | bytes 917536 | tf_op jit(solution)/shard_map/ppermute | solution.py:390
  208.5 3.7 %shard_map.134 = (bf16[2,224,1024]{2,1,0:T(8,128)(2,1)}, bf16[2,224,1024]{2,1,0:T(8,128)(2,1)}) custom-call(bf16[448,1024]{1,0:T(8,128)(2,1)} %get-tuple-element.61.refs_0_.part_up, bf16[448,1024]{1,0:T(8,128)(2,1)} %get-tuple-element.62.refs_1_.part_down, bf16[448,1024]{1,0:T(8,128)(2,1)} %collective-permute-done.8.up_ref, ...), custom_call_target="tpu_custom_call" | custom-call | flops 1 | bytes 1 | tf_op jit(solution)/shard_map/pallas_call | solution.py:428
  214.9 8.5 %all-to-all-done.2 = bf16[8,64,3712]{2,1,0:T(8,128)(2,1)} async-done(((bf16[8,64,3712]{2,1,0:T(8,128)(2,1)}), bf16[8,64,3712]{2,1,0:T(8,128)(2,1)}, u32[]{:S(2)}, u32[]{:S(2)}) %all-to-all-start.2) | async-done | bytes 3801120 | tf_op jit(solution)/shard_map/all_to_all | solution.py:492
  223.4 4.1 %shard_map.135 = (bf16[128,3584]{1,0:T(8,128)(2,1)}, bf16[2,128]{1,0:T(2,128)(2,1)}) custom-call(bf16[2,512,128]{2,1,0:T(8,128)(2,1)} %get-tuple-element.39.picks_ref, bf16[512,3712]{1,0:T(8,128)(2,1)} %bitcast.10.rows_ref, bf16[2,224,1024]{2,1,0:T(8,128)(2,1)} %get-tuple-element.67.refs_0_), custom_call_target="tpu_custom_call" | custom-call | flops 1 | bytes 1 | tf_op jit(solution)/shard_map/pallas_call | solution.py:290
  230.8 10.9 %collective-permute-done.14 = bf16[2,224,1024]{2,1,0:T(8,128)(2,1)} collective-permute-done((bf16[2,224,1024]{2,1,0:T(8,128)(2,1)}, bf16[2,224,1024]{2,1,0:T(8,128)(2,1)}, u32[]{:S(2)}, u32[]{:S(2)}) %collective-permute-start.14) | collective-permute-done | bytes 917536 | tf_op jit(solution)/shard_map/ppermute | solution.py:530
  (36 shorter events, 32.1 us)
Async XLA Ops:
  4.4 49.4 %all-to-all-start.1 = ((bf16[8,64,3584]{2,1,0:T(8,128)(2,1)}), bf16[8,64,3584]{2,1,0:T(8,128)(2,1)}, u32[]{:S(2)}, u32[]{:S(2)}) async-start(bf16[8,64,3584]{2,1,0:T(8,128)(2,1)} %bitcast.20), calls=%async_computation.1 | async-start | bytes 7340032 | tf_op jit(solution)/shard_map/all_to_all | solution.py:492
  53.8 4.7 %copy-start.1 = (s32[160]{0:T(256)S(1)}, s32[160]{0:T(256)}, u32[]{:S(2)}) copy-start(s32[160]{0:T(256)} %constant.14.clone) | copy-start | bytes 1924
  53.8 49.0 %all-to-all-start = ((bf16[8,64,3712]{2,1,0:T(8,128)(2,1)}), bf16[8,64,3712]{2,1,0:T(8,128)(2,1)}, u32[]{:S(2)}, u32[]{:S(2)}) async-start(bf16[8,64,3712]{2,1,0:T(8,128)(2,1)} %bitcast.13), calls=%async_computation | async-start | bytes 7602176 | tf_op jit(solution)/shard_map/all_to_all | solution.py:492
  78.0 24.8 %collective-permute-start = (bf16[4,448,512]{2,1,0:T(8,128)(2,1)}, bf16[4,448,512]{2,1,0:T(8,128)(2,1)}, u32[]{:S(2)}, u32[]{:S(2)}) collective-permute-start(bf16[4,448,512]{2,1,0:T(8,128)(2,1)} %get-tuple-element.45), channel_id=1, source_target_pairs={{0,8},{8,0},{16,24},{24,16},{32,40},{40,32},{48,56},{56,48},{64,72... | collective-permute-start | bytes 5505032 | tf_op jit(solution)/shard_map/ppermute | solution.py:266
  78.0 24.8 %collective-permute-start.1 = (bf16[512,1024]{1,0:T(8,128)(2,1)}, bf16[512,1024]{1,0:T(8,128)(2,1)}, u32[]{:S(2)}, u32[]{:S(2)}) collective-permute-start(bf16[512,1024]{1,0:T(8,128)(2,1)} %get-tuple-element.41.refs_0_.hidden_ref.right_a), channel_id=1, source_target_pairs={{0,8},{8,0},{16,24},{24,16},{32,40},{40,32},{48,56},{56,48},{64,72... | collective-permute-start | bytes 3145736 | tf_op jit(solution)/shard_map/ppermute | solution.py:507
  112.7 6.5 %collective-permute-start.2 = (bf16[2,512,1024]{2,1,0:T(8,128)(2,1)}, bf16[2,512,1024]{2,1,0:T(8,128)(2,1)}, u32[]{:S(2)}, u32[]{:S(2)}) collective-permute-start(bf16[2,512,1024]{2,1,0:T(8,128)(2,1)} %get-tuple-element.46.refs_0_.right_a.both_ref), channel_id=1, source_target_pairs={{0,8},{8,0},{16,24},{24,16},{32,40},{40,32},{48,56},{56,48},{64,72... | collective-permute-start | bytes 6291464 | tf_op jit(solution)/shard_map/ppermute | solution.py:511
  118.7 10.8 %collective-permute-start.3 = (bf16[4,448,512]{2,1,0:T(8,128)(2,1)}, bf16[4,448,512]{2,1,0:T(8,128)(2,1)}, u32[]{:S(2)}, u32[]{:S(2)}) collective-permute-start(bf16[4,448,512]{2,1,0:T(8,128)(2,1)} %get-tuple-element.49), channel_id=1, source_target_pairs={{0,8},{8,0},{16,24},{24,16},{32,40},{40,32},{48,56},{56,48},{64,72... | collective-permute-start | bytes 5505032 | tf_op jit(solution)/shard_map/ppermute | solution.py:266
  125.4 24.9 %collective-permute-start.4 = (bf16[448,1024]{1,0:T(8,128)(2,1)}, bf16[448,1024]{1,0:T(8,128)(2,1)}, u32[]{:S(2)}, u32[]{:S(2)}) collective-permute-start(bf16[448,1024]{1,0:T(8,128)(2,1)} %get-tuple-element.50.refs_0_), channel_id=1, source_target_pairs={{0,32},{8,40},{16,48},{24,56},{32,64},{40,72},{48,80},{56,88},{64,... | collective-permute-start | bytes 2752520 | tf_op jit(solution)/shard_map/ppermute | solution.py:390
  127.3 23.0 %collective-permute-start.5 = (bf16[448,1024]{1,0:T(8,128)(2,1)}, bf16[448,1024]{1,0:T(8,128)(2,1)}, u32[]{:S(2)}, u32[]{:S(2)}) collective-permute-start(bf16[448,1024]{1,0:T(8,128)(2,1)} %get-tuple-element.54), channel_id=1, source_target_pairs={{0,96},{8,104},{16,112},{24,120},{32,0},{40,8},{48,16},{56,24},{64... | collective-permute-start | bytes 2752520 | tf_op jit(solution)/shard_map/ppermute | solution.py:390
  137.8 55.3 %collective-permute-start.10 = (bf16[4,224,1024]{2,1,0:T(8,128)(2,1)}, bf16[4,224,1024]{2,1,0:T(8,128)(2,1)}, u32[]{:S(2)}, u32[]{:S(2)}) collective-permute-start(bf16[4,224,1024]{2,1,0:T(8,128)(2,1)} %get-tuple-element.51.refs_0_), channel_id=1, source_target_pairs={{0,16},{8,24},{16,0},{24,8},{32,48},{40,56},{48,32},{56,40},{64,80... | collective-permute-start | bytes 5505032 | tf_op jit(solution)/shard_map/ppermute | solution.py:516
  153.4 27.2 %collective-permute-start.6 = (bf16[448,1024]{1,0:T(8,128)(2,1)}, bf16[448,1024]{1,0:T(8,128)(2,1)}, u32[]{:S(2)}, u32[]{:S(2)}) collective-permute-start(bf16[448,1024]{1,0:T(8,128)(2,1)} %get-tuple-element.55.refs_0_), channel_id=1, source_target_pairs={{0,32},{8,40},{16,48},{24,56},{32,64},{40,72},{48,80},{56,88},{64,... | collective-permute-start | bytes 2752520 | tf_op jit(solution)/shard_map/ppermute | solution.py:390
  154.6 25.9 %collective-permute-start.7 = (bf16[448,1024]{1,0:T(8,128)(2,1)}, bf16[448,1024]{1,0:T(8,128)(2,1)}, u32[]{:S(2)}, u32[]{:S(2)}) collective-permute-start(bf16[448,1024]{1,0:T(8,128)(2,1)} %get-tuple-element.56.refs_1_), channel_id=1, source_target_pairs={{0,96},{8,104},{16,112},{24,120},{32,0},{40,8},{48,16},{56,24},{64... | collective-permute-start | bytes 2752520 | tf_op jit(solution)/shard_map/ppermute | solution.py:390
  169.8 53.7 %all-to-all-start.2 = ((bf16[8,64,3712]{2,1,0:T(8,128)(2,1)}), bf16[8,64,3712]{2,1,0:T(8,128)(2,1)}, u32[]{:S(2)}, u32[]{:S(2)}) async-start(bf16[8,64,3712]{2,1,0:T(8,128)(2,1)} %bitcast.14), calls=%async_computation.2 | async-start | bytes 7602176 | tf_op jit(solution)/shard_map/all_to_all | solution.py:492
  183.7 24.8 %collective-permute-start.8 = (bf16[448,1024]{1,0:T(8,128)(2,1)}, bf16[448,1024]{1,0:T(8,128)(2,1)}, u32[]{:S(2)}, u32[]{:S(2)}) collective-permute-start(bf16[448,1024]{1,0:T(8,128)(2,1)} %get-tuple-element.59.refs_0_), channel_id=1, source_target_pairs={{0,32},{8,40},{16,48},{24,56},{32,64},{40,72},{48,80},{56,88},{64,... | collective-permute-start | bytes 2752520 | tf_op jit(solution)/shard_map/ppermute | solution.py:390
  183.7 24.8 %collective-permute-start.9 = (bf16[448,1024]{1,0:T(8,128)(2,1)}, bf16[448,1024]{1,0:T(8,128)(2,1)}, u32[]{:S(2)}, u32[]{:S(2)}) collective-permute-start(bf16[448,1024]{1,0:T(8,128)(2,1)} %get-tuple-element.60.refs_1_), channel_id=1, source_target_pairs={{0,96},{8,104},{16,112},{24,120},{32,0},{40,8},{48,16},{56,24},{64... | collective-permute-start | bytes 2752520 | tf_op jit(solution)/shard_map/ppermute | solution.py:390
  196.0 31.5 %collective-permute-start.11 = (bf16[224,1024]{1,0:T(8,128)(2,1)}, bf16[224,1024]{1,0:T(8,128)(2,1)S(1)}, u32[]{:S(2)}, u32[]{:S(2)}) collective-permute-start(bf16[224,1024]{1,0:T(8,128)(2,1)} %get-tuple-element.64.refs_0_), channel_id=1, source_target_pairs={{0,96},{8,104},{16,112},{24,120},{32,0},{40,8},{48,16},{56,24},{64... | collective-permute-start | bytes 1376264 | tf_op jit(solution)/shard_map/ppermute | solution.py:528
  196.6 30.9 %collective-permute-start.12 = (bf16[224,1024]{1,0:T(8,128)(2,1)}, bf16[224,1024]{1,0:T(8,128)(2,1)}, u32[]{:S(2)}, u32[]{:S(2)}) collective-permute-start(bf16[224,1024]{1,0:T(8,128)(2,1)} %get-tuple-element.65.refs_1_), channel_id=1, source_target_pairs={{0,32},{8,40},{16,48},{24,56},{32,64},{40,72},{48,80},{56,88},{64,... | collective-permute-start | bytes 1376264 | tf_op jit(solution)/shard_map/ppermute | solution.py:528
  198.1 29.4 %collective-permute-start.13 = (bf16[224,1024]{1,0:T(8,128)(2,1)}, bf16[224,1024]{1,0:T(8,128)(2,1)}, u32[]{:S(2)}, u32[]{:S(2)}) collective-permute-start(bf16[224,1024]{1,0:T(8,128)(2,1)} %get-tuple-element.66.refs_2_), channel_id=1, source_target_pairs={{0,64},{8,72},{16,80},{24,88},{32,96},{40,104},{48,112},{56,120},{... | collective-permute-start | bytes 1376264 | tf_op jit(solution)/shard_map/ppermute | solution.py:528
  212.2 29.5 %collective-permute-start.14 = (bf16[2,224,1024]{2,1,0:T(8,128)(2,1)}, bf16[2,224,1024]{2,1,0:T(8,128)(2,1)}, u32[]{:S(2)}, u32[]{:S(2)}) collective-permute-start(bf16[2,224,1024]{2,1,0:T(8,128)(2,1)} %get-tuple-element.67.refs_0_), channel_id=1, source_target_pairs={{0,16},{8,24},{16,0},{24,8},{32,48},{40,56},{48,32},{56,40},{64,80... | collective-permute-start | bytes 2752520 | tf_op jit(solution)/shard_map/ppermute | solution.py:530
  227.5 0.8 copy-start

commit v8 on v7

--- a/solution.py
+++ b/solution.py
@@ -408,32 +408,45 @@
     )(*parts, *moved, *after)
 
 
-def wide_last_kernel(part_up, part_down, up_ref, down_ref, *refs):
-    mine_ref, away_ref = refs[-2:]
-    sums = [
-        (a[...].astype(F32) + b[...].astype(F32)).astype(BF)
-        for a, b in ((part_up, up_ref), (part_down, down_ref))
-    ]
-    for step, out_ref in enumerate((away_ref, mine_ref)):
-
-        @pl.when(pl.program_id(0) == step)
-        def _():
-            out_ref[0] = sums[0]
-            out_ref[1] = sums[1]
-
-
-def wide_last(parts, moved, after=()):
-    spec = pl.BlockSpec((SUB, FF), lambda i: (1 - i, 0))
-    out = pl.BlockSpec((2, SUB, FF), lambda i: (0, 0, 0))
-    return pl.pallas_call(
-        wide_last_kernel,
+def wide_away_kernel(part_up, part_down, up_ref, down_ref, *refs):
+    for k, (a, b) in enumerate(((part_up, up_ref), (part_down, down_ref))):
+        refs[-1][k] = (a[...].astype(F32) + b[...].astype(F32)).astype(BF)
+
+
+def wide_away(parts, moved, after=()):
+    half = SUB // 2
+    spec = pl.BlockSpec((half, FF), lambda i: (2 + i, 0))
+    return pl.pallas_call(
+        wide_away_kernel,
         grid=(2,),
         in_specs=[spec] * 4 + [pl.BlockSpec(memory_space=pl.ANY)] * len(after),
-        out_specs=[out] * 2,
-        out_shape=[jax.ShapeDtypeStruct((2, SUB, FF), BF)] * 2,
+        out_specs=pl.BlockSpec((2, half, FF), lambda i: (0, i, 0)),
+        out_shape=jax.ShapeDtypeStruct((2, SUB, FF), BF),
         compiler_params=params(),
         cost_estimate=SHORT,
     )(*parts, *moved, *after)
+
+
+def wide_end_kernel(part_up, part_down, up_ref, down_ref, came_ref, *refs):
+    for k, (a, b) in enumerate(((part_up, up_ref), (part_down, down_ref))):
+        total = a[...].astype(F32) + b[...].astype(F32) + came_ref[k].astype(F32)
+        refs[-2 + k][...] = total.astype(BF)
+
+
+def wide_end(parts, moved, came, after=()):
+    half = SUB // 2
+    spec = pl.BlockSpec((half, FF), lambda i: (i, 0))
+    return pl.pallas_call(
+        wide_end_kernel,
+        grid=(2,),
+        in_specs=[spec] * 4
+        + [pl.BlockSpec((2, half, FF), lambda i: (0, i, 0))]
+        + [pl.BlockSpec(memory_space=pl.ANY)] * len(after),
+        out_specs=[spec] * 2,
+        out_shape=[jax.ShapeDtypeStruct((SUB, FF), BF)] * 2,
+        compiler_params=params(),
+        cost_estimate=SHORT,
+    )(*parts, *moved, came, *after)
 
 
 def down_sums_kernel(near_ref, far_ref, *refs):
@@ -526,13 +539,12 @@
     sums = down_sums(near, far_in, after=parts3)
     ways = (TO_DOWN, TO_UP, TO_TWO)
     down_came = [lax.ppermute(part, "dp", way) for part, way in zip(sums, ways)]
-    mine, away = wide_last(parts3, moved2, after=sums)
+    away = wide_away(parts3, moved2, after=sums)
     came = lax.ppermute(away, "dp", TO_X)
     grad_tokens, grad_weights = combine(picks, returned, after=(away,))
     down_grad = down_last(near, far_in, down_came, after=(grad_tokens,))
-    mine, down_grad = lax.optimization_barrier((mine, down_grad))
-    grad_gate = add(mine[0], came[0])[None]
-    grad_up = add(mine[1], came[1])[None]
+    gate_grad, up_grad = wide_end(parts3, moved2, came, after=(down_grad,))
+    grad_gate, grad_up = gate_grad[None], up_grad[None]
     grad_down = down_grad[None]
     return (grad_tokens, grad_weights.T, grad_gate, grad_up, grad_down)
 

time: 245 us -> 245 us (level)
  other arithmetic: 2.7 us -> 0 us
    convert_element_type x1 -> x0, other arithmetic: 2.7 us -> none  [add(): return total.astype(BF)]
    pallas_call x1 -> x2, Pallas kernels: 3.72 us -> 5.18 us  [the longest x1 2.72 us: wide_end(): pl.pallas_call(wide_end_kernel, grid=(2,), in_specs=[spec] * 4 + [pl.Bloc...]
  transfers between devices with their start and end apart: 18 -> 18, of which waited for: 6 -> 6; matrix products, arithmetic and copies ran while one was open for 0% -> 0% of each run, Pallas kernels for 39% -> 38%
where the time goes in v8:
time: 245 us; the launch traced here: 244 us
  Pallas kernels  110 us (45%)
  waiting for transfers between devices  98.3 us (40%)
  starting transfers between devices  34.1 us (14%)
    all_to_all x3, waiting for transfers between devices, exchange(): lax.all_to_all(rows.reshape(EXPERTS, CAP, width), 'expert', split_axis=0,...  73.9 us
    pallas_call x4, Pallas kernels, wide_parts(): pl.pallas_call(wide_kernel, grid_spec=pltpu.PrefetchScalarGridSpec(num_sc...  24.8 us
    all_to_all x3, starting transfers between devices, exchange(): lax.all_to_all(rows.reshape(EXPERTS, CAP, width), 'expert', split_axis=0,...  14.6 us
    pallas_call x1, Pallas kernels, forward(): pl.pallas_call(forward_kernel, grid=(FF // n,), in_specs=[pl.BlockSpec((R...  13.5 us
    ppermute x6, waiting for transfers between devices, around(): return (lax.ppermute(up, 'dp', TO_UP), lax.ppermute(down, 'dp', TO_DOWN))  13.5 us
    pallas_call x1, Pallas kernels, row_grads(): pl.pallas_call(rows_kernel, grid=(NT + 1,), in_specs=[pl.BlockSpec((2, RO...  13.1 us
    pallas_call x2, Pallas kernels, turned(): pl.pallas_call(functools.partial(turned_kernel, scaled, len(after)), grid...  11.6 us
    ppermute x1, waiting for transfers between devices, local(): came = lax.ppermute(away, 'dp', TO_X)  10.9 us
  transfers between devices with their start and end apart: 18, of which 6 were waited for; matrix products, arithmetic and copies ran while one was open for 0% of the time, Pallas kernels for 38%

profile of v8, /device:TPU:0, one launch (start us, length us, event | category | flops | bytes accessed | tf_op | source)
XLA Modules:
  0.0 244.4 jit_solution(3387873153681809652)
XLA Ops:
  0.6 3.7 %shard_map.119 = (bf16[2,512,128]{2,1,0:T(8,128)(2,1)}, bf16[512,3584]{1,0:T(8,128)(2,1)}) custom-call(s32[2,128]{1,0:T(2,128)} %bitcast.27, bf16[128,3584]{1,0:T(8,128)(2,1)} %tokens_ref.1), custom_call_target="tpu_custom_call" | custom-call | flops 469762048 | bytes 5242880 | tf_op jit(solution)/shard_map/pallas_call | solution.py:68
  4.3 5.5 %all-to-all-start.1 = ((bf16[8,64,3584]{2,1,0:T(8,128)(2,1)}), bf16[8,64,3584]{2,1,0:T(8,128)(2,1)}, u32[]{:S(2)}, u32[]{:S(2)}) async-start(bf16[8,64,3584]{2,1,0:T(8,128)(2,1)} %bitcast.22), calls=%async_computation.1 | async-start | bytes 7340032 | tf_op jit(solution)/shard_map/all_to_all | solution.py:505
  9.8 3.9 %shard_map.120 = bf16[512,3712]{1,0:T(8,128)(2,1)} custom-call(bf16[2,512,128]{2,1,0:T(8,128)(2,1)} %get-tuple-element.37.picks_ref, bf16[2,128]{1,0:T(2,128)(2,1)} %bitcast.24, bf16[128,3584]{1,0:T(8,128)(2,1)} %grads_ref.1), custom_call_target="tpu_custom_call" | custom-call | flops 469762048 | bytes 5242880 | tf_op jit(solution)/shard_map/pallas_call | solution.py:105
  13.7 40.0 %all-to-all-done.1 = bf16[8,64,3584]{2,1,0:T(8,128)(2,1)} async-done(((bf16[8,64,3584]{2,1,0:T(8,128)(2,1)}), bf16[8,64,3584]{2,1,0:T(8,128)(2,1)}, u32[]{:S(2)}, u32[]{:S(2)}) %all-to-all-start.1) | async-done | bytes 3670048 | tf_op jit(solution)/shard_map/all_to_all | solution.py:505
  53.8 4.6 %all-to-all-start = ((bf16[8,64,3712]{2,1,0:T(8,128)(2,1)}), bf16[8,64,3712]{2,1,0:T(8,128)(2,1)}, u32[]{:S(2)}, u32[]{:S(2)}) async-start(bf16[8,64,3712]{2,1,0:T(8,128)(2,1)} %bitcast.15), calls=%async_computation | async-start | bytes 7602176 | tf_op jit(solution)/shard_map/all_to_all | solution.py:505
  59.0 13.5 %shard_map.121 = (bf16[512,1024]{1,0:T(8,128)(2,1)}, f32[512,1024]{1,0:T(8,128)}, f32[512,1024]{1,0:T(8,128)}) custom-call(bf16[512,3584]{1,0:T(8,128)(2,1)} %bitcast.6.x_ref.p_ref, bf16[3584,1024]{1,0:T(8,128)(2,1)} %bitcast.18, bf16[3584,1024]{1,0:T(8,128)(2,1)} %bitcast.20), custom_call_target="tpu_custom_call" | custom-call | flops 7516192768 | bytes 24117248 | tf_op jit(solution)/shard_map/pallas_call | solution.py:133
  72.5 5.7 %shard_map.122 = (bf16[4,448,512]{2,1,0:T(8,128)(2,1)}, bf16[4,448,512]{2,1,0:T(8,128)(2,1)}) custom-call(s32[10]{0:T(128)} %dynamic_slice.3.place_ref, bf16[512,3584]{1,0:T(8,128)(2,1)} %bitcast.6.x_ref.p_ref, bf16[512,3584]{1,0:T(8,128)(2,1)} %bitcast.6.x_ref.p_ref, bf16[512,1024]{1,0:T(8,128)(2,1)} %get-tuple-element.39.refs_0_.hidden_ref.right_a), custom_call_target="tpu_custom_call" | custom-call | flops 1835008 | bytes 8388608 | tf_op jit(solution)/shard_map/pallas_call | solution.py:249
  78.7 24.1 %all-to-all-done = bf16[8,64,3712]{2,1,0:T(8,128)(2,1)} async-done(((bf16[8,64,3712]{2,1,0:T(8,128)(2,1)}), bf16[8,64,3712]{2,1,0:T(8,128)(2,1)}, u32[]{:S(2)}, u32[]{:S(2)}) %all-to-all-start) | async-done | bytes 3801120 | tf_op jit(solution)/shard_map/all_to_all | solution.py:505
  102.8 10.0 %shard_map.123 = (bf16[2,512,1024]{2,1,0:T(8,128)(2,1)}, bf16[512,128]{1,0:T(8,128)(2,1)}) custom-call(bf16[512,3712]{1,0:T(8,128)(2,1)} %bitcast.3.g_ref.x_ref.p_ref, bf16[3584,1024]{1,0:T(8,128)(2,1)} %bitcast.17, bf16[512,1024]{1,0:T(8,128)(2,1)} %get-tuple-element.39.refs_0_.hidden_ref.right_a, f32[512,1024]{1,0:T(8,128)} %get-tuple-element.40.active_ref, ...), custom_call_target="tpu_custom_call" | custom-call | flops 3758096384 | bytes 18874368 | tf_op jit(solution)/shard_map/pallas_call | solution.py:172
  112.7 5.9 %shard_map.124 = (bf16[4,448,512]{2,1,0:T(8,128)(2,1)}, bf16[4,448,512]{2,1,0:T(8,128)(2,1)}) custom-call(s32[10]{0:T(128)} %dynamic_slice.3.place_ref, bf16[512,3712]{1,0:T(8,128)(2,1)} %bitcast.3.g_ref.x_ref.p_ref, bf16[512,3712]{1,0:T(8,128)(2,1)} %bitcast.3.g_ref.x_ref.p_ref, bf16[2,512,1024]{2,1,0:T(8,128)(2,1)} %get-tuple-element.44.refs_0_.right_a.both_ref), custom_call_target="tpu_custom_call" | custom-call | flops 1835008 | bytes 8388608 | tf_op jit(solution)/shard_map/pallas_call | solution.py:249
  119.2 6.2 %shard_map.125 = (bf16[448,1024]{1,0:T(8,128)(2,1)}, bf16[448,1024]{1,0:T(8,128)(2,1)}) custom-call(s32[10]{0:T(128)} %dynamic_slice.3.place_ref, bf16[4,448,512]{2,1,0:T(8,128)(2,1)} %get-tuple-element.42.refs_0_.left_a, bf16[4,448,512]{2,1,0:T(8,128)(2,1)} %collective-permute-done.refs_1_.left_b, ...), custom_call_target="tpu_custom_call" | custom-call | flops 1879048192 | bytes 8388608 | tf_op jit(solution)/shard_map/pallas_call | solution.py:348
  129.4 8.3 %shard_map.126 = (bf16[4,224,1024]{2,1,0:T(8,128)(2,1)}, bf16[4,224,1024]{2,1,0:T(8,128)(2,1)}) custom-call(s32[10]{0:T(128)} %dynamic_slice.3.place_ref, bf16[4,448,512]{2,1,0:T(8,128)(2,1)} %get-tuple-element.46.refs_0_.left_a, bf16[4,448,512]{2,1,0:T(8,128)(2,1)} %collective-permute-done.3.left_b, ...), custom_call_target="tpu_custom_call" | custom-call | flops 1879048192 | bytes 8388608 | tf_op jit(solution)/shard_map/pallas_call | solution.py:374
  140.4 6.2 %shard_map.127 = (bf16[448,1024]{1,0:T(8,128)(2,1)}, bf16[448,1024]{1,0:T(8,128)(2,1)}) custom-call(s32[10]{0:T(128)} %dynamic_slice.3.place_ref, bf16[4,448,512]{2,1,0:T(8,128)(2,1)} %get-tuple-element.42.refs_0_.left_a, bf16[4,448,512]{2,1,0:T(8,128)(2,1)} %collective-permute-done.refs_1_.left_b, ...), custom_call_target="tpu_custom_call" | custom-call | flops 1879048192 | bytes 8388608 | tf_op jit(solution)/shard_map/pallas_call | solution.py:348
  146.6 3.6 %collective-permute-done.4.up_ref = bf16[448,1024]{1,0:T(8,128)(2,1)} collective-permute-done((bf16[448,1024]{1,0:T(8,128)(2,1)}, bf16[448,1024]{1,0:T(8,128)(2,1)}, u32[]{:S(2)}, u32[]{:S(2)}) %collective-permute-start.4) | collective-permute-done | bytes 917536 | tf_op jit(solution)/shard_map/ppermute | solution.py:390
  156.5 13.1 %shard_map.129.refs_0_ = bf16[512,3712]{1,0:T(8,128)(2,1)} custom-call(bf16[2,512,1024]{2,1,0:T(8,128)(2,1)} %get-tuple-element.44.refs_0_.right_a.both_ref, bf16[3584,1024]{1,0:T(8,128)(2,1)} %bitcast.19, bf16[3584,1024]{1,0:T(8,128)(2,1)} %bitcast.21, bf16[512,128]{1,0:T(8,128)(2,1)} %get-tuple-element.45.wg_ref, ...), custom_call_target="tpu_custom_call" | custom-call | flops 1 | bytes 1 | tf_op jit(solution)/shard_map/pallas_call | solution.py:214
  169.7 4.5 %all-to-all-start.2 = ((bf16[8,64,3712]{2,1,0:T(8,128)(2,1)}), bf16[8,64,3712]{2,1,0:T(8,128)(2,1)}, u32[]{:S(2)}, u32[]{:S(2)}) async-start(bf16[8,64,3712]{2,1,0:T(8,128)(2,1)} %bitcast.16), calls=%async_computation.2 | async-start | bytes 7602176 | tf_op jit(solution)/shard_map/all_to_all | solution.py:505
  174.2 6.2 %shard_map.130 = (bf16[448,1024]{1,0:T(8,128)(2,1)}, bf16[448,1024]{1,0:T(8,128)(2,1)}) custom-call(s32[10]{0:T(128)} %dynamic_slice.3.place_ref, bf16[4,448,512]{2,1,0:T(8,128)(2,1)} %get-tuple-element.42.refs_0_.left_a, bf16[4,448,512]{2,1,0:T(8,128)(2,1)} %collective-permute-done.refs_1_.left_b, ...), custom_call_target="tpu_custom_call" | custom-call | flops 24999999488 | bytes 1 | tf_op jit(solution)/shard_map/pallas_call | solution.py:348
  180.4 3.1 %shard_map.131 = (bf16[448,1024]{1,0:T(8,128)(2,1)}, bf16[448,1024]{1,0:T(8,128)(2,1)}) custom-call(bf16[448,1024]{1,0:T(8,128)(2,1)} %get-tuple-element.55.part_up, bf16[448,1024]{1,0:T(8,128)(2,1)} %get-tuple-element.56.part_down, bf16[448,1024]{1,0:T(8,128)(2,1)} %collective-permute-done.6.up_ref, bf16[448,1024]{1,0:T(8,128)(2,1)} %collective-permute-done.7.down_ref), custom_call_target="tpu_custom_call" | custom-call | flops 1 | bytes 1 | tf_op jit(solution)/shard_map/pallas_call | solution.py:400
  183.6 3.2 %collective-permute-start.9 = (bf16[448,1024]{1,0:T(8,128)(2,1)}, bf16[448,1024]{1,0:T(8,128)(2,1)}, u32[]{:S(2)}, u32[]{:S(2)}) collective-permute-start(bf16[448,1024]{1,0:T(8,128)(2,1)} %get-tuple-element.58.refs_1_), channel_id=1, source_target_pairs={{0,96},{8,104},{16,112},{24,120},{32,0},{40,8},{48,16},{56,24},{64... | collective-permute-start | bytes 2752520 | tf_op jit(solution)/shard_map/ppermute | solution.py:390
  186.8 6.2 %shard_map.132 = (bf16[448,1024]{1,0:T(8,128)(2,1)}, bf16[448,1024]{1,0:T(8,128)(2,1)}) custom-call(s32[10]{0:T(128)} %dynamic_slice.3.place_ref, bf16[4,448,512]{2,1,0:T(8,128)(2,1)} %get-tuple-element.42.refs_0_.left_a, bf16[4,448,512]{2,1,0:T(8,128)(2,1)} %collective-permute-done.refs_1_.left_b, ...), custom_call_target="tpu_custom_call" | custom-call | flops 1 | bytes 1 | tf_op jit(solution)/shard_map/pallas_call | solution.py:348
  198.5 9.9 %collective-permute-done.8.up_ref = bf16[448,1024]{1,0:T(8,128)(2,1)} collective-permute-done((bf16[448,1024]{1,0:T(8,128)(2,1)}, bf16[448,1024]{1,0:T(8,128)(2,1)}, u32[]{:S(2)}, u32[]{:S(2)}) %collective-permute-start.8) | collective-permute-done | bytes 917536 | tf_op jit(solution)/shard_map/ppermute | solution.py:390
  213.6 9.8 %all-to-all-done.2 = bf16[8,64,3712]{2,1,0:T(8,128)(2,1)} async-done(((bf16[8,64,3712]{2,1,0:T(8,128)(2,1)}), bf16[8,64,3712]{2,1,0:T(8,128)(2,1)}, u32[]{:S(2)}, u32[]{:S(2)}) %all-to-all-start.2) | async-done | bytes 3801120 | tf_op jit(solution)/shard_map/all_to_all | solution.py:505
  223.3 4.1 %shard_map.135 = (bf16[128,3584]{1,0:T(8,128)(2,1)}, bf16[2,128]{1,0:T(2,128)(2,1)}) custom-call(bf16[2,512,128]{2,1,0:T(8,128)(2,1)} %get-tuple-element.37.picks_ref, bf16[512,3712]{1,0:T(8,128)(2,1)} %bitcast.10.rows_ref, bf16[2,224,1024]{2,1,0:T(8,128)(2,1)} %shard_map.134.refs_0_), custom_call_target="tpu_custom_call" | custom-call | flops 1 | bytes 1 | tf_op jit(solution)/shard_map/pallas_call | solution.py:290
  230.7 10.9 %collective-permute-done.11.came_ref = bf16[2,224,1024]{2,1,0:T(8,128)(2,1)} collective-permute-done((bf16[2,224,1024]{2,1,0:T(8,128)(2,1)}, bf16[2,224,1024]{2,1,0:T(8,128)(2,1)}, u32[]{:S(2)}, u32[]{:S(2)}) %collective-permute-start.11) | collective-permute-done | bytes 917536 | tf_op jit(solution)/shard_map/ppermute | solution.py:543
  (36 shorter events, 31.4 us)
Async XLA Ops:
  4.3 49.4 %all-to-all-start.1 = ((bf16[8,64,3584]{2,1,0:T(8,128)(2,1)}), bf16[8,64,3584]{2,1,0:T(8,128)(2,1)}, u32[]{:S(2)}, u32[]{:S(2)}) async-start(bf16[8,64,3584]{2,1,0:T(8,128)(2,1)} %bitcast.22), calls=%async_computation.1 | async-start | bytes 7340032 | tf_op jit(solution)/shard_map/all_to_all | solution.py:505
  53.8 4.7 %copy-start.1 = (s32[160]{0:T(256)S(1)}, s32[160]{0:T(256)}, u32[]{:S(2)}) copy-start(s32[160]{0:T(256)} %constant.14.clone) | copy-start | bytes 1924
  53.8 49.0 %all-to-all-start = ((bf16[8,64,3712]{2,1,0:T(8,128)(2,1)}), bf16[8,64,3712]{2,1,0:T(8,128)(2,1)}, u32[]{:S(2)}, u32[]{:S(2)}) async-start(bf16[8,64,3712]{2,1,0:T(8,128)(2,1)} %bitcast.15), calls=%async_computation | async-start | bytes 7602176 | tf_op jit(solution)/shard_map/all_to_all | solution.py:505
  78.2 24.6 %collective-permute-start = (bf16[4,448,512]{2,1,0:T(8,128)(2,1)}, bf16[4,448,512]{2,1,0:T(8,128)(2,1)}, u32[]{:S(2)}, u32[]{:S(2)}) collective-permute-start(bf16[4,448,512]{2,1,0:T(8,128)(2,1)} %get-tuple-element.43), channel_id=1, source_target_pairs={{0,8},{8,0},{16,24},{24,16},{32,40},{40,32},{48,56},{56,48},{64,72... | collective-permute-start | bytes 5505032 | tf_op jit(solution)/shard_map/ppermute | solution.py:266
  78.2 24.6 %collective-permute-start.1 = (bf16[512,1024]{1,0:T(8,128)(2,1)}, bf16[512,1024]{1,0:T(8,128)(2,1)}, u32[]{:S(2)}, u32[]{:S(2)}) collective-permute-start(bf16[512,1024]{1,0:T(8,128)(2,1)} %get-tuple-element.39.refs_0_.hidden_ref.right_a), channel_id=1, source_target_pairs={{0,8},{8,0},{16,24},{24,16},{32,40},{40,32},{48,56},{56,48},{64,72... | collective-permute-start | bytes 3145736 | tf_op jit(solution)/shard_map/ppermute | solution.py:520
  112.7 6.4 %collective-permute-start.2 = (bf16[2,512,1024]{2,1,0:T(8,128)(2,1)}, bf16[2,512,1024]{2,1,0:T(8,128)(2,1)}, u32[]{:S(2)}, u32[]{:S(2)}) collective-permute-start(bf16[2,512,1024]{2,1,0:T(8,128)(2,1)} %get-tuple-element.44.refs_0_.right_a.both_ref), channel_id=1, source_target_pairs={{0,8},{8,0},{16,24},{24,16},{32,40},{40,32},{48,56},{56,48},{64,72... | collective-permute-start | bytes 6291464 | tf_op jit(solution)/shard_map/ppermute | solution.py:524
  118.7 10.7 %collective-permute-start.3 = (bf16[4,448,512]{2,1,0:T(8,128)(2,1)}, bf16[4,448,512]{2,1,0:T(8,128)(2,1)}, u32[]{:S(2)}, u32[]{:S(2)}) collective-permute-start(bf16[4,448,512]{2,1,0:T(8,128)(2,1)} %get-tuple-element.47), channel_id=1, source_target_pairs={{0,8},{8,0},{16,24},{24,16},{32,40},{40,32},{48,56},{56,48},{64,72... | collective-permute-start | bytes 5505032 | tf_op jit(solution)/shard_map/ppermute | solution.py:266
  125.3 24.9 %collective-permute-start.4 = (bf16[448,1024]{1,0:T(8,128)(2,1)}, bf16[448,1024]{1,0:T(8,128)(2,1)}, u32[]{:S(2)}, u32[]{:S(2)}) collective-permute-start(bf16[448,1024]{1,0:T(8,128)(2,1)} %get-tuple-element.48.refs_0_), channel_id=1, source_target_pairs={{0,32},{8,40},{16,48},{24,56},{32,64},{40,72},{48,80},{56,88},{64,... | collective-permute-start | bytes 2752520 | tf_op jit(solution)/shard_map/ppermute | solution.py:390
  127.3 23.0 %collective-permute-start.5 = (bf16[448,1024]{1,0:T(8,128)(2,1)}, bf16[448,1024]{1,0:T(8,128)(2,1)}, u32[]{:S(2)}, u32[]{:S(2)}) collective-permute-start(bf16[448,1024]{1,0:T(8,128)(2,1)} %get-tuple-element.52), channel_id=1, source_target_pairs={{0,96},{8,104},{16,112},{24,120},{32,0},{40,8},{48,16},{56,24},{64... | collective-permute-start | bytes 2752520 | tf_op jit(solution)/shard_map/ppermute | solution.py:390
  137.7 55.3 %collective-permute-start.10 = (bf16[4,224,1024]{2,1,0:T(8,128)(2,1)}, bf16[4,224,1024]{2,1,0:T(8,128)(2,1)}, u32[]{:S(2)}, u32[]{:S(2)}) collective-permute-start(bf16[4,224,1024]{2,1,0:T(8,128)(2,1)} %get-tuple-element.49.refs_0_), channel_id=1, source_target_pairs={{0,16},{8,24},{16,0},{24,8},{32,48},{40,56},{48,32},{56,40},{64,80... | collective-permute-start | bytes 5505032 | tf_op jit(solution)/shard_map/ppermute | solution.py:529
  153.3 27.1 %collective-permute-start.6 = (bf16[448,1024]{1,0:T(8,128)(2,1)}, bf16[448,1024]{1,0:T(8,128)(2,1)}, u32[]{:S(2)}, u32[]{:S(2)}) collective-permute-start(bf16[448,1024]{1,0:T(8,128)(2,1)} %get-tuple-element.53.refs_0_), channel_id=1, source_target_pairs={{0,32},{8,40},{16,48},{24,56},{32,64},{40,72},{48,80},{56,88},{64,... | collective-permute-start | bytes 2752520 | tf_op jit(solution)/shard_map/ppermute | solution.py:390
  154.6 25.9 %collective-permute-start.7 = (bf16[448,1024]{1,0:T(8,128)(2,1)}, bf16[448,1024]{1,0:T(8,128)(2,1)}, u32[]{:S(2)}, u32[]{:S(2)}) collective-permute-start(bf16[448,1024]{1,0:T(8,128)(2,1)} %get-tuple-element.54.refs_1_), channel_id=1, source_target_pairs={{0,96},{8,104},{16,112},{24,120},{32,0},{40,8},{48,16},{56,24},{64... | collective-permute-start | bytes 2752520 | tf_op jit(solution)/shard_map/ppermute | solution.py:390
  169.7 53.7 %all-to-all-start.2 = ((bf16[8,64,3712]{2,1,0:T(8,128)(2,1)}), bf16[8,64,3712]{2,1,0:T(8,128)(2,1)}, u32[]{:S(2)}, u32[]{:S(2)}) async-start(bf16[8,64,3712]{2,1,0:T(8,128)(2,1)} %bitcast.16), calls=%async_computation.2 | async-start | bytes 7602176 | tf_op jit(solution)/shard_map/all_to_all | solution.py:505
  183.5 24.8 %collective-permute-start.8 = (bf16[448,1024]{1,0:T(8,128)(2,1)}, bf16[448,1024]{1,0:T(8,128)(2,1)}, u32[]{:S(2)}, u32[]{:S(2)}) collective-permute-start(bf16[448,1024]{1,0:T(8,128)(2,1)} %get-tuple-element.57.refs_0_), channel_id=1, source_target_pairs={{0,32},{8,40},{16,48},{24,56},{32,64},{40,72},{48,80},{56,88},{64,... | collective-permute-start | bytes 2752520 | tf_op jit(solution)/shard_map/ppermute | solution.py:390
  183.6 24.8 %collective-permute-start.9 = (bf16[448,1024]{1,0:T(8,128)(2,1)}, bf16[448,1024]{1,0:T(8,128)(2,1)}, u32[]{:S(2)}, u32[]{:S(2)}) collective-permute-start(bf16[448,1024]{1,0:T(8,128)(2,1)} %get-tuple-element.58.refs_1_), channel_id=1, source_target_pairs={{0,96},{8,104},{16,112},{24,120},{32,0},{40,8},{48,16},{56,24},{64... | collective-permute-start | bytes 2752520 | tf_op jit(solution)/shard_map/ppermute | solution.py:390
  195.9 31.5 %collective-permute-start.12 = (bf16[224,1024]{1,0:T(8,128)(2,1)}, bf16[224,1024]{1,0:T(8,128)(2,1)S(1)}, u32[]{:S(2)}, u32[]{:S(2)}) collective-permute-start(bf16[224,1024]{1,0:T(8,128)(2,1)} %get-tuple-element.62.refs_0_), channel_id=1, source_target_pairs={{0,96},{8,104},{16,112},{24,120},{32,0},{40,8},{48,16},{56,24},{64... | collective-permute-start | bytes 1376264 | tf_op jit(solution)/shard_map/ppermute | solution.py:541
  196.5 31.0 %collective-permute-start.13 = (bf16[224,1024]{1,0:T(8,128)(2,1)}, bf16[224,1024]{1,0:T(8,128)(2,1)}, u32[]{:S(2)}, u32[]{:S(2)}) collective-permute-start(bf16[224,1024]{1,0:T(8,128)(2,1)} %get-tuple-element.63.refs_1_), channel_id=1, source_target_pairs={{0,32},{8,40},{16,48},{24,56},{32,64},{40,72},{48,80},{56,88},{64,... | collective-permute-start | bytes 1376264 | tf_op jit(solution)/shard_map/ppermute | solution.py:541
  198.0 29.5 %collective-permute-start.14 = (bf16[224,1024]{1,0:T(8,128)(2,1)}, bf16[224,1024]{1,0:T(8,128)(2,1)}, u32[]{:S(2)}, u32[]{:S(2)}) collective-permute-start(bf16[224,1024]{1,0:T(8,128)(2,1)} %get-tuple-element.64.refs_2_), channel_id=1, source_target_pairs={{0,64},{8,72},{16,80},{24,88},{32,96},{40,104},{48,112},{56,120},{... | collective-permute-start | bytes 1376264 | tf_op jit(solution)/shard_map/ppermute | solution.py:541
  210.8 30.8 %collective-permute-start.11 = (bf16[2,224,1024]{2,1,0:T(8,128)(2,1)}, bf16[2,224,1024]{2,1,0:T(8,128)(2,1)}, u32[]{:S(2)}, u32[]{:S(2)}) collective-permute-start(bf16[2,224,1024]{2,1,0:T(8,128)(2,1)} %shard_map.134.refs_0_), channel_id=1, source_target_pairs={{0,16},{8,24},{16,0},{24,8},{32,48},{40,56},{48,32},{56,40},{64,80... | collective-permute-start | bytes 2752520 | tf_op jit(solution)/shard_map/ppermute | solution.py:543
  227.4 0.8 copy-start
